TPU v7x, 32 devices: a whole 2x2x4 slice. The times are simulated.
32 devices in a mesh: batch: 8 (over z, x), seq: 4 (over y, core).
Axes of the slice: x: 2, y: 2, z: 4, core: 2. Of those that a mesh axis runs over, the one named last changes fastest.
Arguments:
- tokens: bfloat16 [8, 2048, 512], P('batch', 'seq'), may hold values from -6 to 6
- prefix: int32 [8], P('batch'), may hold values from 0 to 1023
- cotangent: bfloat16 [8, 2048, 512], P('batch', 'seq'), may hold values from -6 to 6
- ln1_gain: bfloat16 [512], replicated, may hold values from 0.25 to 1.75
- ln1_bias: bfloat16 [512], replicated, may hold values from -1.5 to 1.5
- w_qkv: bfloat16 [512, 1536], replicated, may hold values from -0.25 to 0.25
- w_out: bfloat16 [512, 512], replicated, may hold values from -1 to 1
- ln2_gain: bfloat16 [512], replicated, may hold values from 0.25 to 1.75
- ln2_bias: bfloat16 [512], replicated, may hold values from -1.5 to 1.5
- w_up: bfloat16 [512, 2048], replicated, may hold values from -0.25 to 0.25
- w_down: bfloat16 [2048, 512], replicated, may hold values from -0.125 to 0.125
Outputs:
- output: bfloat16 [8, 2048, 512], P('batch', 'seq')
- grad_tokens: bfloat16 [8, 2048, 512], P('batch', 'seq')
- grad_ln1_gain: float32 [512], replicated
- grad_ln1_bias: float32 [512], replicated
- grad_w_qkv: float32 [512, 1536], replicated
- grad_w_out: float32 [512, 512], replicated
- grad_ln2_gain: float32 [512], replicated
- grad_ln2_bias: float32 [512], replicated
- grad_w_up: float32 [512, 2048], replicated
- grad_w_down: float32 [2048, 512], replicated
All inputs are finite; a program needn't handle non-finite values.
Results may differ from a plain program's by a relative error of at most 0.011.
Values may be sent and summed in bfloat16 or wider, within the bound.
No kernel may reach another device: no remote copies, remote signals or barrier semaphores. Data moves between devices by JAX's collectives and lax.ppermute only.
A program may use at most 128 MiB of HBM per device.

v0:
```python
from functools import partial
import math

import jax
import jax.numpy as jnp
from jax import lax
from jax.sharding import PartitionSpec as P

HEADS = 8
BLOCK = 16
LEVELS = 6


def shifted(value, axis, by):
    size = lax.axis_size(axis)
    pairs = [(i, i + by) for i in range(size) if 0 <= i + by < size]
    return lax.ppermute(value, axis, pairs)


def layer_norm(values, gain_vec, bias_vec):
    average = jnp.mean(values, axis=-1, keepdims=True)
    centred = values - average
    variance = jnp.mean(centred * centred, axis=-1, keepdims=True)
    return centred * lax.rsqrt(variance + 1e-05) * gain_vec + bias_vec


def level_masks(positions, level_idx):
    group_size = 2**level_idx
    offsets = jnp.arange(2 * BLOCK, dtype=jnp.int32)
    coarse_idx = (positions[:, None] // (BLOCK * group_size) - 1) * BLOCK + offsets[None, :]
    if level_idx == 0:
        return (coarse_idx >= 0) & (coarse_idx <= positions[:, None])
    half_block = BLOCK // 2 * group_size
    finer_start = (positions[:, None] // half_block - 1) * half_block
    return (coarse_idx >= 0) & ((coarse_idx + 1) * group_size <= finer_start)


def body(
    tokens, prefix, cotangent, ln1_gain, ln1_bias, w_qkv, w_out, ln2_gain, ln2_bias, w_up, w_down
):
    row_count, span_len, model_width = tokens.shape
    head_dim = model_width // HEADS
    score_scale = 1.0 / math.sqrt(head_dim)
    positions = lax.axis_index("seq") * span_len + jnp.arange(span_len, dtype=jnp.int32)
    tokens_f = tokens.astype(jnp.float32)
    normed_f, ln1_pull = jax.vjp(
        layer_norm, tokens_f, ln1_gain.astype(jnp.float32), ln1_bias.astype(jnp.float32)
    )
    normed = normed_f.astype(jnp.bfloat16)
    projected = jnp.dot(normed, w_qkv, preferred_element_type=jnp.float32).astype(jnp.bfloat16)
    queries = projected[..., :model_width]
    key_rows = projected[..., model_width : 2 * model_width]
    value_rows = projected[..., 2 * model_width :]
    coarse_keys = [key_rows]
    coarse_vals = [value_rows]
    for level_idx in range(1, LEVELS):
        group_size = 2**level_idx
        grouped_shape = (row_count, span_len // group_size, group_size, model_width)
        coarse_keys.append(
            (
                jnp.sum(key_rows.reshape(grouped_shape), axis=2, dtype=jnp.float32) / group_size
            ).astype(jnp.bfloat16)
        )
        coarse_vals.append(
            (
                jnp.sum(value_rows.reshape(grouped_shape), axis=2, dtype=jnp.float32) / group_size
            ).astype(jnp.bfloat16)
        )
    edge_keys = jnp.concatenate([c[:, -BLOCK:] for c in coarse_keys], axis=1)
    edge_vals = jnp.concatenate([c[:, -BLOCK:] for c in coarse_vals], axis=1)
    recv_keys, recv_vals = shifted((edge_keys, edge_vals), "seq", 1)

    def as_blocks(coarse):
        count = coarse.shape[1] // BLOCK
        return coarse.reshape(row_count, count, BLOCK, HEADS, head_dim)

    prev_keys = []
    own_keys = []
    prev_vals = []
    own_vals = []
    mask_list = []
    for level_idx in range(LEVELS):
        lower = BLOCK * level_idx
        own_k = coarse_keys[level_idx]
        own_v = coarse_vals[level_idx]
        prev_keys.append(
            as_blocks(
                jnp.concatenate([recv_keys[:, lower : lower + BLOCK], own_k[:, :-BLOCK]], axis=1)
            )
        )
        prev_vals.append(
            as_blocks(
                jnp.concatenate([recv_vals[:, lower : lower + BLOCK], own_v[:, :-BLOCK]], axis=1)
            )
        )
        own_keys.append(as_blocks(own_k))
        own_vals.append(as_blocks(own_v))
        mask_list.append(level_masks(positions, level_idx))

    def blocked(tensor, level_idx):
        group_size = 2**level_idx
        block_count = span_len // (BLOCK * group_size)
        return tensor.reshape(row_count, block_count, BLOCK * group_size, HEADS, head_dim)

    def by_level(weights, level_idx):
        group_size = 2**level_idx
        block_count = span_len // (BLOCK * group_size)
        sliced = weights[..., 2 * BLOCK * level_idx : 2 * BLOCK * (level_idx + 1)]
        return sliced.reshape(row_count, block_count, BLOCK * group_size, HEADS, 2 * BLOCK)

    def unblocked(tensor, last_dim):
        return tensor.reshape(row_count, span_len, last_dim)

    def all_scores():
        parts = []
        for level_idx in range(LEVELS):
            query_blk = blocked(queries, level_idx)
            earlier = jnp.einsum(
                "rbqhd,rbkhd->rbqhk",
                query_blk,
                prev_keys[level_idx],
                preferred_element_type=jnp.float32,
            )
            current = jnp.einsum(
                "rbqhd,rbkhd->rbqhk",
                query_blk,
                own_keys[level_idx],
                preferred_element_type=jnp.float32,
            )
            raw_scores = jnp.concatenate([earlier, current], axis=-1)
            raw_scores = raw_scores.reshape(
                row_count, span_len, HEADS, 2 * BLOCK
            ) * score_scale + math.log(2**level_idx)
            parts.append(jnp.where(mask_list[level_idx][None, :, None, :], raw_scores, -1e30))
        return jnp.concatenate(parts, axis=-1)

    scores = all_scores()
    row_max = jnp.max(scores, axis=-1, keepdims=True)
    expo = jnp.exp(scores - row_max)
    denom_sum = jnp.sum(expo, axis=-1, keepdims=True)
    log_total = row_max + jnp.log(denom_sum)
    probs_low = (expo / denom_sum).astype(jnp.bfloat16)
    attended_f = jnp.zeros((row_count, span_len, model_width), jnp.float32)
    for level_idx in range(LEVELS):
        prob_blk = by_level(probs_low, level_idx)
        mixed = jnp.einsum(
            "rbqhk,rbkhd->rbqhd",
            prob_blk[..., :BLOCK],
            prev_vals[level_idx],
            preferred_element_type=jnp.float32,
        )
        mixed = mixed + jnp.einsum(
            "rbqhk,rbkhd->rbqhd",
            prob_blk[..., BLOCK:],
            own_vals[level_idx],
            preferred_element_type=jnp.float32,
        )
        attended_f = attended_f + unblocked(mixed, model_width)
    attended = attended_f.astype(jnp.bfloat16)
    mid = tokens_f + jnp.dot(attended, w_out, preferred_element_type=jnp.float32)
    normed2_f, ln2_pull = jax.vjp(
        layer_norm, mid, ln2_gain.astype(jnp.float32), ln2_bias.astype(jnp.float32)
    )
    normed2 = normed2_f.astype(jnp.bfloat16)
    up_proj = jnp.dot(normed2, w_up, preferred_element_type=jnp.float32)
    hidden_f, gelu_pull = jax.vjp(partial(jax.nn.gelu, approximate=True), up_proj)
    hidden = hidden_f.astype(jnp.bfloat16)
    result = mid + jnp.dot(hidden, w_down, preferred_element_type=jnp.float32)
    scored = (positions[None, :] >= prefix[:, None])[..., None]
    grad_y = jnp.where(scored, cotangent.astype(jnp.float32), 0.0)
    d_ffn = grad_y.astype(jnp.bfloat16)
    grad_down = jnp.einsum("rsf,rsd->fd", hidden, d_ffn, preferred_element_type=jnp.float32)
    d_hidden = jnp.einsum("rsd,fd->rsf", d_ffn, w_down, preferred_element_type=jnp.float32)
    d_up = gelu_pull(d_hidden)[0].astype(jnp.bfloat16)
    grad_up = jnp.einsum("rsd,rsf->df", normed2, d_up, preferred_element_type=jnp.float32)
    d_normed2 = jnp.einsum("rsf,df->rsd", d_up, w_up, preferred_element_type=jnp.float32)
    d_mid, grad_g2, grad_b2 = ln2_pull(d_normed2)
    d_mid = d_mid + grad_y
    d_branch = d_mid.astype(jnp.bfloat16)
    grad_out = jnp.einsum("rsi,rsd->id", attended, d_branch, preferred_element_type=jnp.float32)
    d_attended = jnp.einsum(
        "rsd,id->rsi", d_branch, w_out, preferred_element_type=jnp.float32
    ).astype(jnp.bfloat16)

    def combine(own_grad, prev_grad):
        flat_own = own_grad.reshape(row_count, -1, model_width)
        flat_prev = prev_grad.reshape(row_count, -1, model_width)
        count = flat_own.shape[1]
        whole = flat_own.at[:, : count - BLOCK].add(flat_prev[:, BLOCK:])
        return (whole, flat_prev[:, :BLOCK])

    scores = all_scores()
    soft_probs = jnp.exp(scores - log_total)
    probs_low = soft_probs.astype(jnp.bfloat16)
    grad_prob_parts = []
    full_dvals = []
    lent_dvals = []
    for level_idx in range(LEVELS):
        attended_blk = blocked(d_attended, level_idx)
        earlier = jnp.einsum(
            "rbqhd,rbkhd->rbqhk",
            attended_blk,
            prev_vals[level_idx],
            preferred_element_type=jnp.float32,
        )
        current = jnp.einsum(
            "rbqhd,rbkhd->rbqhk",
            attended_blk,
            own_vals[level_idx],
            preferred_element_type=jnp.float32,
        )
        grad_prob_parts.append(
            jnp.concatenate([earlier, current], axis=-1).reshape(
                row_count, span_len, HEADS, 2 * BLOCK
            )
        )
        prob_blk = by_level(probs_low, level_idx)
        grad_prev = jnp.einsum(
            "rbqhk,rbqhd->rbkhd",
            prob_blk[..., :BLOCK],
            attended_blk,
            preferred_element_type=jnp.float32,
        )
        grad_own = jnp.einsum(
            "rbqhk,rbqhd->rbkhd",
            prob_blk[..., BLOCK:],
            attended_blk,
            preferred_element_type=jnp.float32,
        )
        whole, lent = combine(grad_own, grad_prev)
        full_dvals.append(whole)
        lent_dvals.append(lent)
    grad_probs = jnp.concatenate(grad_prob_parts, axis=-1)
    inner_sum = jnp.sum(soft_probs * grad_probs, axis=-1, keepdims=True)
    d_scores = (soft_probs * (grad_probs - inner_sum)).astype(jnp.bfloat16)
    d_queries = jnp.zeros((row_count, span_len, model_width), jnp.float32)
    full_dkeys = []
    lent_dkeys = []
    for level_idx in range(LEVELS):
        score_blk = by_level(d_scores, level_idx)
        query_blk = blocked(queries, level_idx)
        part = jnp.einsum(
            "rbqhk,rbkhd->rbqhd",
            score_blk[..., :BLOCK],
            prev_keys[level_idx],
            preferred_element_type=jnp.float32,
        )
        part = part + jnp.einsum(
            "rbqhk,rbkhd->rbqhd",
            score_blk[..., BLOCK:],
            own_keys[level_idx],
            preferred_element_type=jnp.float32,
        )
        d_queries = d_queries + unblocked(part, model_width) * score_scale
        grad_prev = (
            jnp.einsum(
                "rbqhk,rbqhd->rbkhd",
                score_blk[..., :BLOCK],
                query_blk,
                preferred_element_type=jnp.float32,
            )
            * score_scale
        )
        grad_own = (
            jnp.einsum(
                "rbqhk,rbqhd->rbkhd",
                score_blk[..., BLOCK:],
                query_blk,
                preferred_element_type=jnp.float32,
            )
            * score_scale
        )
        whole, lent = combine(grad_own, grad_prev)
        full_dkeys.append(whole)
        lent_dkeys.append(lent)
    send_keys = jnp.concatenate(lent_dkeys, axis=1)
    send_vals = jnp.concatenate(lent_dvals, axis=1)
    back_keys, back_vals = (
        shifted(send_keys.astype(jnp.bfloat16), "seq", -1).astype(send_keys.dtype),
        shifted(send_vals.astype(jnp.bfloat16), "seq", -1).astype(send_vals.dtype),
    )

    def settle(full_grads, received):
        settled = None
        for level_idx in range(LEVELS):
            group_size = 2**level_idx
            lower = BLOCK * level_idx
            own_grads = full_grads[level_idx].at[:, -BLOCK:].add(received[:, lower : lower + BLOCK])
            if level_idx == 0:
                settled = own_grads
            else:
                rounded = lax.optimization_barrier(own_grads.astype(jnp.bfloat16)).astype(
                    jnp.float32
                )
                count = rounded.shape[1]
                spread = jnp.broadcast_to(
                    rounded[:, :, None, :], (row_count, count, group_size, model_width)
                )
                settled = settled + spread.reshape(row_count, span_len, model_width) / group_size
        return settled

    d_keys = settle(full_dkeys, back_keys)
    d_values = settle(full_dvals, back_vals)
    d_projected = jnp.concatenate([d_queries, d_keys, d_values], axis=-1).astype(jnp.bfloat16)
    grad_qkv = jnp.einsum("rsd,rse->de", normed, d_projected, preferred_element_type=jnp.float32)
    d_normed = jnp.einsum("rse,de->rsd", d_projected, w_qkv, preferred_element_type=jnp.float32)
    d_tokens, grad_g1, grad_b1 = ln1_pull(d_normed)
    d_tokens = d_tokens + d_mid
    summed = lax.psum(
        (grad_g1, grad_b1, grad_qkv, grad_out, grad_g2, grad_b2, grad_up, grad_down),
        ("batch", "seq"),
    )
    return (
        result.astype(jnp.bfloat16),
        d_tokens.astype(jnp.bfloat16),
        summed[0],
        summed[1],
        summed[2],
        summed[3],
        summed[4],
        summed[5],
        summed[6],
        summed[7],
    )


def solution(mesh):
    placed = (
        P("batch", "seq", None),
        P("batch"),
        P("batch", "seq", None),
        P(),
        P(),
        P(),
        P(),
        P(),
        P(),
        P(),
        P(),
    )
    return jax.shard_map(
        body,
        mesh=mesh,
        in_specs=placed,
        out_specs=(
            P("batch", "seq", None),
            P("batch", "seq", None),
            P(),
            P(),
            P(),
            P(),
            P(),
            P(),
            P(),
            P(),
        ),
        check_vma=False,
    )
```

profile of v0, /device:TPU:0, one launch (start us, length us, event | category | flops | bytes accessed | tf_op | source)
XLA Modules:
  0.0 872.6 jit_solution(5762477387030396082)
XLA Ops:
  11.5 2.5 fusion.8
  16.6 2.8 reshape.3883
  22.0 2.6 bitcast_reduce_fusion.1
  26.6 3.2 reduce_sum.223
  33.2 3.3 reduce_sum.212
  49.1 3.0 collective-permute-start.1
  54.2 2.5 reduce_sum.216
  63.8 4.7 collective-permute-start
  127.7 3.7 convolution_bitcast_fusion.4
  147.5 2.8 reshape.3757
  156.8 3.0 copy.560
  166.1 2.5 copy.565
  168.6 3.1 add.1027
  222.5 2.7 copy.747
  225.3 3.0 copy.604
  230.2 2.7 reshape.3875
  244.1 2.7 reshape.3774
  246.9 3.2 copy.745
  257.3 3.0 copy.599
  260.3 3.1 reshape.3779
  263.4 3.3 copy.746
  269.3 3.9 fusion.43
  273.2 2.6 copy.619
  275.9 2.7 reshape.3889
  278.5 2.7 reshape.3888
  281.2 2.7 reshape.3784
  283.9 3.8 fusion.303
  290.8 3.7 fusion.6
  294.6 2.8 fusion.305
  305.5 3.6 convolution_bitcast_fusion.2
  312.8 3.1 convolution_bitcast_fusion.10
  341.9 2.5 copy.634
  357.7 2.9 multiply_reduce_fusion
  384.0 2.6 copy.653
  386.6 3.1 fusion.285
  400.9 3.4 fusion.274
  404.2 4.2 fusion.108
  419.9 3.4 fusion.287
  430.1 2.7 reshape.3848
  481.7 2.6 copy.785
  494.3 3.8 copy.689
  498.1 2.7 reshape.3834
  502.2 2.5 copy.691
  538.2 2.5 copy.683
  540.8 2.6 fusion.17
  543.4 3.2 copy.760
  546.6 2.7 reshape.3891
  552.9 2.7 reshape.3890
  555.6 3.4 add_bitcast_fusion
  559.0 3.0 copy.668
  562.0 2.8 reshape.3820
  569.2 3.0 reshape.3812
  577.2 2.8 fusion.306
  580.0 3.9 multiply_convert_fusion.2
  590.4 2.6 div.397
  595.5 3.0 div.394
  602.0 2.6 div.382
  606.0 2.9 div.379
  614.4 2.7 fusion.82
  617.2 5.1 fusion.22
  623.3 2.6 fusion.304
  629.3 43.8 %all-reduce = (f32[512]{0:T(512)}, f32[512]{0:T(512)}, f32[512]{0:T(512)}, f32[512]{0:T(512)}) all-reduce(f32[512]{0:T(512)S(1)} %get-tuple-element.332, f32[512]{0:T(512)S(1)} %get-tuple-element.453, f32[512]{0:T(512)S(1)} %copy-done.202, f32[512]{0:T(512)S(1)} %copy-done.218), channel_id=1, replica_groups=mesh['batch'=8,'seq'=4] {'batch','seq'}, use_global_device_ids=true, to_apply=%region_27.28 | all-reduce | flops 2048 | bytes 16384 | tf_op jit(solution)/shard_map/psum | solution.py:309
  673.1 180.5 %all-reduce.4.cloned.1.call-done = (f32[512,1536]{1,0:T(8,128)}, f32[512,512]{1,0:T(8,128)}, f32[512,2048]{1,0:T(8,128)}, f32[2048,512]{1,0:T(8,128)}) async-done(((f32[512,1536]{1,0:T(8,128)}, f32[512,512]{1,0:T(8,128)}, f32[512,2048]{1,0:T(8,128)}, f32[2048,512]{1,0:T(8,128)}), (f32[512,1536]{1,0:T(8,128)}, f32[512,512]{1,0:T(8,128)}, f32[512,2048]{1,0:T(8,128)}, ...) | async-done | bytes 12582928 | tf_op jit(solution)/shard_map/psum | solution.py:309
  853.6 3.9 copy.1094
  (850 shorter events, 440.8 us)
Async XLA Ops:
  7.2 281.9 %copy-start = (bf16[512,2048]{1,0:T(8,128)(2,1)S(1)}, bf16[512,2048]{1,0:T(8,128)(2,1)}, u32[]{:S(2)}) copy-start(bf16[512,2048]{1,0:T(8,128)(2,1)} %param.68) | copy-start | bytes 6291460
  7.2 846.4 %all-reduce.4.cloned.1.call-start = ((), (), s32[]{:S(2)}) async-start(), calls=%async_computation | async-start | bytes 25165824 | tf_op jit(solution)/shard_map/psum | solution.py:309
  26.0 7.3 copy-start.133
  45.2 15.3 %copy-start.134 = (bf16[64,512]{1,0:T(8,128)(2,1)}, bf16[64,512]{1,0:T(8,128)(2,1)S(1)}, u32[]{:S(2)}) copy-start(bf16[64,512]{1,0:T(8,128)(2,1)S(1)} %get-tuple-element.462) | copy-start | bytes 196612
  49.1 93.0 %collective-permute-start.1 = (bf16[1,96,512]{2,1,0:T(8,128)(2,1)}, bf16[1,96,512]{2,1,0:T(8,128)(2,1)}, u32[]{:S(2)}, u32[]{:S(2)}) collective-permute-start(bf16[1,96,512]{2,1,0:T(8,128)(2,1)} %get-tuple-element.350), channel_id=1, source_target_pairs={{0,1},{1,2},{2,3},{4,5},{5,6},{6,7},{8,9},{9,10},{10,11},{12,13},{... | collective-permute-start | bytes 294920 | tf_op jit(solution)/shard_map/ppermute | solution.py:17
  53.6 21.3 %copy-start.136 = (f32[32,512]{1,0:T(8,128)}, f32[32,512]{1,0:T(8,128)S(1)}, u32[]{:S(2)}) copy-start(f32[32,512]{1,0:T(8,128)S(1)} %reduce_sum.218) | copy-start | bytes 196612
  63.8 136.7 %collective-permute-start = (bf16[1,96,512]{2,1,0:T(8,128)(2,1)}, bf16[1,96,512]{2,1,0:T(8,128)(2,1)}, u32[]{:S(2)}, u32[]{:S(2)}) collective-permute-start(bf16[1,96,512]{2,1,0:T(8,128)(2,1)} %get-tuple-element.346), channel_id=1, source_target_pairs={{0,1},{1,2},{2,3},{4,5},{5,6},{6,7},{8,9},{9,10},{10,11},{12,13},{... | collective-permute-start | bytes 294920 | tf_op jit(solution)/shard_map/ppermute | solution.py:17
  70.3 8.6 copy-start.22
  74.9 5.6 copy-start.53
  83.5 88.5 %copy-start.4 = (bf16[8,64,8,64]{3,2,1,0:T(8,128)(2,1)}, bf16[8,64,8,64]{3,2,1,0:T(8,128)(2,1)S(1)}, u32[]{:S(2)}) copy-start(bf16[8,64,8,64]{3,2,1,0:T(8,128)(2,1)S(1)} %reshape.3763) | copy-start | bytes 1572868
  84.2 16.3 %copy-start.85 = (f32[128,512]{1,0:T(8,128)S(1)}, f32[128,512]{1,0:T(8,128)}, u32[]{:S(2)}) copy-start(f32[128,512]{1,0:T(8,128)} %reduce_sum.216) | copy-start | bytes 786436
  86.4 50.8 %copy-start.102 = (bf16[4,16,8,64]{3,2,1,0:T(8,128)(2,1)}, bf16[4,16,8,64]{3,2,1,0:T(8,128)(2,1)S(1)}, u32[]{:S(2)}) copy-start(bf16[4,16,8,64]{3,2,1,0:T(8,128)(2,1)S(1)} %convert_element_type.610) | copy-start | bytes 196612
  106.1 11.4 %copy-start.183 = (bf16[16,512]{1,0:T(8,128)(2,1)S(1)}, bf16[16,512]{1,0:T(8,128)(2,1)}, u32[]{:S(2)}) copy-start(bf16[16,512]{1,0:T(8,128)(2,1)} %get-tuple-element.347) | copy-start | bytes 49156
  108.3 26.3 %copy-start.77 = (bf16[8,16,8,64]{3,2,1,0:T(8,128)(2,1)}, bf16[8,16,8,64]{3,2,1,0:T(8,128)(2,1)S(1)}, u32[]{:S(2)}) copy-start(bf16[8,16,8,64]{3,2,1,0:T(8,128)(2,1)S(1)} %convert_element_type.609) | copy-start | bytes 393220
  132.1 5.1 copy-start.42
  132.1 6.0 copy-start.209
  132.1 6.0 copy-start.211
  132.2 6.7 copy-start.214
  132.2 6.6 copy-start.215
  133.8 5.6 copy-start.56
  133.8 5.6 copy-start.137
  133.8 6.5 copy-start.205
  133.8 6.5 copy-start.208
  133.8 7.2 copy-start.203
  133.8 7.2 copy-start.204
  133.8 7.1 copy-start.206
  143.7 9.0 %copy-start.149 = (bf16[16,8,64]{2,1,0:T(8,128)(2,1)}, bf16[16,8,64]{2,1,0:T(8,128)(2,1)S(1)}, u32[]{:S(2)}) copy-start(bf16[16,8,64]{2,1,0:T(8,128)(2,1)S(1)} %reshape.3768) | copy-start | bytes 49156
  159.8 4.9 copy-start.154
  183.8 8.0 copy-start.146
  183.8 10.7 %copy-start.91 = (f32[512,8,32]{0,2,1:T(8,128)S(1)}, f32[512,8,32]{0,2,1:T(8,128)}, u32[]{:S(2)}) copy-start(f32[512,8,32]{0,2,1:T(8,128)} %copy.560) | copy-start | bytes 1572868
  185.6 9.8 %copy-start.92 = (f32[512,8,32]{0,2,1:T(8,128)S(1)}, f32[512,8,32]{0,2,1:T(8,128)}, u32[]{:S(2)}) copy-start(f32[512,8,32]{0,2,1:T(8,128)} %add.1027) | copy-start | bytes 1572868
  263.4 5.9 copy-start.62
  283.9 5.1 copy-start.161
  283.9 5.1 copy-start.172
  302.7 24.1 %copy-start.23 = (bf16[4,128,8,64]{1,0,3,2:T(4,128)(2,1)}, bf16[4,128,8,64]{1,0,3,2:T(4,128)(2,1)S(1)}, u32[]{:S(2)}) copy-start(bf16[4,128,8,64]{1,0,3,2:T(4,128)(2,1)S(1)} %reshape.3806) | copy-start | bytes 1572868
  321.0 5.8 copy-start.108
  326.8 4.9 copy-start.151
  327.9 7.0 copy-start.61
  366.4 6.3 copy-start.120
  369.6 6.1 copy-start.106
  373.5 7.4 copy-start.5
  409.3 9.0 %copy-start.115 = (bf16[1,512,8,32]{1,3,2,0:T(8,128)(2,1)S(1)}, bf16[1,512,8,32]{1,3,2,0:T(8,128)(2,1)}, u32[]{:S(2)}) copy-start(bf16[1,512,8,32]{1,3,2,0:T(8,128)(2,1)} %get-tuple-element.367) | copy-start | bytes 786436
  445.0 8.3 copy-start.118
  449.1 22.5 %copy-start.109 = (f32[1,64,512]{2,1,0:T(8,128)}, f32[1,64,512]{2,1,0:T(8,128)S(1)}, u32[]{:S(2)}) copy-start(f32[1,64,512]{2,1,0:T(8,128)S(1)} %fusion.164) | copy-start | bytes 393220
  454.0 19.0 %copy-start.124 = (bf16[1,8,64,8,16]{2,1,4,3,0:T(8,128)(2,1)S(1)}, bf16[1,8,64,8,16]{2,1,4,3,0:T(8,128)(2,1)}, u32[]{:S(2)}) copy-start(bf16[1,8,64,8,16]{2,1,4,3,0:T(8,128)(2,1)} %get-tuple-element.401) | copy-start | bytes 393220
  463.7 121.2 %collective-permute-start.3 = (bf16[1,96,512]{2,1,0:T(8,128)(2,1)}, bf16[1,96,512]{2,1,0:T(8,128)(2,1)}, u32[]{:S(2)}, u32[]{:S(2)}) collective-permute-start(bf16[1,96,512]{2,1,0:T(8,128)(2,1)} %constant_dynamic-update-slice_fusion.22), channel_id=1, source_target_pairs={{1,0},{2,1},{3,2},{5,4},{6,5},{7,6},{9,8},{10,9},{11,10},{13,12},{... | collective-permute-start | bytes 294920 | tf_op jit(solution)/shard_map/ppermute | solution.py:17
  491.8 6.2 copy-start.24
  500.8 6.3 copy-start.90
  504.7 13.3 %copy-start.59 = (bf16[2,256,8,64]{1,0,3,2:T(2,128)(2,1)S(1)}, bf16[2,256,8,64]{1,0,3,2:T(2,128)(2,1)}, u32[]{:S(2)}) copy-start(bf16[2,256,8,64]{1,0,3,2:T(2,128)(2,1)} %reshape.3767) | copy-start | bytes 1572868
  507.1 12.9 %copy-start.83 = (bf16[1,8,64,8,16]{2,1,4,3,0:T(8,128)(2,1)S(1)}, bf16[1,8,64,8,16]{2,1,4,3,0:T(8,128)(2,1)}, u32[]{:S(2)}) copy-start(bf16[1,8,64,8,16]{2,1,4,3,0:T(8,128)(2,1)} %get-tuple-element.399) | copy-start | bytes 393220
  509.2 10.1 %copy-start.129 = (f32[1,128,512]{2,1,0:T(8,128)}, f32[1,128,512]{2,1,0:T(8,128)S(1)}, u32[]{:S(2)}) copy-start(f32[1,128,512]{2,1,0:T(8,128)S(1)} %reshape.3836) | copy-start | bytes 786436
  510.3 11.1 %copy-start.111 = (f32[1,64,512]{2,1,0:T(8,128)}, f32[1,64,512]{2,1,0:T(8,128)S(1)}, u32[]{:S(2)}) copy-start(f32[1,64,512]{2,1,0:T(8,128)S(1)} %fusion.165) | copy-start | bytes 393220
  516.7 81.7 %collective-permute-start.2 = (bf16[1,96,512]{2,1,0:T(8,128)(2,1)}, bf16[1,96,512]{2,1,0:T(8,128)(2,1)}, u32[]{:S(2)}, u32[]{:S(2)}) collective-permute-start(bf16[1,96,512]{2,1,0:T(8,128)(2,1)} %constant_dynamic-update-slice_fusion.16), channel_id=1, source_target_pairs={{1,0},{2,1},{3,2},{5,4},{6,5},{7,6},{9,8},{10,9},{11,10},{13,12},{... | collective-permute-start | bytes 294920 | tf_op jit(solution)/shard_map/ppermute | solution.py:17
  524.7 5.7 copy-start.13
  524.7 5.7 copy-start.35
  580.0 5.8 copy-start.25
  580.0 5.8 copy-start.46
  580.0 5.8 copy-start.110
  593.0 6.3 copy-start.47
  593.0 6.4 copy-start.88
  593.0 6.4 copy-start.112
  593.0 6.4 copy-start.132
  593.0 6.4 copy-start.171
  617.2 6.2 copy-start.144
  (168 other events, 401.2 us)
Sparse Core Ops, SparseCore 0:
  617.3 236.2 all-reduce.3
where the time goes:
time: 887 us; the launch traced here: 873 us
  local copies, waits for them, and re-layouts  366 us (41%)
  waiting for transfers between devices  181 us (20%)
  matrix products  140 us (16%)
  other arithmetic  113 us (13%)
  blocking collectives  43.8 us (5%)
  between operations  17.8 us (2%)
  starting transfers between devices  10.3 us (1%)
    psum x1, waiting for transfers between devices, body(): lax.psum((grad_g1, grad_b1, grad_qkv, grad_out, grad_g2, grad_b2, grad_up...  181 us
    unnamed x478, local copies, waits for them, and re-layouts  57.2 us
    reshape x20, local copies, waits for them, and re-layouts, unblocked(): return tensor.reshape(row_count, span_len, last_dim)  51.8 us
    psum x1, blocking collectives, body(): lax.psum((grad_g1, grad_b1, grad_qkv, grad_out, grad_g2, grad_b2, grad_up...  43.8 us
    another operation x25, local copies, waits for them, and re-layouts  31.4 us
  transfers between devices with their start and end apart: 5, of which 1 were waited for; matrix products, arithmetic and copies ran while one was open for 32% of the time, Pallas kernels for 0%

commit v1 on v0

v1 whole, which is shorter than its diff:
```python
from functools import partial
import math

import jax
import jax.numpy as jnp
from jax import lax
from jax.experimental import pallas as pl
from jax.experimental.pallas import tpu as pltpu
from jax.sharding import PartitionSpec as P

HEADS = 8
BLOCK = 16
LEVELS = 6
CHUNK = 32
KEYS = 128
f32 = jnp.float32
bf16 = jnp.bfloat16


def nn(a, b):
    return lax.dot_general(a, b, (((1,), (0,)), ((), ())), preferred_element_type=f32)


def nt(a, b):
    return lax.dot_general(a, b, (((1,), (1,)), ((), ())), preferred_element_type=f32)


def tn(a, b):
    return lax.dot_general(a, b, (((0,), (0,)), ((), ())), preferred_element_type=f32)


def call(kernel, outs, *args, scratch=(), smem=(), name=None, flops=0, limit=40):
    specs = [
        pl.BlockSpec(memory_space=pltpu.SMEM if i in smem else pltpu.VMEM) for i in range(len(args))
    ]
    return pl.pallas_call(
        kernel,
        out_shape=[jax.ShapeDtypeStruct(s, d) for s, d in outs],
        in_specs=specs,
        out_specs=[pl.BlockSpec(memory_space=pltpu.VMEM)] * len(outs),
        scratch_shapes=scratch,
        compiler_params=pltpu.CompilerParams(vmem_limit_bytes=limit * 2**20),
        cost_estimate=pl.CostEstimate(flops=flops, bytes_accessed=2**20, transcendentals=0),
        name=name,
    )(*args)


def level_start(span, level):
    return span - (span >> (level - 1)) if level else 0


def unit(values):
    centred = values - jnp.mean(values, axis=-1, keepdims=True)
    inv = lax.rsqrt(jnp.mean(centred * centred, axis=-1, keepdims=True) + 1e-05)
    return centred * inv, inv


def unit_back(grad, hat, inv):
    along = jnp.mean(grad * hat, axis=-1, keepdims=True)
    return inv * (grad - jnp.mean(grad, axis=-1, keepdims=True) - hat * along)


def pool_matrix(span):
    parts = []
    for level in range(1, LEVELS):
        rows = span >> level
        row = lax.broadcasted_iota(jnp.int32, (rows, span), 0)
        col = lax.broadcasted_iota(jnp.int32, (rows, span), 1)
        parts.append(jnp.where((col >> level) == row, 1.0 / 2**level, 0.0))
    return jnp.concatenate(parts, axis=0).astype(bf16)


def project_kv(tokens, gain, bias, w_qkv, normed, kv, coarse, edge):
    span, width = tokens.shape
    hat, _ = unit(tokens[...].astype(f32))
    rows = (hat * gain[...].astype(f32) + bias[...].astype(f32)).astype(bf16)
    normed[...] = rows
    both = nn(rows, w_qkv[:, width:]).astype(bf16)
    kv[...] = both
    pooled = nn(pool_matrix(span), both).astype(bf16)
    coarse[...] = pooled
    edge[0:BLOCK] = both[span - BLOCK :]
    for level in range(1, LEVELS):
        end = level_start(span, level + 1)
        edge[BLOCK * level : BLOCK * (level + 1)] = pooled[end - BLOCK : end]


def project_q(place, normed, w_qkv, cotangent, w_down, queries, d_ffn, d_hidden):
    span, width = normed.shape
    q = nn(normed[...], w_qkv[:, :width]).astype(bf16).astype(f32)
    queries[...] = (q * (1.0 / math.sqrt(width // HEADS))).astype(bf16)
    position = place[0] * span + lax.broadcasted_iota(jnp.int32, (span, width), 0)
    masked = jnp.where(position >= place[2], cotangent[...].astype(f32), 0.0).astype(bf16)
    d_ffn[...] = masked
    d_hidden[...] = nt(masked, w_down[...])


def window_bias(chunk, first):
    row = lax.broadcasted_iota(jnp.int32, (CHUNK, KEYS), 0)
    col = lax.broadcasted_iota(jnp.int32, (CHUNK, KEYS), 1)
    late = row >= BLOCK
    low = jnp.where(late, BLOCK, 0)
    edge = 3 * BLOCK
    ok = (col >= low) & (col <= BLOCK + row)
    if chunk == 0:
        ok = ok & ((col >= BLOCK) | jnp.logical_not(first))
    bias = jnp.where(ok & (col < edge), 0.0, -1e30)
    for level in range(1, LEVELS):
        start = edge + BLOCK * (level - 1)
        inside = (col >= start) & (col < start + BLOCK)
        half = inside & (col < start + BLOCK // 2)
        if level == 1:
            ok = half | (inside & late)
        else:
            ok = inside if (chunk >> (level - 2)) & 1 else half
        if chunk >> (level - 1) == 0:
            ok = ok & jnp.logical_not(first)
        bias = jnp.where(ok, math.log(2**level), bias)
    return bias


def window_rows(kv, coarse, recv, chunk, low, high, span):
    start = CHUNK * chunk
    if chunk == 0:
        parts = [recv[0:BLOCK, low:high], kv[0:CHUNK, low:high]]
    else:
        parts = [kv[start - BLOCK : start + CHUNK, low:high]]
    for level in range(1, LEVELS):
        block = chunk >> (level - 1)
        if block == 0:
            parts.append(recv[BLOCK * level : BLOCK * (level + 1), low:high])
        else:
            base = level_start(span, level) + BLOCK * (block - 1)
            parts.append(coarse[base : base + BLOCK, low:high])
    return jnp.concatenate(parts, axis=0)


def by_head(rows):
    lane = lax.broadcasted_iota(jnp.int32, (CHUNK, 128), 1)
    zero = jnp.zeros((CHUNK, 128), bf16)
    pairs = []
    for pair in range(HEADS // 2):
        part = rows[:, 128 * pair : 128 * (pair + 1)]
        pairs.append(
            jnp.concatenate(
                [jnp.where(lane < 64, part, zero), jnp.where(lane >= 64, part, zero)], axis=0
            )
        )
    return pairs


def from_heads(pairs):
    lane = lax.broadcasted_iota(jnp.int32, (CHUNK, 128), 1)
    return jnp.concatenate([jnp.where(lane < 64, p[:CHUNK], p[CHUNK:]) for p in pairs], axis=1)


def attend(place, queries, kv, coarse, recv, attended, probs):
    span, width = queries.shape
    first = place[0] == 0
    rows = CHUNK * HEADS
    for chunk in range(span // CHUNK):
        start = CHUNK * chunk
        bias = window_bias(chunk, first)
        keys = window_rows(kv, coarse, recv, chunk, 0, width, span)
        vals = window_rows(kv, coarse, recv, chunk, width, 2 * width, span)
        split = by_head(queries[start : start + CHUNK])
        raw = [nt(s, keys[:, 128 * p : 128 * (p + 1)]) for p, s in enumerate(split)]
        scores = jnp.concatenate(raw, axis=0) + jnp.concatenate([bias] * HEADS, axis=0)
        expo = jnp.exp(scores - jnp.max(scores, axis=-1, keepdims=True))
        soft = expo / jnp.sum(expo, axis=-1, keepdims=True)
        low = soft.astype(bf16)
        probs[rows * chunk : rows * (chunk + 1)] = low
        mixed = [
            nn(low[64 * p : 64 * (p + 1)], vals[:, 128 * p : 128 * (p + 1)])
            for p in range(HEADS // 2)
        ]
        attended[start : start + CHUNK] = from_heads(mixed).astype(bf16)


def halves(whole, keep, send, core):
    rows = keep.shape[0]
    keep[...] = whole[pl.ds(core * rows, rows)]
    send[...] = whole[pl.ds((1 - core) * rows, rows)]


def feed_forward(
    attended, tokens, w_out, gain, bias, w_up, d_hidden, d_ffn, place, mid, normed, hidden, d_up, keep, send, whole
):
    span, width = tokens.shape
    ff = w_up.shape[1]
    middle = tokens[...].astype(f32) + nn(attended[...], w_out[...])
    mid[...] = middle
    hat, _ = unit(middle)
    rows = (hat * gain[...].astype(f32) + bias[...].astype(f32)).astype(bf16)
    normed[...] = rows
    c0 = math.sqrt(2.0 / math.pi)
    tile = 256
    for start in range(0, ff, tile):
        cols = slice(start, start + tile)
        x = nn(rows, w_up[:, cols])
        square = x * x
        half = 0.5 + 0.5 * jnp.tanh(x * (c0 + (c0 * 0.044715) * square))
        act = (x * half).astype(bf16)
        slope = half + 2.0 * half * (1.0 - half) * x * (c0 + (3 * c0 * 0.044715) * square)
        hidden[:, cols] = act
        d_up[:, cols] = (slope * d_hidden[:, cols]).astype(bf16)
        whole[cols] = tn(act, d_ffn[...]).astype(bf16)
    halves(whole, keep, send, place[1])


def up_back(normed, d_up, place, keep, send, whole):
    width = normed.shape[1]
    for part in range(d_up.shape[1] // width):
        cols = slice(width * part, width * (part + 1))
        whole[cols] = tn(normed[...], d_up[:, cols]).astype(bf16)
    halves(whole, keep, send, place[1])


def mid_back(
    mid, hidden, w_down, d_up, w_up, gain, d_ffn, attended, w_out, out, d_mid, d_attended, grad_out, grad_norm
):
    middle = mid[...]
    out[...] = (middle + nn(hidden[...], w_down[...])).astype(bf16)
    d_normed = nt(d_up[...], w_up[...])
    hat, inv = unit(middle)
    grad_norm[0:1] = jnp.sum(d_normed * hat, axis=0, keepdims=True)
    grad_norm[1:2] = jnp.sum(d_normed, axis=0, keepdims=True)
    d_middle = d_ffn[...].astype(f32) + unit_back(d_normed * gain[...].astype(f32), hat, inv)
    d_mid[...] = d_middle
    d_branch = d_middle.astype(bf16)
    grad_out[...] = tn(attended[...], d_branch).astype(bf16)
    d_attended[...] = nt(d_branch, w_out[...]).astype(bf16)


def attend_back(queries, kv, coarse, recv, probs, d_attended, d_queries, fine, wide, lent):
    span, width = queries.shape
    rows = CHUNK * HEADS
    scale = 1.0 / math.sqrt(width // HEADS)
    fine[...] = jnp.zeros_like(fine)
    wide[...] = jnp.zeros_like(wide)
    zero = jnp.zeros((2 * CHUNK, 128), bf16)
    for chunk in range(span // CHUNK):
        start = CHUNK * chunk
        keys = window_rows(kv, coarse, recv, chunk, 0, width, span)
        vals = window_rows(kv, coarse, recv, chunk, width, 2 * width, span)
        split_q = by_head(queries[start : start + CHUNK])
        split_a = by_head(d_attended[start : start + CHUNK])
        low = probs[rows * chunk : rows * (chunk + 1)]
        soft = low.astype(f32)
        d_probs = jnp.concatenate(
            [nt(s, vals[:, 128 * p : 128 * (p + 1)]) for p, s in enumerate(split_a)], axis=0
        )
        inner = jnp.sum(soft * d_probs, axis=-1, keepdims=True)
        d_scores = (soft * (d_probs - inner)).astype(bf16)
        mixed = [
            nn(d_scores[64 * p : 64 * (p + 1)], keys[:, 128 * p : 128 * (p + 1)])
            for p in range(HEADS // 2)
        ]
        d_queries[start : start + CHUNK] = (from_heads(mixed) * scale).astype(bf16)
        for part, (left, split) in enumerate(((d_scores, split_q), (low, split_a))):
            for quad in range(HEADS // 4):
                pair = 2 * quad
                right = jnp.concatenate(
                    [
                        jnp.concatenate([split[pair], zero], axis=1),
                        jnp.concatenate([zero, split[pair + 1]], axis=1),
                    ],
                    axis=0,
                )
                grad = tn(left[128 * quad : 128 * (quad + 1)], right)
                cols = slice(width * part + 256 * quad, width * part + 256 * (quad + 1))
                fine[start : start + 3 * BLOCK, cols] += grad[: 3 * BLOCK]
                for level in range(1, LEVELS):
                    base = level_start(span, level) + BLOCK * (chunk >> (level - 1))
                    at = BLOCK * (level + 2)
                    wide[base : base + BLOCK, cols] += grad[at : at + BLOCK]
    lent[0:BLOCK] = fine[0:BLOCK].astype(bf16)
    for level in range(1, LEVELS):
        base = level_start(span, level)
        lent[BLOCK * level : BLOCK * (level + 1)] = wide[base : base + BLOCK].astype(bf16)


def project_back(
    fine, wide, back, d_queries, normed, w_qkv, tokens, gain, d_mid, grad_out, grad_norm, place,
    d_tokens, keep, send, d_proj, whole,
):
    span, width = tokens.shape
    parts = []
    for level in range(1, LEVELS):
        base, end = level_start(span, level), level_start(span, level + 1)
        if base + BLOCK < end:
            parts.append(wide[base + BLOCK : end].astype(bf16))
        parts.append(back[BLOCK * level : BLOCK * (level + 1)])
    spread = tn(pool_matrix(span), jnp.concatenate(parts, axis=0))
    d_proj[:, :width] = d_queries[...]
    body = span - BLOCK
    d_proj[:body, width:] = (fine[BLOCK:span] + spread[:body]).astype(bf16)
    d_proj[body:, width:] = (
        fine[span:] + back[0:BLOCK].astype(f32) + spread[body:]
    ).astype(bf16)
    grads = d_proj[...]
    whole[:, : 3 * width] = tn(normed[...], grads).astype(bf16)
    whole[:, 3 * width : 4 * width] = grad_out[...]
    d_normed = nt(grads, w_qkv[...])
    hat, inv = unit(tokens[...].astype(f32))
    d_tokens[...] = (
        d_mid[...] + unit_back(d_normed * gain[...].astype(f32), hat, inv)
    ).astype(bf16)
    rows = [
        jnp.sum(d_normed * hat, axis=0, keepdims=True),
        jnp.sum(d_normed, axis=0, keepdims=True),
        grad_norm[0:2],
        jnp.zeros((124, width), f32),
    ]
    whole[:, 4 * width :] = jnp.concatenate(rows, axis=0).T.astype(bf16)
    halves(whole, keep, send, place[1])


def flips(size, bit):
    return [(i, i ^ (1 << bit)) for i in range(size)]


def reduce_scatter(keep, send, orders, index, size):
    axes = ("batch", "seq")
    own = keep.astype(f32) + lax.ppermute(send, axes, flips(size, 0)).astype(f32)
    own = own.astype(bf16)
    for even, odd in zip(*orders):
        rows = own.shape[0] // 2
        bit = jnp.where(index & 1, (index >> odd) & 1, (index >> even) & 1)
        pairs = [(i, i ^ (1 << (odd if i & 1 else even))) for i in range(size)]
        away = lax.dynamic_slice_in_dim(own, (1 - bit) * rows, rows, 0)
        here = lax.dynamic_slice_in_dim(own, bit * rows, rows, 0)
        own = (here.astype(f32) + lax.ppermute(away, axes, pairs).astype(f32)).astype(bf16)
    return own


def all_gather(own, orders, index, size):
    axes = ("batch", "seq")
    steps = [(0, 0)] + list(zip(*orders))
    for even, odd in reversed(steps):
        bit = jnp.where(index & 1, (index >> odd) & 1, (index >> even) & 1)
        pairs = [(i, i ^ (1 << (odd if i & 1 else even))) for i in range(size)]
        other = lax.ppermute(own, axes, pairs)
        own = jnp.where(
            bit == 0, jnp.concatenate([own, other], 0), jnp.concatenate([other, own], 0)
        )
    return own


def body(
    tokens, prefix, cotangent, ln1_gain, ln1_bias, w_qkv, w_out, ln2_gain, ln2_bias, w_up, w_down
):
    row_count, span, width = tokens.shape
    ff = w_up.shape[1]
    seq_size, batch_size = lax.axis_size("seq"), lax.axis_size("batch")
    size = seq_size * batch_size
    seq_at = lax.axis_index("seq")
    index = lax.axis_index("batch") * seq_size + seq_at
    place = jnp.stack([seq_at, index & 1, prefix[0], prefix[0]]).astype(jnp.int32)
    tokens = tokens.reshape(span, width)
    cotangent = cotangent.reshape(span, width)
    gain1, bias1, gain2, bias2 = (
        v.reshape(1, width) for v in (ln1_gain, ln1_bias, ln2_gain, ln2_bias)
    )
    edge_rows = BLOCK * LEVELS
    coarse_rows = level_start(span, LEVELS)
    normed1, kv, coarse, edge = call(
        project_kv,
        [((span, width), bf16), ((span, 2 * width), bf16), ((coarse_rows, 2 * width), bf16), ((edge_rows, 2 * width), bf16)],
        tokens, gain1, bias1, w_qkv,
        name="project_kv",
    )
    onward = [(i, i + 1) for i in range(seq_size - 1)]
    recv = lax.ppermute(edge, "seq", onward)
    queries, d_ffn, d_hidden = call(
        project_q,
        [((span, width), bf16), ((span, width), bf16), ((span, ff), f32)],
        place, normed1, w_qkv, cotangent, w_down,
        smem=(0,), name="project_q",
    )
    attended, probs = call(
        attend,
        [((span, width), bf16), ((span * HEADS, KEYS), bf16)],
        place, queries, kv, coarse, recv,
        smem=(0,), name="attend",
    )
    mid, normed2, hidden, d_up, keep_down, send_down = call(
        feed_forward,
        [((span, width), f32), ((span, width), bf16), ((span, ff), bf16), ((span, ff), bf16),
         ((ff // 2, width), bf16), ((ff // 2, width), bf16)],
        attended, tokens, w_out, gain2, bias2, w_up, d_hidden, d_ffn, place,
        smem=(8,), scratch=[pltpu.VMEM((ff, width), bf16)], name="feed_forward",
    )
    keep_up, send_up = call(
        up_back,
        [((ff // 2, width), bf16), ((ff // 2, width), bf16)],
        normed2, d_up, place,
        smem=(2,), scratch=[pltpu.VMEM((ff, width), bf16)], name="up_back",
    )
    out, d_mid, d_attended, grad_out, grad_norm = call(
        mid_back,
        [((span, width), bf16), ((span, width), f32), ((span, width), bf16), ((width, width), bf16), ((8, width), f32)],
        mid, hidden, w_down, d_up, w_up, gain2, d_ffn, attended, w_out,
        name="mid_back",
    )
    d_queries, fine, wide, lent = call(
        attend_back,
        [((span, width), bf16), ((span + BLOCK, 2 * width), f32), ((coarse_rows, 2 * width), f32), ((edge_rows, 2 * width), bf16)],
        queries, kv, coarse, recv, probs, d_attended,
        name="attend_back",
    )
    back = lax.ppermute(lent, "seq", [(b, a) for a, b in onward])
    d_tokens, keep_qkv, send_qkv = call(
        project_back,
        [((span, width), bf16), ((width // 2, 4 * width + 128), bf16), ((width // 2, 4 * width + 128), bf16)],
        fine, wide, back, d_queries, normed1, w_qkv, tokens, gain1, d_mid, grad_out, grad_norm, place,
        smem=(11,),
        scratch=[pltpu.VMEM((span, 3 * width), bf16), pltpu.VMEM((width, 4 * width + 128), bf16)],
        name="project_back",
    )
    bits = range(1, size.bit_length() - 1)
    orders = (list(bits), [2, 1] + list(bits)[2:])
    down = all_gather(reduce_scatter(keep_down, send_down, orders, index, size), orders, index, size)
    up = all_gather(reduce_scatter(keep_up, send_up, orders, index, size), orders, index, size)
    rest = all_gather(reduce_scatter(keep_qkv, send_qkv, orders, index, size), orders, index, size)
    parts = up.shape[0] // width
    up = jnp.concatenate([up[width * i : width * (i + 1)] for i in range(parts)], axis=1)
    small = rest[:, 4 * width :].astype(f32)
    return (
        out.reshape(row_count, span, width),
        d_tokens.reshape(row_count, span, width),
        small[:, 0],
        small[:, 1],
        rest[:, : 3 * width].astype(f32),
        rest[:, 3 * width : 4 * width].astype(f32),
        small[:, 2],
        small[:, 3],
        up.astype(f32),
        down.astype(f32),
    )


def solution(mesh):
    placed = (
        P("batch", "seq", None),
        P("batch"),
        P("batch", "seq", None),
        P(),
        P(),
        P(),
        P(),
        P(),
        P(),
        P(),
        P(),
    )
    return jax.shard_map(
        body,
        mesh=mesh,
        in_specs=placed,
        out_specs=(
            P("batch", "seq", None),
            P("batch", "seq", None),
            P(),
            P(),
            P(),
            P(),
            P(),
            P(),
            P(),
            P(),
        ),
        check_vma=False,
    )
```

time: 887 us -> 164 us (0.18); the launches traced: 873 us -> 163 us
  local copies, waits for them, and re-layouts: 366 us -> 15 us
  matrix products: 140 us -> 0 us
  waiting for transfers between devices: 181 us -> 53.4 us
  other arithmetic: 113 us -> 19.7 us
  blocking collectives: 43.8 us -> 0 us
  Pallas kernels: 0 us -> 35.5 us
  starting transfers between devices: 10.3 us -> 37.6 us
  between operations: 17.8 us -> 1.84 us
    psum x1 -> x0, waiting for transfers between devices: 181 us -> none  [body(): lax.psum((grad_g1, grad_b1, grad_qkv, grad_out, grad_g2, grad_b2, grad_up...]
    dot_general x84 -> x0, matrix products: 140 us -> none  [the longest x6 13 us: body(): jnp.einsum('rbqhk,rbkhd->rbqhd', score_blk[..., BLOCK:], own_keys[level_i...]
    reshape x54 -> x4, local copies, waits for them, and re-layouts: 97 us -> 1.39 us  [body(): v.reshape(1, width)]
    ppermute x4 -> x32, waiting for transfers between devices: 0.01 us -> 53.4 us  [the longest x12 25.8 us: reduce_scatter(): lax.ppermute(away, axes, pairs).astype(f32)]
    slice x36 -> x2, local copies, waits for them, and re-layouts: 48.9 us -> 1.29 us  [the longest x1 1.16 us: body(): small[:, 3]]
    unnamed x478 -> x46, local copies, waits for them, and re-layouts: 57.2 us -> 12 us
    psum x1 -> x0, blocking collectives: 43.8 us -> none  [body(): lax.psum((grad_g1, grad_b1, grad_qkv, grad_out, grad_g2, grad_b2, grad_up...]
    add x17 -> x0, local copies, waits for them, and re-layouts: 35.5 us -> none  [the longest x6 14.4 us: body(): mixed + jnp.einsum('rbqhk,rbkhd->rbqhd', prob_blk[..., BLOCK:], own_vals[...]
  transfers between devices with their start and end apart: 5 -> 32, of which waited for: 1 -> 14; matrix products, arithmetic and copies ran while one was open for 32% -> 10% of each run, Pallas kernels for 0% -> 10%
where the time goes in v1:
time: 164 us; the launch traced here: 163 us
  waiting for transfers between devices  53.4 us (33%)
  starting transfers between devices  37.6 us (23%)
  Pallas kernels  35.5 us (22%)
  other arithmetic  19.7 us (12%)
  local copies, waits for them, and re-layouts  15 us (9%)
  between operations  1.84 us (1%)
    pallas_call x8, Pallas kernels, call(): pl.pallas_call(kernel, out_shape=[jax.ShapeDtypeStruct(s, d) for s, d in...  35.5 us
    ppermute x12, waiting for transfers between devices, reduce_scatter(): lax.ppermute(away, axes, pairs).astype(f32)  25.8 us
    ppermute x15, waiting for transfers between devices, all_gather(): other = lax.ppermute(own, axes, pairs)  25.6 us
    ppermute x12, starting transfers between devices, reduce_scatter(): lax.ppermute(away, axes, pairs).astype(f32)  16.9 us
    unnamed x46, local copies, waits for them, and re-layouts  12 us
    ppermute x15, starting transfers between devices, all_gather(): other = lax.ppermute(own, axes, pairs)  10.3 us
    select_n x14, other arithmetic, all_gather(): jnp.where(bit == 0, jnp.concatenate([own, other], 0), jnp.concatenate([ot...  6.86 us
    ppermute x3, starting transfers between devices, reduce_scatter(): lax.ppermute(send, axes, flips(size, 0)).astype(f32)  6.8 us
  transfers between devices with their start and end apart: 32, of which 14 were waited for; matrix products, arithmetic and copies ran while one was open for 10% of the time, Pallas kernels for 10%

profile of v1, /device:TPU:0, one launch (start us, length us, event | category | flops | bytes accessed | tf_op | source)
XLA Modules:
  0.0 163.1 jit_solution(609723423623540455)
XLA Ops:
  0.7 0.7 reshape.45.gain
  1.4 0.7 reshape.46.bias
  2.0 1.4 copy-done
  3.5 1.0 copy-done.5
  4.5 1.5 project_kv.1
  6.0 0.9 copy-done.8
  7.0 2.4 %collective-permute-start = (bf16[96,1024]{1,0:T(8,128)(2,1)S(1)}, bf16[96,1024]{1,0:T(8,128)(2,1)S(1)}, u32[]{:S(2)}, u32[]{:S(2)}) collective-permute-start(bf16[96,1024]{1,0:T(8,128)(2,1)S(1)} %get-tuple-element.43), channel_id=1, source_target_pairs={{0,1},{1,2},{2,3},{4,5},{5,6},{6,7},{8,9},{9,10},{10,11},{12,13},{... | collective-permute-start | bytes 589832 | tf_op jit(solution)/shard_map/ppermute | solution.py:374
  10.1 1.6 copy-done.2
  11.7 1.0 copy-done.20
  12.8 2.1 %project_q.1 = (bf16[512,512]{1,0:T(8,128)(2,1)S(1)}, bf16[512,512]{1,0:T(8,128)(2,1)S(1)}, f32[512,2048]{1,0:T(8,128)S(1)}) custom-call(s32[4]{0:T(128)S(1)} %pad_add_fusion.place, bf16[512,512]{1,0:T(8,128)(2,1)S(1)} %get-tuple-element.39.normed, bf16[512,1536]{1,0:T(8,128)(2,1)S(1)} %copy-done.1, bf16[512,512]{1,0:T(8,128)(2,1)S(1)} %bitcast.9, ...), custom_call_target="tpu_custom_call" | custom-call | bytes 1048576 | tf_op jit(solution)/shard_map/project_q/pallas_call | solution.py:36
  14.9 2.0 %copy-done.7 = f32[512,2048]{1,0:T(8,128)} copy-done((f32[512,2048]{1,0:T(8,128)}, f32[512,2048]{1,0:T(8,128)S(1)}, u32[]{:S(2)}) %copy-start.7) | copy-done | bytes 4194328
  16.9 6.8 %attend.1 = (bf16[512,512]{1,0:T(8,128)(2,1)S(1)}, bf16[4096,128]{1,0:T(8,128)(2,1)S(1)}) custom-call(s32[4]{0:T(128)S(1)} %pad_add_fusion.place, bf16[512,512]{1,0:T(8,128)(2,1)S(1)} %get-tuple-element.40.queries, bf16[512,1024]{1,0:T(8,128)(2,1)S(1)} %get-tuple-element.41.kv, bf16[496,1024]{1,0:T(8,128)(2,1)S(1)} %copy-done.9, ...), custom_call_target="tpu_custom_call" | custom-call | bytes 1048576 | tf_op jit(solution)/shard_map/attend/pallas_call | solution.py:36
  23.7 8.0 %feed_forward.1 = (f32[512,512]{1,0:T(8,128)S(1)}, bf16[512,512]{1,0:T(8,128)(2,1)S(1)}, bf16[512,2048]{1,0:T(8,128)(2,1)S(1)}, bf16[512,2048]{1,0:T(8,128)(2,1)...) custom-call(bf16[512,512]{1,0:T(8,128)(2,1)S(1)} %get-tuple-element.44.attended, ...), custom_call_target="tpu_custom_call" | custom-call | bytes 1048576 | tf_op jit(solution)/shard_map/feed_forward/pallas_call | solution.py:36
  31.8 1.0 copy-done.14
  32.8 2.9 %up_back.1 = (bf16[1024,512]{1,0:T(8,128)(2,1)S(1)}, bf16[1024,512]{1,0:T(8,128)(2,1)}) custom-call(bf16[512,512]{1,0:T(8,128)(2,1)S(1)} %get-tuple-element.63.normed, bf16[512,2048]{1,0:T(8,128)(2,1)S(1)} %get-tuple-element.49.d_up, s32[4]{0:T(128)S(1)} %pad_add_fusion.place), custom_call_target="tpu_custom_call" | custom-call | bytes 1048576 | tf_op jit(solution)/shard_map/up_back/pallas_call | solution.py:36
  35.7 1.0 copy-done.16
  36.7 2.6 %collective-permute-start.12 = (bf16[1024,512]{1,0:T(8,128)(2,1)}, bf16[1024,512]{1,0:T(8,128)(2,1)}, u32[]{:S(2)}, u32[]{:S(2)}) collective-permute-start(bf16[1024,512]{1,0:T(8,128)(2,1)} %get-tuple-element.65), channel_id=1, source_target_pairs={{0,1},{1,0},{2,3},{3,2},{4,5},{5,4},{6,7},{7,6},{8,9},{9,8},{10,11... | collective-permute-start | bytes 3145736 | tf_op jit(solution)/shard_map/ppermute | solution.py:325
  39.4 3.7 %mid_back.1 = (bf16[512,512]{1,0:T(8,128)(2,1)}, f32[512,512]{1,0:T(8,128)S(1)}, bf16[512,512]{1,0:T(8,128)(2,1)S(1)}, bf16[512,512]{1,0:T(8,128)(2,1)S(1)}, f32[8,512]{1,0:T(8,128)S(1)}) custom-call(f32[512,512]{1,0:T(8,128)S(1)} %get-tuple-element.47.mid, bf16[512,2048]{1,0:T(8,128)(2,1)S(1)} %get-tuple-element.48.hidden, bf16[2048,512]{1,0:T(8,128)(2,1)S(1)} %copy-done.3, ...), custom_call_target="tpu_custom_call" | custom-call | bytes 1048576 | tf_op jit(solution)/shard_map/mid_back/pallas_call | solution.py:36
  43.0 1.0 copy-done.18
  44.0 5.9 %attend_back.1 = (bf16[512,512]{1,0:T(8,128)(2,1)S(1)}, f32[528,1024]{1,0:T(8,128)S(1)}, f32[496,1024]{1,0:T(8,128)S(1)}, bf16[96,1024]{1,0:T(8,128)(2,1)S(1)}) custom-call(bf16[512,512]{1,0:T(8,128)(2,1)S(1)} %get-tuple-element.40.queries, bf16[512,1024]{1,0:T(8,128)(2,1)S(1)} %get-tuple-element.41.kv, bf16[496,1024]{1,0:T(8,128)(2,1)S(1)} %copy-done.9, ...), custom_call_target="tpu_custom_call" | custom-call | bytes 1048576 | tf_op jit(solution)/shard_map/attend_back/pallas_call | solution.py:36
  49.9 1.3 collective-permute-start.1
  51.2 2.0 %collective-permute-done.1.back = bf16[96,1024]{1,0:T(8,128)(2,1)S(1)} collective-permute-done((bf16[96,1024]{1,0:T(8,128)(2,1)S(1)}, bf16[96,1024]{1,0:T(8,128)(2,1)S(1)}, u32[]{:S(2)}, u32[]{:S(2)}) %collective-permute-start.1) | collective-permute-done | bytes 196640 | tf_op jit(solution)/shard_map/ppermute | solution.py:412
  53.3 4.5 %project_back.1 = (bf16[512,512]{1,0:T(8,128)(2,1)}, bf16[256,2176]{1,0:T(8,128)(2,1)S(1)}, bf16[256,2176]{1,0:T(8,128)(2,1)}) custom-call(f32[528,1024]{1,0:T(8,128)S(1)} %get-tuple-element.53.fine, f32[496,1024]{1,0:T(8,128)S(1)} %get-tuple-element.54.wide, bf16[96,1024]{1,0:T(8,128)(2,1)S(1)} %collective-permute-done.1.back, ...), custom_call_target="tpu_custom_call" | custom-call | bytes 1048576 | tf_op jit(solution)/shard_map/project_back/pallas_call | solution.py:36
  57.8 1.0 copy-done.12
  58.8 4.2 %collective-permute-start.2 = (bf16[256,2176]{1,0:T(8,128)(2,1)}, bf16[256,2176]{1,0:T(8,128)(2,1)S(1)}, u32[]{:S(2)}, u32[]{:S(2)}) collective-permute-start(bf16[256,2176]{1,0:T(8,128)(2,1)} %get-tuple-element.62), channel_id=1, source_target_pairs={{0,1},{1,0},{2,3},{3,2},{4,5},{5,4},{6,7},{7,6},{8,9},{9,8},{10,11... | collective-permute-start | bytes 3342344 | tf_op jit(solution)/shard_map/ppermute | solution.py:325
  63.0 1.6 add_convert_fusion.2
  64.7 1.6 add_convert_fusion.1
  66.4 2.1 %collective-permute-start.23 = (bf16[512,512]{1,0:T(8,128)(2,1)S(1)}, bf16[512,512]{1,0:T(8,128)(2,1)S(1)}, u32[]{:S(2)}, u32[]{:S(2)}) collective-permute-start(bf16[512,512]{1,0:T(8,128)(2,1)S(1)} %constant_dynamic-slice_fusion.3), channel_id=1, source_target_pairs={{0,2},{1,5},{2,0},{3,7},{4,6},{5,1},{6,4},{7,3},{8,10},{9,13},{10,... | collective-permute-start | bytes 1572872 | tf_op jit(solution)/shard_map/ppermute | solution.py:333
  68.9 4.9 %collective-permute-done.13 = bf16[512,512]{1,0:T(8,128)(2,1)S(1)} collective-permute-done((bf16[512,512]{1,0:T(8,128)(2,1)S(1)}, bf16[512,512]{1,0:T(8,128)(2,1)S(1)}, u32[]{:S(2)}, u32[]{:S(2)}) %collective-permute-start.13) | collective-permute-done | bytes 524320 | tf_op jit(solution)/shard_map/ppermute | solution.py:333
  74.1 1.5 collective-permute-start.14
  75.6 6.7 %collective-permute-done.23 = bf16[512,512]{1,0:T(8,128)(2,1)S(1)} collective-permute-done((bf16[512,512]{1,0:T(8,128)(2,1)S(1)}, bf16[512,512]{1,0:T(8,128)(2,1)S(1)}, u32[]{:S(2)}, u32[]{:S(2)}) %collective-permute-start.23) | collective-permute-done | bytes 524320 | tf_op jit(solution)/shard_map/ppermute | solution.py:333
  82.5 1.5 collective-permute-start.24
  84.1 1.7 %collective-permute-start.15 = (bf16[128,512]{1,0:T(8,128)(2,1)S(1)}, bf16[128,512]{1,0:T(8,128)(2,1)S(1)}, u32[]{:S(2)}, u32[]{:S(2)}) collective-permute-start(bf16[128,512]{1,0:T(8,128)(2,1)S(1)} %constant_dynamic-slice_fusion.5), channel_id=1, source_target_pairs={{0,8},{1,9},{2,10},{3,11},{4,12},{5,13},{6,14},{7,15},{8,0},{9,1},... | collective-permute-start | bytes 393224 | tf_op jit(solution)/shard_map/ppermute | solution.py:333
  85.8 4.3 %collective-permute-done.24 = bf16[256,512]{1,0:T(8,128)(2,1)S(1)} collective-permute-done((bf16[256,512]{1,0:T(8,128)(2,1)S(1)}, bf16[256,512]{1,0:T(8,128)(2,1)S(1)}, u32[]{:S(2)}, u32[]{:S(2)}) %collective-permute-start.24) | collective-permute-done | bytes 262176 | tf_op jit(solution)/shard_map/ppermute | solution.py:333
  90.2 1.6 %collective-permute-start.25 = (bf16[128,512]{1,0:T(8,128)(2,1)S(1)}, bf16[128,512]{1,0:T(8,128)(2,1)S(1)}, u32[]{:S(2)}, u32[]{:S(2)}) collective-permute-start(bf16[128,512]{1,0:T(8,128)(2,1)S(1)} %constant_dynamic-slice_fusion.1), channel_id=1, source_target_pairs={{0,8},{1,9},{2,10},{3,11},{4,12},{5,13},{6,14},{7,15},{8,0},{9,1},... | collective-permute-start | bytes 393224 | tf_op jit(solution)/shard_map/ppermute | solution.py:333
  92.1 1.6 collective-permute-start.4
  93.7 2.6 %collective-permute-start.16 = (bf16[64,512]{1,0:T(8,128)(2,1)S(1)}, bf16[64,512]{1,0:T(8,128)(2,1)S(1)}, u32[]{:S(2)}, u32[]{:S(2)}) collective-permute-start(bf16[64,512]{1,0:T(8,128)(2,1)S(1)} %constant_dynamic-slice_fusion.4), channel_id=1, source_target_pairs={{0,16},{1,17},{2,18},{3,19},{4,20},{5,21},{6,22},{7,23},{8,24},{9,... | collective-permute-start | bytes 196616 | tf_op jit(solution)/shard_map/ppermute | solution.py:333
  96.4 2.2 %collective-permute-start.26 = (bf16[64,512]{1,0:T(8,128)(2,1)S(1)}, bf16[64,512]{1,0:T(8,128)(2,1)S(1)}, u32[]{:S(2)}, u32[]{:S(2)}) collective-permute-start(bf16[64,512]{1,0:T(8,128)(2,1)S(1)} %constant_dynamic-slice_fusion), channel_id=1, source_target_pairs={{0,16},{1,17},{2,18},{3,19},{4,20},{5,21},{6,22},{7,23},{8,24},{9,... | collective-permute-start | bytes 196616 | tf_op jit(solution)/shard_map/ppermute | solution.py:333
  98.6 2.5 %collective-permute-done.16 = bf16[64,512]{1,0:T(8,128)(2,1)S(1)} collective-permute-done((bf16[64,512]{1,0:T(8,128)(2,1)S(1)}, bf16[64,512]{1,0:T(8,128)(2,1)S(1)}, u32[]{:S(2)}, u32[]{:S(2)}) %collective-permute-start.16) | collective-permute-done | bytes 65568 | tf_op jit(solution)/shard_map/ppermute | solution.py:333
  101.2 1.2 collective-permute-start.17
  102.4 1.8 %collective-permute-start.5 = (bf16[32,2176]{1,0:T(8,128)(2,1)S(1)}, bf16[32,2176]{1,0:T(8,128)(2,1)S(1)}, u32[]{:S(2)}, u32[]{:S(2)}) collective-permute-start(bf16[32,2176]{1,0:T(8,128)(2,1)S(1)} %constant_dynamic-slice_fusion.9), channel_id=1, source_target_pairs={{0,8},{1,9},{2,10},{3,11},{4,12},{5,13},{6,14},{7,15},{8,0},{9,1},... | collective-permute-start | bytes 417800 | tf_op jit(solution)/shard_map/ppermute | solution.py:333
  104.7 3.1 %collective-permute-done.17 = bf16[64,512]{1,0:T(8,128)(2,1)S(1)} collective-permute-done((bf16[64,512]{1,0:T(8,128)(2,1)S(1)}, bf16[64,512]{1,0:T(8,128)(2,1)S(1)}, u32[]{:S(2)}, u32[]{:S(2)}) %collective-permute-start.17) | collective-permute-done | bytes 65568 | tf_op jit(solution)/shard_map/ppermute | solution.py:343
  107.9 3.0 %collective-permute-done.5 = bf16[32,2176]{1,0:T(8,128)(2,1)S(1)} collective-permute-done((bf16[32,2176]{1,0:T(8,128)(2,1)S(1)}, bf16[32,2176]{1,0:T(8,128)(2,1)S(1)}, u32[]{:S(2)}, u32[]{:S(2)}) %collective-permute-start.5) | collective-permute-done | bytes 139296 | tf_op jit(solution)/shard_map/ppermute | solution.py:333
  111.0 0.9 collective-permute-start.28
  112.0 4.3 %collective-permute-done.6 = bf16[16,2176]{1,0:T(8,128)(2,1)S(1)} collective-permute-done((bf16[16,2176]{1,0:T(8,128)(2,1)S(1)}, bf16[16,2176]{1,0:T(8,128)(2,1)S(1)}, u32[]{:S(2)}, u32[]{:S(2)}) %collective-permute-start.6) | collective-permute-done | bytes 69664 | tf_op jit(solution)/shard_map/ppermute | solution.py:333
  116.4 1.3 collective-permute-start.19
  117.8 3.8 %collective-permute-done.7 = bf16[16,2176]{1,0:T(8,128)(2,1)S(1)} collective-permute-done((bf16[16,2176]{1,0:T(8,128)(2,1)S(1)}, bf16[16,2176]{1,0:T(8,128)(2,1)S(1)}, u32[]{:S(2)}, u32[]{:S(2)}) %collective-permute-start.7) | collective-permute-done | bytes 69664 | tf_op jit(solution)/shard_map/ppermute | solution.py:343
  121.7 4.1 %collective-permute-done.19 = bf16[256,512]{1,0:T(8,128)(2,1)S(1)} collective-permute-done((bf16[256,512]{1,0:T(8,128)(2,1)S(1)}, bf16[256,512]{1,0:T(8,128)(2,1)S(1)}, u32[]{:S(2)}, u32[]{:S(2)}) %collective-permute-start.19) | collective-permute-done | bytes 262176 | tf_op jit(solution)/shard_map/ppermute | solution.py:343
  126.3 1.2 collective-permute-start.29
  127.5 1.0 collective-permute-start.9
  128.5 6.4 %collective-permute-done.29 = bf16[256,512]{1,0:T(8,128)(2,1)S(1)} collective-permute-done((bf16[256,512]{1,0:T(8,128)(2,1)S(1)}, bf16[256,512]{1,0:T(8,128)(2,1)S(1)}, u32[]{:S(2)}, u32[]{:S(2)}) %collective-permute-start.29) | collective-permute-done | bytes 262176 | tf_op jit(solution)/shard_map/ppermute | solution.py:343
  135.0 1.8 %collective-permute-start.30 = (bf16[512,512]{1,0:T(8,128)(2,1)S(1)}, bf16[512,512]{1,0:T(8,128)(2,1)}, u32[]{:S(2)}, u32[]{:S(2)}) collective-permute-start(bf16[512,512]{1,0:T(8,128)(2,1)S(1)} %maximum_select_fusion.8), channel_id=1, source_target_pairs={{0,2},{1,5},{2,0},{3,7},{4,6},{5,1},{6,4},{7,3},{8,10},{9,13},{10,... | collective-permute-start | bytes 1572872 | tf_op jit(solution)/shard_map/ppermute | solution.py:343
  137.9 1.2 maximum_select_fusion.6
  139.1 1.8 %collective-permute-start.10 = (bf16[128,2176]{1,0:T(8,128)(2,1)S(1)}, bf16[128,2176]{1,0:T(8,128)(2,1)}, u32[]{:S(2)}, u32[]{:S(2)}) collective-permute-start(bf16[128,2176]{1,0:T(8,128)(2,1)S(1)} %maximum_select_fusion.6), channel_id=1, source_target_pairs={{0,2},{1,5},{2,0},{3,7},{4,6},{5,1},{6,4},{7,3},{8,10},{9,13},{10,... | collective-permute-start | bytes 1671176 | tf_op jit(solution)/shard_map/ppermute | solution.py:343
  140.9 3.5 %collective-permute-done.30 = bf16[512,512]{1,0:T(8,128)(2,1)} collective-permute-done((bf16[512,512]{1,0:T(8,128)(2,1)S(1)}, bf16[512,512]{1,0:T(8,128)(2,1)}, u32[]{:S(2)}, u32[]{:S(2)}) %collective-permute-start.30) | collective-permute-done | bytes 524320 | tf_op jit(solution)/shard_map/ppermute | solution.py:343
  144.4 1.7 %maximum_select_fusion.5 = bf16[1024,512]{1,0:T(8,128)(2,1)S(1)} fusion(bf16[512,512]{1,0:T(8,128)(2,1)} %collective-permute-done.30, bf16[512,512]{1,0:T(8,128)(2,1)S(1)} %maximum_select_fusion.8, pred[]{:T(512)S(6)} %eq.11), kind=kLoop, calls=%fused_computation.12 | loop fusion | flops 4718592 | bytes 2097153 | tf_op jit(solution)/shard_map/jit(_where)/select_n | solution.py:344
  146.1 4.2 %collective-permute-done.10 = bf16[128,2176]{1,0:T(8,128)(2,1)} collective-permute-done((bf16[128,2176]{1,0:T(8,128)(2,1)S(1)}, bf16[128,2176]{1,0:T(8,128)(2,1)}, u32[]{:S(2)}, u32[]{:S(2)}) %collective-permute-start.10) | collective-permute-done | bytes 557088 | tf_op jit(solution)/shard_map/ppermute | solution.py:343
  150.4 1.5 maximum_select_fusion.3
  152.7 2.6 %maximum_convert_fusion = f32[512,2048]{1,0:T(8,128)} fusion(bf16[512,512]{1,0:T(8,128)(2,1)S(1)} %get-tuple-element.73, bf16[512,512]{1,0:T(8,128)(2,1)S(1)} %get-tuple-element.74, bf16[512,512]{1,0:T(8,128)(2,1)S(1)} %get-tuple-element.75, bf16[512,512]{1,0:T(8,128)(2,1)S(1)} %get-tuple-element.72), kind=kLoop, calls=%fused_computation.3 | loop fusion | flops 8388608 | bytes 6291456 | tf_op jit(solution)/shard_map/convert_element_type | solution.py:438
  155.2 2.7 %fusion = f32[2048,512]{1,0:T(8,128)} fusion(bf16[1024,512]{1,0:T(8,128)(2,1)S(1)} %collective-permute-done.31, bf16[1024,512]{1,0:T(8,128)(2,1)S(1)} %maximum_select_fusion.5, pred[]{:T(512)S(6)} %eq.10), kind=kLoop, calls=%fused_computation.5 | loop fusion | flops 10485760 | bytes 6291457 | tf_op jit(solution)/shard_map/convert_element_type | solution.py:439
  157.9 0.9 maximum_select_fusion
  158.8 2.1 %slice_convert_fusion = f32[512,1536]{1,0:T(8,128)} fusion(bf16[512,2176]{1,0:T(8,128)(2,1)S(1)} %maximum_select_fusion), kind=kLoop, calls=%fused_computation.8 | loop fusion | flops 786432 | bytes 4718592 | tf_op jit(solution)/shard_map/convert_element_type | solution.py:434
  160.9 1.1 slice_convert_fusion.1
  162.0 1.2 slice_reduce_fusion
  (107 shorter events, 5.4 us)
Async XLA Ops:
  0.6 9.4 %copy-start.21 = (bf16[512]{0:T(512)(128)(2,1)S(1)}, bf16[512]{0:T(512)(128)(2,1)}, u32[]{:S(2)}) copy-start(bf16[512]{0:T(512)(128)(2,1)} %param.18) | copy-start | bytes 3076
  0.7 9.4 %copy-start.22 = (bf16[512]{0:T(512)(128)(2,1)S(1)}, bf16[512]{0:T(512)(128)(2,1)}, u32[]{:S(2)}) copy-start(bf16[512]{0:T(512)(128)(2,1)} %param.19) | copy-start | bytes 3076
  2.0 1.4 copy-start
  3.4 1.0 copy-start.5
  4.5 5.7 %copy-start.1 = (bf16[512,1536]{1,0:T(8,128)(2,1)S(1)}, bf16[512,1536]{1,0:T(8,128)(2,1)}, u32[]{:S(2)}) copy-start(bf16[512,1536]{1,0:T(8,128)(2,1)} %w_qkv.5) | copy-start | bytes 4718596
  6.0 1.0 copy-start.8
  7.0 9.9 %collective-permute-start = (bf16[96,1024]{1,0:T(8,128)(2,1)S(1)}, bf16[96,1024]{1,0:T(8,128)(2,1)S(1)}, u32[]{:S(2)}, u32[]{:S(2)}) collective-permute-start(bf16[96,1024]{1,0:T(8,128)(2,1)S(1)} %get-tuple-element.43), channel_id=1, source_target_pairs={{0,1},{1,2},{2,3},{4,5},{5,6},{6,7},{8,9},{9,10},{10,11},{12,13},{... | collective-permute-start | bytes 589832 | tf_op jit(solution)/shard_map/ppermute | solution.py:374
  10.1 1.6 copy-start.2
  11.7 1.0 copy-start.20
  12.8 4.2 %copy-start.9 = (bf16[496,1024]{1,0:T(8,128)(2,1)S(1)}, bf16[496,1024]{1,0:T(8,128)(2,1)}, u32[]{:S(2)}) copy-start(bf16[496,1024]{1,0:T(8,128)(2,1)} %copy-done.8) | copy-start | bytes 3047428
  12.8 10.9 %copy-start.10 = (bf16[512,512]{1,0:T(8,128)(2,1)S(1)}, bf16[512,512]{1,0:T(8,128)(2,1)}, u32[]{:S(2)}) copy-start(bf16[512,512]{1,0:T(8,128)(2,1)} %w_out.3) | copy-start | bytes 1572868
  14.9 2.0 %copy-start.7 = (f32[512,2048]{1,0:T(8,128)}, f32[512,2048]{1,0:T(8,128)S(1)}, u32[]{:S(2)}) copy-start(f32[512,2048]{1,0:T(8,128)S(1)} %get-tuple-element.45.d_hidden) | copy-start | bytes 12582916
  16.9 6.8 %copy-start.4 = (bf16[512,2048]{1,0:T(8,128)(2,1)S(1)}, bf16[512,2048]{1,0:T(8,128)(2,1)}, u32[]{:S(2)}) copy-start(bf16[512,2048]{1,0:T(8,128)(2,1)} %w_up.3) | copy-start | bytes 6291460
  16.9 6.8 %copy-start.6 = (bf16[1,512,512]{2,1,0:T(8,128)(2,1)S(1)}, bf16[1,512,512]{2,1,0:T(8,128)(2,1)}, u32[]{:S(2)}) copy-start(bf16[1,512,512]{2,1,0:T(8,128)(2,1)} %param.11) | copy-start | bytes 1572868
  31.8 1.0 copy-start.14
  32.8 6.6 %copy-start.3 = (bf16[2048,512]{1,0:T(8,128)(2,1)S(1)}, bf16[2048,512]{1,0:T(8,128)(2,1)}, u32[]{:S(2)}) copy-start(bf16[2048,512]{1,0:T(8,128)(2,1)} %w_down.3) | copy-start | bytes 6291460
  32.8 6.6 %copy-start.11 = (bf16[512,512]{1,0:T(8,128)(2,1)S(1)}, bf16[512,512]{1,0:T(8,128)(2,1)}, u32[]{:S(2)}) copy-start(bf16[512,512]{1,0:T(8,128)(2,1)} %w_out.3) | copy-start | bytes 1572868
  35.7 1.0 copy-start.16
  36.7 26.3 %collective-permute-start.12 = (bf16[1024,512]{1,0:T(8,128)(2,1)}, bf16[1024,512]{1,0:T(8,128)(2,1)}, u32[]{:S(2)}, u32[]{:S(2)}) collective-permute-start(bf16[1024,512]{1,0:T(8,128)(2,1)} %get-tuple-element.65), channel_id=1, source_target_pairs={{0,1},{1,0},{2,3},{3,2},{4,5},{5,4},{6,7},{7,6},{8,9},{9,8},{10,11... | collective-permute-start | bytes 3145736 | tf_op jit(solution)/shard_map/ppermute | solution.py:325
  39.3 25.4 %collective-permute-start.22 = (bf16[1024,512]{1,0:T(8,128)(2,1)}, bf16[1024,512]{1,0:T(8,128)(2,1)}, u32[]{:S(2)}, u32[]{:S(2)}) collective-permute-start(bf16[1024,512]{1,0:T(8,128)(2,1)} %get-tuple-element.67), channel_id=1, source_target_pairs={{0,1},{1,0},{2,3},{3,2},{4,5},{5,4},{6,7},{7,6},{8,9},{9,8},{10,11... | collective-permute-start | bytes 3145736 | tf_op jit(solution)/shard_map/ppermute | solution.py:325
  43.0 1.0 copy-start.18
  44.0 9.3 %copy-start.19 = (f32[512,512]{1,0:T(8,128)S(1)}, f32[512,512]{1,0:T(8,128)}, u32[]{:S(2)}) copy-start(f32[512,512]{1,0:T(8,128)} %copy-done.18) | copy-start | bytes 3145732
  49.9 3.3 %collective-permute-start.1 = (bf16[96,1024]{1,0:T(8,128)(2,1)S(1)}, bf16[96,1024]{1,0:T(8,128)(2,1)S(1)}, u32[]{:S(2)}, u32[]{:S(2)}) collective-permute-start(bf16[96,1024]{1,0:T(8,128)(2,1)S(1)} %get-tuple-element.55), channel_id=1, source_target_pairs={{1,0},{2,1},{3,2},{5,4},{6,5},{7,6},{9,8},{10,9},{11,10},{13,12},{... | collective-permute-start | bytes 589832 | tf_op jit(solution)/shard_map/ppermute | solution.py:412
  53.3 9.7 %copy-start.17 = (bf16[1024,512]{1,0:T(8,128)(2,1)S(1)}, bf16[1024,512]{1,0:T(8,128)(2,1)}, u32[]{:S(2)}) copy-start(bf16[1024,512]{1,0:T(8,128)(2,1)} %copy-done.16) | copy-start | bytes 3145732
  57.8 1.0 copy-start.12
  58.8 9.7 %collective-permute-start.2 = (bf16[256,2176]{1,0:T(8,128)(2,1)}, bf16[256,2176]{1,0:T(8,128)(2,1)S(1)}, u32[]{:S(2)}, u32[]{:S(2)}) collective-permute-start(bf16[256,2176]{1,0:T(8,128)(2,1)} %get-tuple-element.62), channel_id=1, source_target_pairs={{0,1},{1,0},{2,3},{3,2},{4,5},{5,4},{6,7},{7,6},{8,9},{9,8},{10,11... | collective-permute-start | bytes 3342344 | tf_op jit(solution)/shard_map/ppermute | solution.py:325
  63.0 1.7 %copy-start.15 = (bf16[1024,512]{1,0:T(8,128)(2,1)S(1)}, bf16[1024,512]{1,0:T(8,128)(2,1)}, u32[]{:S(2)}) copy-start(bf16[1024,512]{1,0:T(8,128)(2,1)} %copy-done.14) | copy-start | bytes 3145732
  64.6 9.2 %collective-permute-start.13 = (bf16[512,512]{1,0:T(8,128)(2,1)S(1)}, bf16[512,512]{1,0:T(8,128)(2,1)S(1)}, u32[]{:S(2)}, u32[]{:S(2)}) collective-permute-start(bf16[512,512]{1,0:T(8,128)(2,1)S(1)} %constant_dynamic-slice_fusion.7), channel_id=1, source_target_pairs={{0,2},{1,5},{2,0},{3,7},{4,6},{5,1},{6,4},{7,3},{8,10},{9,13},{10,... | collective-permute-start | bytes 1572872 | tf_op jit(solution)/shard_map/ppermute | solution.py:333
  64.7 3.7 %copy-start.13 = (bf16[256,2176]{1,0:T(8,128)(2,1)S(1)}, bf16[256,2176]{1,0:T(8,128)(2,1)}, u32[]{:S(2)}) copy-start(bf16[256,2176]{1,0:T(8,128)(2,1)} %copy-done.12) | copy-start | bytes 3342340
  66.4 15.9 %collective-permute-start.23 = (bf16[512,512]{1,0:T(8,128)(2,1)S(1)}, bf16[512,512]{1,0:T(8,128)(2,1)S(1)}, u32[]{:S(2)}, u32[]{:S(2)}) collective-permute-start(bf16[512,512]{1,0:T(8,128)(2,1)S(1)} %constant_dynamic-slice_fusion.3), channel_id=1, source_target_pairs={{0,2},{1,5},{2,0},{3,7},{4,6},{5,1},{6,4},{7,3},{8,10},{9,13},{10,... | collective-permute-start | bytes 1572872 | tf_op jit(solution)/shard_map/ppermute | solution.py:333
  68.8 23.0 %collective-permute-start.3 = (bf16[128,2176]{1,0:T(8,128)(2,1)S(1)}, bf16[128,2176]{1,0:T(8,128)(2,1)S(1)}, u32[]{:S(2)}, u32[]{:S(2)}) collective-permute-start(bf16[128,2176]{1,0:T(8,128)(2,1)S(1)} %constant_dynamic-slice_fusion.11), channel_id=1, source_target_pairs={{0,2},{1,5},{2,0},{3,7},{4,6},{5,1},{6,4},{7,3},{8,10},{9,13},{10,... | collective-permute-start | bytes 1671176 | tf_op jit(solution)/shard_map/ppermute | solution.py:333
  74.1 10.0 %collective-permute-start.14 = (bf16[256,512]{1,0:T(8,128)(2,1)S(1)}, bf16[256,512]{1,0:T(8,128)(2,1)S(1)}, u32[]{:S(2)}, u32[]{:S(2)}) collective-permute-start(bf16[256,512]{1,0:T(8,128)(2,1)S(1)} %constant_dynamic-slice_fusion.6), channel_id=1, source_target_pairs={{0,4},{1,3},{2,6},{3,1},{4,0},{5,7},{6,2},{7,5},{8,12},{9,11},{10,... | collective-permute-start | bytes 786440 | tf_op jit(solution)/shard_map/ppermute | solution.py:333
  82.5 7.6 %collective-permute-start.24 = (bf16[256,512]{1,0:T(8,128)(2,1)S(1)}, bf16[256,512]{1,0:T(8,128)(2,1)S(1)}, u32[]{:S(2)}, u32[]{:S(2)}) collective-permute-start(bf16[256,512]{1,0:T(8,128)(2,1)S(1)} %constant_dynamic-slice_fusion.2), channel_id=1, source_target_pairs={{0,4},{1,3},{2,6},{3,1},{4,0},{5,7},{6,2},{7,5},{8,12},{9,11},{10,... | collective-permute-start | bytes 786440 | tf_op jit(solution)/shard_map/ppermute | solution.py:333
  84.1 9.5 %collective-permute-start.15 = (bf16[128,512]{1,0:T(8,128)(2,1)S(1)}, bf16[128,512]{1,0:T(8,128)(2,1)S(1)}, u32[]{:S(2)}, u32[]{:S(2)}) collective-permute-start(bf16[128,512]{1,0:T(8,128)(2,1)S(1)} %constant_dynamic-slice_fusion.5), channel_id=1, source_target_pairs={{0,8},{1,9},{2,10},{3,11},{4,12},{5,13},{6,14},{7,15},{8,0},{9,1},... | collective-permute-start | bytes 393224 | tf_op jit(solution)/shard_map/ppermute | solution.py:333
  90.2 6.1 %collective-permute-start.25 = (bf16[128,512]{1,0:T(8,128)(2,1)S(1)}, bf16[128,512]{1,0:T(8,128)(2,1)S(1)}, u32[]{:S(2)}, u32[]{:S(2)}) collective-permute-start(bf16[128,512]{1,0:T(8,128)(2,1)S(1)} %constant_dynamic-slice_fusion.1), channel_id=1, source_target_pairs={{0,8},{1,9},{2,10},{3,11},{4,12},{5,13},{6,14},{7,15},{8,0},{9,1},... | collective-permute-start | bytes 393224 | tf_op jit(solution)/shard_map/ppermute | solution.py:333
  92.1 10.3 %collective-permute-start.4 = (bf16[64,2176]{1,0:T(8,128)(2,1)S(1)}, bf16[64,2176]{1,0:T(8,128)(2,1)S(1)}, u32[]{:S(2)}, u32[]{:S(2)}) collective-permute-start(bf16[64,2176]{1,0:T(8,128)(2,1)S(1)} %constant_dynamic-slice_fusion.10), channel_id=1, source_target_pairs={{0,4},{1,3},{2,6},{3,1},{4,0},{5,7},{6,2},{7,5},{8,12},{9,11},{10,... | collective-permute-start | bytes 835592 | tf_op jit(solution)/shard_map/ppermute | solution.py:333
  93.7 7.4 %collective-permute-start.16 = (bf16[64,512]{1,0:T(8,128)(2,1)S(1)}, bf16[64,512]{1,0:T(8,128)(2,1)S(1)}, u32[]{:S(2)}, u32[]{:S(2)}) collective-permute-start(bf16[64,512]{1,0:T(8,128)(2,1)S(1)} %constant_dynamic-slice_fusion.4), channel_id=1, source_target_pairs={{0,16},{1,17},{2,18},{3,19},{4,20},{5,21},{6,22},{7,23},{8,24},{9,... | collective-permute-start | bytes 196616 | tf_op jit(solution)/shard_map/ppermute | solution.py:333
  96.4 7.9 %collective-permute-start.26 = (bf16[64,512]{1,0:T(8,128)(2,1)S(1)}, bf16[64,512]{1,0:T(8,128)(2,1)S(1)}, u32[]{:S(2)}, u32[]{:S(2)}) collective-permute-start(bf16[64,512]{1,0:T(8,128)(2,1)S(1)} %constant_dynamic-slice_fusion), channel_id=1, source_target_pairs={{0,16},{1,17},{2,18},{3,19},{4,20},{5,21},{6,22},{7,23},{8,24},{9,... | collective-permute-start | bytes 196616 | tf_op jit(solution)/shard_map/ppermute | solution.py:333
  101.2 6.6 %collective-permute-start.17 = (bf16[64,512]{1,0:T(8,128)(2,1)S(1)}, bf16[64,512]{1,0:T(8,128)(2,1)S(1)}, u32[]{:S(2)}, u32[]{:S(2)}) collective-permute-start(bf16[64,512]{1,0:T(8,128)(2,1)S(1)} %add_convert_fusion.14), channel_id=1, source_target_pairs={{0,16},{1,17},{2,18},{3,19},{4,20},{5,21},{6,22},{7,23},{8,24},{9,... | collective-permute-start | bytes 196616 | tf_op jit(solution)/shard_map/ppermute | solution.py:343
  102.4 8.4 %collective-permute-start.5 = (bf16[32,2176]{1,0:T(8,128)(2,1)S(1)}, bf16[32,2176]{1,0:T(8,128)(2,1)S(1)}, u32[]{:S(2)}, u32[]{:S(2)}) collective-permute-start(bf16[32,2176]{1,0:T(8,128)(2,1)S(1)} %constant_dynamic-slice_fusion.9), channel_id=1, source_target_pairs={{0,8},{1,9},{2,10},{3,11},{4,12},{5,13},{6,14},{7,15},{8,0},{9,1},... | collective-permute-start | bytes 417800 | tf_op jit(solution)/shard_map/ppermute | solution.py:333
  104.3 6.7 %collective-permute-start.27 = (bf16[64,512]{1,0:T(8,128)(2,1)S(1)}, bf16[64,512]{1,0:T(8,128)(2,1)S(1)}, u32[]{:S(2)}, u32[]{:S(2)}) collective-permute-start(bf16[64,512]{1,0:T(8,128)(2,1)S(1)} %add_convert_fusion.13), channel_id=1, source_target_pairs={{0,16},{1,17},{2,18},{3,19},{4,20},{5,21},{6,22},{7,23},{8,24},{9,... | collective-permute-start | bytes 196616 | tf_op jit(solution)/shard_map/ppermute | solution.py:343
  107.8 8.6 %collective-permute-start.18 = (bf16[128,512]{1,0:T(8,128)(2,1)S(1)}, bf16[128,512]{1,0:T(8,128)(2,1)S(1)}, u32[]{:S(2)}, u32[]{:S(2)}) collective-permute-start(bf16[128,512]{1,0:T(8,128)(2,1)S(1)} %maximum_select_fusion.13), channel_id=1, source_target_pairs={{0,8},{1,9},{2,10},{3,11},{4,12},{5,13},{6,14},{7,15},{8,0},{9,1},... | collective-permute-start | bytes 393224 | tf_op jit(solution)/shard_map/ppermute | solution.py:343
  110.9 5.4 %collective-permute-start.6 = (bf16[16,2176]{1,0:T(8,128)(2,1)S(1)}, bf16[16,2176]{1,0:T(8,128)(2,1)S(1)}, u32[]{:S(2)}, u32[]{:S(2)}) collective-permute-start(bf16[16,2176]{1,0:T(8,128)(2,1)S(1)} %constant_dynamic-slice_fusion.8), channel_id=1, source_target_pairs={{0,16},{1,17},{2,18},{3,19},{4,20},{5,21},{6,22},{7,23},{8,24},{9,... | collective-permute-start | bytes 208904 | tf_op jit(solution)/shard_map/ppermute | solution.py:333
  111.0 15.2 %collective-permute-start.28 = (bf16[128,512]{1,0:T(8,128)(2,1)S(1)}, bf16[128,512]{1,0:T(8,128)(2,1)S(1)}, u32[]{:S(2)}, u32[]{:S(2)}) collective-permute-start(bf16[128,512]{1,0:T(8,128)(2,1)S(1)} %maximum_select_fusion.14), channel_id=1, source_target_pairs={{0,8},{1,9},{2,10},{3,11},{4,12},{5,13},{6,14},{7,15},{8,0},{9,1},... | collective-permute-start | bytes 393224 | tf_op jit(solution)/shard_map/ppermute | solution.py:343
  116.3 5.3 %collective-permute-start.7 = (bf16[16,2176]{1,0:T(8,128)(2,1)S(1)}, bf16[16,2176]{1,0:T(8,128)(2,1)S(1)}, u32[]{:S(2)}, u32[]{:S(2)}) collective-permute-start(bf16[16,2176]{1,0:T(8,128)(2,1)S(1)} %add_convert_fusion.12), channel_id=1, source_target_pairs={{0,16},{1,17},{2,18},{3,19},{4,20},{5,21},{6,22},{7,23},{8,24},{9,... | collective-permute-start | bytes 208904 | tf_op jit(solution)/shard_map/ppermute | solution.py:343
  116.4 9.3 %collective-permute-start.19 = (bf16[256,512]{1,0:T(8,128)(2,1)S(1)}, bf16[256,512]{1,0:T(8,128)(2,1)S(1)}, u32[]{:S(2)}, u32[]{:S(2)}) collective-permute-start(bf16[256,512]{1,0:T(8,128)(2,1)S(1)} %maximum_select_fusion.10), channel_id=1, source_target_pairs={{0,4},{1,3},{2,6},{3,1},{4,0},{5,7},{6,2},{7,5},{8,12},{9,11},{10,... | collective-permute-start | bytes 786440 | tf_op jit(solution)/shard_map/ppermute | solution.py:343
  121.6 5.9 %collective-permute-start.8 = (bf16[32,2176]{1,0:T(8,128)(2,1)S(1)}, bf16[32,2176]{1,0:T(8,128)(2,1)S(1)}, u32[]{:S(2)}, u32[]{:S(2)}) collective-permute-start(bf16[32,2176]{1,0:T(8,128)(2,1)S(1)} %maximum_select_fusion.12), channel_id=1, source_target_pairs={{0,8},{1,9},{2,10},{3,11},{4,12},{5,13},{6,14},{7,15},{8,0},{9,1},... | collective-permute-start | bytes 417800 | tf_op jit(solution)/shard_map/ppermute | solution.py:343
  126.0 10.9 %collective-permute-start.20 = (bf16[512,512]{1,0:T(8,128)(2,1)S(1)}, bf16[512,512]{1,0:T(8,128)(2,1)S(1)}, u32[]{:S(2)}, u32[]{:S(2)}) collective-permute-start(bf16[512,512]{1,0:T(8,128)(2,1)S(1)} %maximum_select_fusion.7), channel_id=1, source_target_pairs={{0,2},{1,5},{2,0},{3,7},{4,6},{5,1},{6,4},{7,3},{8,10},{9,13},{10,... | collective-permute-start | bytes 1572872 | tf_op jit(solution)/shard_map/ppermute | solution.py:343
  126.3 8.6 %collective-permute-start.29 = (bf16[256,512]{1,0:T(8,128)(2,1)S(1)}, bf16[256,512]{1,0:T(8,128)(2,1)S(1)}, u32[]{:S(2)}, u32[]{:S(2)}) collective-permute-start(bf16[256,512]{1,0:T(8,128)(2,1)S(1)} %maximum_select_fusion.11), channel_id=1, source_target_pairs={{0,4},{1,3},{2,6},{3,1},{4,0},{5,7},{6,2},{7,5},{8,12},{9,11},{10,... | collective-permute-start | bytes 786440 | tf_op jit(solution)/shard_map/ppermute | solution.py:343
  127.5 10.4 %collective-permute-start.9 = (bf16[64,2176]{1,0:T(8,128)(2,1)S(1)}, bf16[64,2176]{1,0:T(8,128)(2,1)}, u32[]{:S(2)}, u32[]{:S(2)}) collective-permute-start(bf16[64,2176]{1,0:T(8,128)(2,1)S(1)} %maximum_select_fusion.9), channel_id=1, source_target_pairs={{0,4},{1,3},{2,6},{3,1},{4,0},{5,7},{6,2},{7,5},{8,12},{9,11},{10,... | collective-permute-start | bytes 835592 | tf_op jit(solution)/shard_map/ppermute | solution.py:343
  135.0 9.4 %collective-permute-start.30 = (bf16[512,512]{1,0:T(8,128)(2,1)S(1)}, bf16[512,512]{1,0:T(8,128)(2,1)}, u32[]{:S(2)}, u32[]{:S(2)}) collective-permute-start(bf16[512,512]{1,0:T(8,128)(2,1)S(1)} %maximum_select_fusion.8), channel_id=1, source_target_pairs={{0,2},{1,5},{2,0},{3,7},{4,6},{5,1},{6,4},{7,3},{8,10},{9,13},{10,... | collective-permute-start | bytes 1572872 | tf_op jit(solution)/shard_map/ppermute | solution.py:343
  137.3 14.6 %collective-permute-start.21 = (bf16[1024,512]{1,0:T(8,128)(2,1)S(1)}, bf16[1024,512]{1,0:T(8,128)(2,1)S(1)}, u32[]{:S(2)}, u32[]{:S(2)}) collective-permute-start(bf16[1024,512]{1,0:T(8,128)(2,1)S(1)} %maximum_select_fusion.4), channel_id=1, source_target_pairs={{0,1},{1,0},{2,3},{3,2},{4,5},{5,4},{6,7},{7,6},{8,9},{9,8},{10,11... | collective-permute-start | bytes 3145736 | tf_op jit(solution)/shard_map/ppermute | solution.py:343
  139.1 11.3 %collective-permute-start.10 = (bf16[128,2176]{1,0:T(8,128)(2,1)S(1)}, bf16[128,2176]{1,0:T(8,128)(2,1)}, u32[]{:S(2)}, u32[]{:S(2)}) collective-permute-start(bf16[128,2176]{1,0:T(8,128)(2,1)S(1)} %maximum_select_fusion.6), channel_id=1, source_target_pairs={{0,2},{1,5},{2,0},{3,7},{4,6},{5,1},{6,4},{7,3},{8,10},{9,13},{10,... | collective-permute-start | bytes 1671176 | tf_op jit(solution)/shard_map/ppermute | solution.py:343
  146.1 9.2 %collective-permute-start.31 = (bf16[1024,512]{1,0:T(8,128)(2,1)S(1)}, bf16[1024,512]{1,0:T(8,128)(2,1)S(1)}, u32[]{:S(2)}, u32[]{:S(2)}) collective-permute-start(bf16[1024,512]{1,0:T(8,128)(2,1)S(1)} %maximum_select_fusion.5), channel_id=1, source_target_pairs={{0,1},{1,0},{2,3},{3,2},{4,5},{5,4},{6,7},{7,6},{8,9},{9,8},{10,11... | collective-permute-start | bytes 3145736 | tf_op jit(solution)/shard_map/ppermute | solution.py:343
  151.8 6.1 %collective-permute-start.11 = (bf16[256,2176]{1,0:T(8,128)(2,1)S(1)}, bf16[256,2176]{1,0:T(8,128)(2,1)S(1)}, u32[]{:S(2)}, u32[]{:S(2)}) collective-permute-start(bf16[256,2176]{1,0:T(8,128)(2,1)S(1)} %maximum_select_fusion.3), channel_id=1, source_target_pairs={{0,1},{1,0},{2,3},{3,2},{4,5},{5,4},{6,7},{7,6},{8,9},{9,8},{10,11... | collective-permute-start | bytes 3342344 | tf_op jit(solution)/shard_map/ppermute | solution.py:343

commit v2 on v1

v2 whole, which is shorter than its diff:
```python
from functools import partial
import math

import jax
import jax.numpy as jnp
from jax import lax
from jax.experimental import pallas as pl
from jax.experimental.pallas import tpu as pltpu
from jax.sharding import PartitionSpec as P

HEADS = 8
BLOCK = 16
LEVELS = 6
CHUNK = 32
KEYS = 128
f32 = jnp.float32
bf16 = jnp.bfloat16


def nn(a, b):
    return lax.dot_general(a, b, (((1,), (0,)), ((), ())), preferred_element_type=f32)


def nt(a, b):
    return lax.dot_general(a, b, (((1,), (1,)), ((), ())), preferred_element_type=f32)


def tn(a, b):
    return lax.dot_general(a, b, (((0,), (0,)), ((), ())), preferred_element_type=f32)


def call(kernel, outs, *args, scratch=(), smem=(), far=(), far_out=(), deps=(), name=None, us=0.5, limit=8):
    def spec(at, apart):
        return pl.BlockSpec(memory_space=pltpu.HBM if at in apart else pltpu.VMEM)

    specs = [
        pl.BlockSpec(memory_space=pltpu.SMEM) if i in smem else spec(i, far) for i in range(len(args))
    ]
    specs += [pl.BlockSpec(memory_space=pl.ANY)] * len(deps)
    count = len(args)

    def run(*refs):
        kernel(*refs[:count], *refs[count + len(deps) :])

    return pl.pallas_call(
        run,
        out_shape=[jax.ShapeDtypeStruct(s, d) for s, d in outs],
        in_specs=specs,
        out_specs=[spec(i, far_out) for i in range(len(outs))],
        scratch_shapes=scratch,
        compiler_params=pltpu.CompilerParams(vmem_limit_bytes=limit * 2**20),
        cost_estimate=pl.CostEstimate(
            flops=int(us * 1.15e9), bytes_accessed=2**16, transcendentals=0
        ),
        name=name,
    )(*args, *deps)


def level_start(span, level):
    return span - (span >> (level - 1)) if level else 0


def unit(values):
    centred = values - jnp.mean(values, axis=-1, keepdims=True)
    inv = lax.rsqrt(jnp.mean(centred * centred, axis=-1, keepdims=True) + 1e-05)
    return centred * inv, inv


def unit_back(grad, hat, inv):
    along = jnp.mean(grad * hat, axis=-1, keepdims=True)
    return inv * (grad - jnp.mean(grad, axis=-1, keepdims=True) - hat * along)


def pool_matrix(span):
    parts = []
    for level in range(1, LEVELS):
        rows = span >> level
        row = lax.broadcasted_iota(jnp.int32, (rows, span), 0)
        col = lax.broadcasted_iota(jnp.int32, (rows, span), 1)
        parts.append(jnp.where((col >> level) == row, 1.0 / 2**level, 0.0))
    return jnp.concatenate(parts, axis=0).astype(bf16)


def edge_matrix(span):
    parts = []
    row = lax.broadcasted_iota(jnp.int32, (BLOCK, span), 0)
    col = lax.broadcasted_iota(jnp.int32, (BLOCK, span), 1)
    for level in range(LEVELS):
        group = (span >> level) - BLOCK + row
        parts.append(jnp.where((col >> level) == group, 1.0 / 2**level, 0.0))
    return jnp.concatenate(parts, axis=0).astype(bf16)


def standardize(tokens, hat):
    hat[...] = unit(tokens[...].astype(f32))[0]


def project(hat, gain, bias, w_qkv, normed, queries, kv, coarse, edge):
    span, width = hat.shape
    rows = (hat[...] * gain[...].astype(f32)[None] + bias[...].astype(f32)[None]).astype(bf16)
    normed[...] = rows
    both = nn(rows, w_qkv[:, width:]).astype(bf16)
    kv[...] = both
    pooled = nn(pool_matrix(span), both).astype(bf16)
    coarse[...] = pooled
    edge[0:BLOCK, : 2 * width] = both[span - BLOCK :]
    for level in range(1, LEVELS):
        end = level_start(span, level + 1)
        edge[BLOCK * level : BLOCK * (level + 1), : 2 * width] = pooled[end - BLOCK : end]
    edge[:, 2 * width :] = nn(edge_matrix(span), hat[...].astype(bf16)).astype(bf16)
    q = nn(rows, w_qkv[:, :width]).astype(bf16).astype(f32)
    queries[...] = (q * (1.0 / math.sqrt(width // HEADS))).astype(bf16)


def hidden_back(prefix, cotangent, w_down, d_ffn, d_hidden):
    span, width = cotangent.shape
    position = lax.axis_index("seq") * span + lax.broadcasted_iota(jnp.int32, (span, width), 0)
    masked = jnp.where(position >= prefix[0], cotangent[...].astype(f32), 0.0).astype(bf16)
    d_ffn[...] = masked
    d_hidden[...] = nt(masked, w_down[...])


def window_bias(chunk, first):
    row = lax.broadcasted_iota(jnp.int32, (CHUNK, KEYS), 0)
    col = lax.broadcasted_iota(jnp.int32, (CHUNK, KEYS), 1)
    late = row >= BLOCK
    low = jnp.where(late, BLOCK, 0)
    edge = 3 * BLOCK
    ok = (col >= low) & (col <= BLOCK + row)
    if chunk == 0:
        ok = ok & ((col >= BLOCK) | jnp.logical_not(first))
    bias = jnp.where(ok & (col < edge), 0.0, -1e30)
    for level in range(1, LEVELS):
        start = edge + BLOCK * (level - 1)
        inside = (col >= start) & (col < start + BLOCK)
        half = inside & (col < start + BLOCK // 2)
        if level == 1:
            ok = half | (inside & late)
        else:
            ok = inside if (chunk >> (level - 2)) & 1 else half
        if chunk >> (level - 1) == 0:
            ok = ok & jnp.logical_not(first)
        bias = jnp.where(ok, math.log(2**level), bias)
    return bias


def window_rows(kv, coarse, recv, chunk, low, high, span):
    start = CHUNK * chunk
    if chunk == 0:
        parts = [recv[0:BLOCK, low:high], kv[0:CHUNK, low:high]]
    else:
        parts = [kv[start - BLOCK : start + CHUNK, low:high]]
    for level in range(1, LEVELS):
        block = chunk >> (level - 1)
        if block == 0:
            parts.append(recv[BLOCK * level : BLOCK * (level + 1), low:high])
        else:
            base = level_start(span, level) + BLOCK * (block - 1)
            parts.append(coarse[base : base + BLOCK, low:high])
    return jnp.concatenate(parts, axis=0)


def by_head(rows):
    lane = lax.broadcasted_iota(jnp.int32, (CHUNK, 128), 1)
    zero = jnp.zeros((CHUNK, 128), bf16)
    pairs = []
    for pair in range(HEADS // 2):
        part = rows[:, 128 * pair : 128 * (pair + 1)]
        pairs.append(
            jnp.concatenate(
                [jnp.where(lane < 64, part, zero), jnp.where(lane >= 64, part, zero)], axis=0
            )
        )
    return pairs


def from_heads(pairs):
    lane = lax.broadcasted_iota(jnp.int32, (CHUNK, 128), 1)
    return jnp.concatenate([jnp.where(lane < 64, p[:CHUNK], p[CHUNK:]) for p in pairs], axis=1)


SIDE = 4


def attend(queries, kv, coarse, recv, attended, probs):
    span, width = queries.shape
    first = lax.axis_index("seq") == 0
    rows = CHUNK * HEADS
    for base in range(0, span // CHUNK, SIDE):
        group = range(base, base + SIDE)
        scores = []
        for chunk in group:
            bias = window_bias(chunk, first)
            keys = window_rows(kv, coarse, recv, chunk, 0, width, span)
            split = by_head(queries[CHUNK * chunk : CHUNK * (chunk + 1)])
            raw = [nt(s, keys[:, 128 * p : 128 * (p + 1)]) for p, s in enumerate(split)]
            scores.append(jnp.concatenate(raw, axis=0) + jnp.concatenate([bias] * HEADS, axis=0))
        tops = [jnp.max(s, axis=-1, keepdims=True) for s in scores]
        expos = [jnp.exp(s - t) for s, t in zip(scores, tops)]
        sums = [jnp.sum(e, axis=-1, keepdims=True) for e in expos]
        lows = [(e * (1.0 / t)).astype(bf16) for e, t in zip(expos, sums)]
        for chunk, low in zip(group, lows):
            probs[rows * chunk : rows * (chunk + 1)] = low
            vals = window_rows(kv, coarse, recv, chunk, width, 2 * width, span)
            mixed = [
                nn(low[64 * p : 64 * (p + 1)], vals[:, 128 * p : 128 * (p + 1)])
                for p in range(HEADS // 2)
            ]
            attended[CHUNK * chunk : CHUNK * (chunk + 1)] = from_heads(mixed).astype(bf16)


def core_index():
    return (lax.axis_index("batch") * lax.axis_size("seq") + lax.axis_index("seq")) & 1


def halves(whole, keep, send):
    core = core_index()
    rows = keep.shape[0]
    keep[...] = whole[pl.ds(pl.multiple_of(core * rows, BLOCK), rows)]
    send[...] = whole[pl.ds(pl.multiple_of((1 - core) * rows, BLOCK), rows)]


def feed_forward(
    attended, tokens, w_out, gain, bias, w_up, d_hidden, d_ffn, mid, normed, hidden, d_up, keep, send, whole
):
    span, width = tokens.shape
    ff = w_up.shape[1]
    middle = tokens[...].astype(f32) + nn(attended[...], w_out[...])
    mid[...] = middle
    hat, _ = unit(middle)
    rows = (hat * gain[...].astype(f32)[None] + bias[...].astype(f32)[None]).astype(bf16)
    normed[...] = rows
    c0 = math.sqrt(2.0 / math.pi)
    tile = 256
    for start in range(0, ff, tile):
        cols = slice(start, start + tile)
        x = nn(rows, w_up[:, cols])
        square = x * x
        half = 0.5 + 0.5 * jnp.tanh(x * (c0 + (c0 * 0.044715) * square))
        act = (x * half).astype(bf16)
        slope = half + 2.0 * half * (1.0 - half) * x * (c0 + (3 * c0 * 0.044715) * square)
        hidden[:, cols] = act
        d_up[:, cols] = (slope * d_hidden[:, cols]).astype(bf16)
        whole[cols] = tn(act, d_ffn[...]).astype(bf16)
    halves(whole, keep, send)


def up_back(normed, d_up, keep, send, whole):
    width = normed.shape[1]
    for part in range(d_up.shape[1] // width):
        cols = slice(width * part, width * (part + 1))
        whole[cols] = tn(normed[...], d_up[:, cols]).astype(bf16)
    halves(whole, keep, send)


def mid_back(
    mid, hidden, w_down, d_up, w_up, gain, d_ffn, attended, w_out, out, d_mid, d_attended, keep, send, grad_norm, whole
):
    middle = mid[...]
    out[...] = (middle + nn(hidden[...], w_down[...])).astype(bf16)
    d_normed = nt(d_up[...], w_up[...])
    hat, inv = unit(middle)
    grad_norm[0:1] = jnp.sum(d_normed * hat, axis=0, keepdims=True)
    grad_norm[1:2] = jnp.sum(d_normed, axis=0, keepdims=True)
    d_middle = d_ffn[...].astype(f32) + unit_back(d_normed * gain[...].astype(f32)[None], hat, inv)
    d_mid[...] = d_middle
    d_branch = d_middle.astype(bf16)
    whole[...] = tn(attended[...], d_branch).astype(bf16)
    halves(whole, keep, send)
    d_attended[...] = nt(d_branch, w_out[...]).astype(bf16)


def attend_back(queries, kv, coarse, recv, probs, d_attended, d_proj, lent, fine, wide):
    span, width = queries.shape
    rows = CHUNK * HEADS
    scale = 1.0 / math.sqrt(width // HEADS)
    fine[...] = jnp.zeros_like(fine)
    wide[...] = jnp.zeros_like(wide)
    zero = jnp.zeros((2 * CHUNK, 128), bf16)

    def widened(split, quad):
        return jnp.concatenate(
            [
                jnp.concatenate([split[2 * quad], zero], axis=1),
                jnp.concatenate([zero, split[2 * quad + 1]], axis=1),
            ],
            axis=0,
        )

    for base in range(0, span // CHUNK, SIDE):
        group = range(base, base + SIDE)
        softs, d_probs, splits_a = [], [], []
        for chunk in group:
            vals = window_rows(kv, coarse, recv, chunk, width, 2 * width, span)
            split = by_head(d_attended[CHUNK * chunk : CHUNK * (chunk + 1)])
            splits_a.append(split)
            softs.append(probs[rows * chunk : rows * (chunk + 1)].astype(f32))
            d_probs.append(
                jnp.concatenate(
                    [nt(s, vals[:, 128 * p : 128 * (p + 1)]) for p, s in enumerate(split)], axis=0
                )
            )
        inners = [jnp.sum(s * d, axis=-1, keepdims=True) for s, d in zip(softs, d_probs)]
        d_scores = [(s * (d - t)).astype(bf16) for s, d, t in zip(softs, d_probs, inners)]
        for chunk, d_score, split_a in zip(group, d_scores, splits_a):
            start = CHUNK * chunk
            keys = window_rows(kv, coarse, recv, chunk, 0, width, span)
            mixed = [
                nn(d_score[64 * p : 64 * (p + 1)], keys[:, 128 * p : 128 * (p + 1)])
                for p in range(HEADS // 2)
            ]
            d_proj[start : start + CHUNK, :width] = (from_heads(mixed) * scale).astype(bf16)
            split_q = by_head(queries[start : start + CHUNK])
            low = probs[rows * chunk : rows * (chunk + 1)]
            for part, (left, split) in enumerate(((d_score, split_q), (low, split_a))):
                for quad in range(HEADS // 4):
                    grad = tn(left[128 * quad : 128 * (quad + 1)], widened(split, quad))
                    cols = slice(width * part + 256 * quad, width * part + 256 * (quad + 1))
                    fine[start : start + 3 * BLOCK, cols] += grad[: 3 * BLOCK]
                    for level in range(1, LEVELS):
                        at = level_start(span, level) + BLOCK * (chunk >> (level - 1))
                        own = BLOCK * (level + 2)
                        wide[at : at + BLOCK, cols] += grad[own : own + BLOCK]

    zero = jnp.zeros((BLOCK, 2 * width), bf16)
    lent[0:BLOCK] = fine[0:BLOCK].astype(bf16)
    parts = []
    for level in range(1, LEVELS):
        at, end = level_start(span, level), level_start(span, level + 1)
        lent[BLOCK * level : BLOCK * (level + 1)] = wide[at : at + BLOCK].astype(bf16)
        if at + BLOCK < end:
            parts.append(wide[at + BLOCK : end].astype(bf16))
        parts.append(zero)
    spread = tn(pool_matrix(span), jnp.concatenate(parts, axis=0))
    d_proj[:, width:] = (fine[BLOCK:] + spread).astype(bf16)


def project_back(
    d_proj, lent, recv, normed, w_qkv, tokens, grad_norm, gain, bias, d_normed, keep, send, whole
):
    span, width = tokens.shape
    grads, away = d_proj[...], lent[...]
    gains, shifts = gain[...].astype(f32)[None], bias[...].astype(f32)[None]
    edge_hat = recv[:, 2 * width :].astype(f32)
    edge_normed = (edge_hat * gains + shifts).astype(bf16)
    whole[:, :width] = tn(normed[...], grads[:, :width]).astype(bf16)
    whole[:, width : 3 * width] = (
        tn(normed[...], grads[:, width:]) + tn(edge_normed, away)
    ).astype(bf16)
    d_rows = nt(grads, w_qkv[...])
    d_normed[...] = d_rows
    d_edge = nt(away, w_qkv[:, width:])
    hat, _ = unit(tokens[...].astype(f32))
    small = [
        jnp.sum(d_rows * hat, axis=0, keepdims=True) + jnp.sum(d_edge * edge_hat, axis=0, keepdims=True),
        jnp.sum(d_rows, axis=0, keepdims=True) + jnp.sum(d_edge, axis=0, keepdims=True),
        grad_norm[0:2],
        jnp.zeros((124, width), f32),
    ]
    whole[:, 3 * width :] = jnp.concatenate(small, axis=0).T.astype(bf16)
    halves(whole, keep, send)


def tokens_back(d_normed, back, w_qkv, tokens, gain, d_mid, d_tokens):
    span, width = tokens.shape
    d_edge = nt(back[...], w_qkv[:, width:]).astype(bf16)
    grad = d_normed[...] + tn(edge_matrix(span), d_edge)
    hat, inv = unit(tokens[...].astype(f32))
    d_tokens[...] = (
        d_mid[...] + unit_back(grad * gain[...].astype(f32)[None], hat, inv)
    ).astype(bf16)


def half_of(step, rows, base=0):
    index = lax.axis_index("batch") * lax.axis_size("seq") + lax.axis_index("seq")
    bit = jnp.where((index & 1) == 1, index >> step[1], index >> step[0]) & 1
    here, away = base + bit * rows, base + (1 - bit) * rows
    return pl.ds(pl.multiple_of(here, BLOCK), rows), pl.ds(pl.multiple_of(away, BLOCK), rows)


def add(own, other, total):
    total[...] = own[...] + other[...]


def join(step, parts, own, other, both):
    at = 0
    for rows in parts:
        here, away = half_of(step, rows, 2 * at)
        both[here] = own[at : at + rows]
        both[away] = other[at : at + rows]
        at += rows


def finish_down(own, other, out, tile, sems):
    rows = own.shape[0]
    size = tile.shape[1]
    core = core_index()
    copies = []
    for half, ref in enumerate((own, other)):
        base = (core ^ half) * rows
        for part in range(rows // size):
            slot = half * (rows // size) + part
            tile[slot] = ref[size * part : size * (part + 1)].astype(f32)
            at = pl.ds(pl.multiple_of(base + size * part, size), size)
            copies.append(pltpu.make_async_copy(tile.at[slot], out.at[at], sems.at[slot]))
            copies[-1].start()
    for copy in copies:
        copy.wait()


def finish_up(own, other, out, small, tile, small_tile, sems):
    width, ff = out.shape
    across = ff // width // 2
    rest = small.shape[0] // 2
    core = core_index()
    copies = []
    for half, ref in enumerate((own, other)):
        base = (core ^ half) * across
        for part in range(across):
            slot = half * across + part
            tile[slot] = ref[width * part : width * (part + 1)].astype(f32)
            cols = pl.ds(pl.multiple_of((base + part) * width, width), width)
            copies.append(pltpu.make_async_copy(tile.at[slot], out.at[:, cols], sems.at[slot]))
            copies[-1].start()
        small_tile[half] = ref[width * across :].astype(f32)
        at = pl.ds(pl.multiple_of((core ^ half) * rest, rest), rest)
        copies.append(
            pltpu.make_async_copy(small_tile.at[half], small.at[at], sems.at[2 * across + half])
        )
        copies[-1].start()
    for copy in copies:
        copy.wait()


def finish_rest(own, other, g_qkv, gain1, bias1, gain2, bias2, tile, sems):
    rows = own.shape[0]
    cols = g_qkv.shape[1]
    core = core_index()
    copies = []
    for half, ref in enumerate((own, other)):
        at = pl.ds(pl.multiple_of((core ^ half) * rows, BLOCK), rows)
        tile[half] = ref[:, :cols].astype(f32)
        copies.append(pltpu.make_async_copy(tile.at[half], g_qkv.at[at], sems.at[half]))
        copies[-1].start()
    mine, yours = own[:, cols:].astype(f32), other[:, cols:].astype(f32)
    low = core == 0
    small = jnp.concatenate(
        [jnp.where(low, mine, yours), jnp.where(low, yours, mine)], axis=0
    ).T
    for i, ref in enumerate((gain1, bias1, gain2, bias2)):
        ref[...] = small[i]
    for copy in copies:
        copy.wait()


def flips(size, even, odd):
    return [(i, i ^ (1 << (odd if i & 1 else even))) for i in range(size)]


def add_split(step, *refs):
    parts = (len(refs) - 2) // 2
    keep, send = refs[2 * parts :]
    at = 0
    for own, other in zip(refs[:parts], refs[parts : 2 * parts]):
        rows = own.shape[0] // 2
        here, away = half_of(step, rows)
        send[at : at + rows] = own[away] + other[away]
        keep[at : at + rows] = own[here] + other[here]
        at += rows


class Sum:
    def __init__(self, keep, send, orders, size):
        self.own, self.away = keep, send
        self.parts = [v.shape[0] // 2 for v in keep]
        self.steps = [(0, 0)] + list(zip(*orders))
        self.size = size
        self.at, self.back = 0, False

    def start(self):
        value = self.own if self.back or self.at == len(self.steps) - 1 else self.away
        pairs = flips(self.size, *self.steps[self.at])
        self.other = [lax.ppermute(v, ("batch", "seq"), pairs) for v in value]

    def turn(self, *deps):
        result = self.done(*deps)
        if self.at >= 0:
            self.start()
        return result

    def done(self, *deps):
        own, other = self.own, self.other
        rows, cols = sum(v.shape[0] for v in own), own[0].shape[1]
        last = len(self.steps) - 1
        whole = ((rows, cols), bf16)
        if self.back:
            step = self.steps[self.at]
            self.at -= 1
            if self.at < 0:
                self.own = own[0]
                return other[0]
            parts = self.parts if self.at == 0 else (rows,)
            self.own = call(
                partial(join, step, parts), [((2 * rows, cols), bf16)], *own, *other, deps=deps, name="join"
            )
        elif self.at >= last - 1:
            self.own = call(add, [whole], *own, *other, deps=deps, name="add")
            if self.at == last:
                self.back, self.at = True, last - 1
            else:
                self.at += 1
        else:
            half = ((rows // 2, cols), bf16)
            keep, send = call(
                partial(add_split, self.steps[self.at + 1]), [half, half], *own, *other,
                deps=deps, name="add_split",
            )
            self.own, self.away = [keep], [send]
            self.at += 1
        return self.own[0]


TAIL = "DUDRUDRUDRURDRURDRURDURDUR"


def body(
    tokens, prefix, cotangent, gain1, bias1, w_qkv, w_out, gain2, bias2, w_up, w_down
):
    row_count, span, width = tokens.shape
    ff = w_up.shape[1]
    seq_size, batch_size = lax.axis_size("seq"), lax.axis_size("batch")
    size = seq_size * batch_size
    tokens = tokens.reshape(span, width)
    cotangent = cotangent.reshape(span, width)
    edge_rows = BLOCK * LEVELS
    coarse_rows = level_start(span, LEVELS)
    dma = pltpu.SemaphoreType.DMA
    flat = ((span, width), bf16)
    pair = ((span, 2 * width), bf16)
    pooled = ((coarse_rows, 2 * width), bf16)
    (hat1,) = call(standardize, [((span, width), f32)], tokens, name="standardize", us=3)
    normed1, queries, kv, coarse, edge = call(
        project,
        [flat, flat, pair, pooled, ((edge_rows, 3 * width), bf16)],
        hat1, gain1, bias1, w_qkv, name="project", us=3,
    )
    onward = [(i, (i + 1) % seq_size) for i in range(seq_size)]
    recv = lax.ppermute(edge, "seq", onward)
    d_ffn, d_hidden = call(
        hidden_back, [flat, ((span, ff), f32)], prefix, cotangent, w_down,
        smem=(0,), name="hidden_back",
    )
    attended, probs = call(
        attend,
        [flat, ((span * HEADS, KEYS), bf16)],
        queries, kv, coarse, recv,
        deps=(d_ffn,), name="attend",
    )
    mid, normed2, hidden, d_up, keep_down, send_down = call(
        feed_forward,
        [((span, width), f32), flat, ((span, ff), bf16), ((span, ff), bf16),
         ((ff // 2, width), bf16), ((ff // 2, width), bf16)],
        attended, tokens, w_out, gain2, bias2, w_up, d_hidden, d_ffn,
        scratch=[pltpu.VMEM((ff, width), bf16)], name="feed_forward",
    )
    bits = list(range(1, size.bit_length() - 1))
    one = (bits, bits[1:] + bits[:1])
    two = (bits[1:2] + bits[:1] + bits[2:], bits[:1] + bits[2:] + bits[1:2])
    down = Sum([keep_down], [send_down], one, size)
    down.start()
    half = ((ff // 2, width), bf16)
    keep_up, send_up = call(
        up_back, [half, half], normed2, d_up, scratch=[pltpu.VMEM((ff, width), bf16)], name="up_back",
    )
    step = down.turn(keep_up)
    half = ((width // 2, width), bf16)
    out, d_mid, d_attended, keep_out, send_out, grad_norm = call(
        mid_back,
        [flat, ((span, width), f32), flat, half, half, ((8, width), f32)],
        mid, hidden, w_down, d_up, w_up, gain2, d_ffn, attended, w_out,
        deps=(step,), scratch=[pltpu.VMEM((width, width), bf16)], name="mid_back",
    )
    up = Sum([keep_up, keep_out], [send_up, send_out], two, size)
    up.start()
    step = up.turn(d_attended)
    d_proj, lent = call(
        attend_back,
        [((span, 3 * width), bf16), ((edge_rows, 2 * width), bf16)],
        queries, kv, coarse, recv, probs, d_attended,
        deps=(step,),
        scratch=[pltpu.VMEM((span + BLOCK, 2 * width), f32), pltpu.VMEM((coarse_rows, 2 * width), f32)],
        name="attend_back", limit=16,
    )
    step = down.turn(d_proj)
    half = ((width // 2, 3 * width + 128), bf16)
    d_normed, keep_rest, send_rest = call(
        project_back,
        [((span, width), f32), half, half],
        d_proj, lent, recv, normed1, w_qkv, tokens, grad_norm, gain1, bias1,
        deps=(step,), scratch=[pltpu.VMEM((width, 3 * width + 128), bf16)], name="project_back",
    )
    rest = Sum([keep_rest], [send_rest], one, size)
    rest.start()
    back = lax.ppermute(lent, "seq", [(b, a) for a, b in onward])
    step = up.turn(keep_rest)
    step = rest.turn(step)
    (d_tokens,) = call(
        tokens_back, [flat], d_normed, back, w_qkv, tokens, gain1, d_mid,
        deps=(step,), name="tokens_back",
    )
    step = d_tokens
    ends = {}
    sums = {"D": down, "U": up, "R": rest}
    for key in TAIL * 2:
        if key in ends:
            continue
        step = sums[key].turn(step)
        if sums[key].at < 0:
            ends[key] = (sums[key].own, step)
    tiles = lambda count, rows, cols: pltpu.VMEM((count, rows, cols), f32)
    (grad_down,) = call(
        finish_down, [((ff, width), f32)], *ends["D"], far_out=(0,),
        scratch=[tiles(8, ff // 8, width), dma((8,))], name="finish_down", limit=12,
    )
    grad_up, grad_out = call(
        finish_up, [((width, ff), f32), ((width, width), f32)], *ends["U"], far_out=(0, 1),
        scratch=[tiles(ff // width, width, width), tiles(2, width // 2, width), dma((ff // width + 2,))],
        name="finish_up", limit=12,
    )
    line = ((width,), f32)
    grad_qkv, g_gain1, g_bias1, g_gain2, g_bias2 = call(
        finish_rest, [((width, 3 * width), f32), line, line, line, line],
        *ends["R"], far_out=(0,),
        scratch=[tiles(2, width // 2, 3 * width), dma((2,))],
        name="finish_rest", limit=12,
    )
    shape = (row_count, span, width)
    return (
        out.reshape(shape), d_tokens.reshape(shape), g_gain1, g_bias1, grad_qkv, grad_out,
        g_gain2, g_bias2, grad_up, grad_down,
    )


def solution(mesh):
    placed = (
        P("batch", "seq", None),
        P("batch"),
        P("batch", "seq", None),
        P(),
        P(),
        P(),
        P(),
        P(),
        P(),
        P(),
        P(),
    )
    return jax.shard_map(
        body,
        mesh=mesh,
        in_specs=placed,
        out_specs=(
            P("batch", "seq", None),
            P("batch", "seq", None),
            P(),
            P(),
            P(),
            P(),
            P(),
            P(),
            P(),
            P(),
        ),
        check_vma=False,
    )
```

time: 164 us -> 132 us (0.80)
  other arithmetic: 19.7 us -> 0 us
  local copies, waits for them, and re-layouts: 15 us -> 3.2 us
  waiting for transfers between devices: 53.4 us -> 55.5 us
    convert_element_type x20 -> x0, other arithmetic: 12.8 us -> none  [the longest x3 3.52 us: reduce_scatter(): own = own.astype(bf16)]
    unnamed x46 -> x24, local copies, waits for them, and re-layouts: 12 us -> 3.2 us
    select_n x14 -> x0, other arithmetic: 6.86 us -> none  [all_gather(): jnp.where(bit == 0, jnp.concatenate([own, other], 0), jnp.concatenate([ot...]
    ppermute x1, waiting for transfers between devices: 0.01 us -> 4.32 us  [body(): recv = lax.ppermute(edge, 'seq', onward)]
    ppermute x30 -> x28, starting transfers between devices: 34 us -> 36.7 us  [start(): self.other = [lax.ppermute(v, ('batch', 'seq'), pairs) for v in value]]
    ppermute x1, waiting for transfers between devices: 2.05 us -> 0.01 us  [body(): back = lax.ppermute(lent, 'seq', [(b, a) for a, b in onward])]
    ppermute x1, starting transfers between devices: 2.36 us -> 0.51 us  [body(): recv = lax.ppermute(edge, 'seq', onward)]
    pallas_call x8 -> x37, Pallas kernels: 35.5 us -> 33.9 us  [call(): pl.pallas_call(run, out_shape=[jax.ShapeDtypeStruct(s, d) for s, d in out...]
  transfers between devices with their start and end apart: 32 -> 30, of which waited for: 14 -> 17; matrix products, arithmetic and copies ran while one was open for 10% -> 0% of each run, Pallas kernels for 10% -> 14%
where the time goes in v2:
time: 132 us
  waiting for transfers between devices  55.5 us (42%)
  starting transfers between devices  37.5 us (28%)
  Pallas kernels  33.9 us (26%)
  local copies, waits for them, and re-layouts  3.2 us (2%)
  between operations  1.8 us (1%)
    ppermute x28, waiting for transfers between devices, start(): self.other = [lax.ppermute(v, ('batch', 'seq'), pairs) for v in value]  51.2 us
    ppermute x28, starting transfers between devices, start(): self.other = [lax.ppermute(v, ('batch', 'seq'), pairs) for v in value]  36.7 us
    pallas_call x37, Pallas kernels, call(): pl.pallas_call(run, out_shape=[jax.ShapeDtypeStruct(s, d) for s, d in out...  33.9 us
    ppermute x1, waiting for transfers between devices, body(): recv = lax.ppermute(edge, 'seq', onward)  4.32 us
    unnamed x24, local copies, waits for them, and re-layouts  3.2 us
  transfers between devices with their start and end apart: 30, of which 17 were waited for; matrix products, arithmetic and copies ran while one was open for 0% of the time, Pallas kernels for 14%

profile of v2, /device:TPU:0, one launch (start us, length us, event | category | flops | bytes accessed | tf_op | source)
XLA Modules:
  0.0 131.8 jit_solution(2193775530293618800)
XLA Ops:
  0.7 1.0 copy-done.3
  1.7 0.3 standardize.1.refs_0_
  2.0 1.1 copy-done.2
  3.1 1.6 %project.1 = (bf16[512,512]{1,0:T(8,128)(2,1)S(1)}, bf16[512,512]{1,0:T(8,128)(2,1)S(1)}, bf16[512,1024]{1,0:T(8,128)(2,1)S(1)}, bf16[496,1024]{1,0:T(8,128)(2,1)S(1)}, bf16[96,1536]{1,0:T(8,128)(2,1)S(1)}) custom-call(f32[512,512]{1,0:T(8,128)S(1)} %standardize.1.refs_0_, bf16[512]{0:T(512)(128)(2,1)S(1)} %copy-done.9, bf16[512]{0:T(512)(128)(2,1)S(1)} %copy-done.11, ...), custom_call_target="tpu_custom_call" | custom-call | flops 3449999872 | bytes 65536 | tf_op jit(solution)/shard_map/project/pallas_call | solution.py:45
  4.8 0.5 collective-permute-start
  5.9 1.3 hidden_back.1
  7.3 4.3 %collective-permute-done.refs_3_.refs_2_ = bf16[96,1536]{1,0:T(8,128)(2,1)S(1)} collective-permute-done((bf16[96,1536]{1,0:T(8,128)(2,1)S(1)}, bf16[96,1536]{1,0:T(8,128)(2,1)S(1)}, u32[]{:S(2)}, u32[]{:S(2)}) %collective-permute-start) | collective-permute-done | bytes 294944 | tf_op jit(solution)/shard_map/ppermute | solution.py:548
  11.6 2.8 %attend.1 = (bf16[512,512]{1,0:T(8,128)(2,1)S(1)}, bf16[4096,128]{1,0:T(8,128)(2,1)S(1)}) custom-call(bf16[512,512]{1,0:T(8,128)(2,1)S(1)} %get-tuple-element.63.refs_0_, bf16[512,1024]{1,0:T(8,128)(2,1)S(1)} %get-tuple-element.64.refs_1_, bf16[496,1024]{1,0:T(8,128)(2,1)S(1)} %get-tuple-element.65.refs_2_, ...), custom_call_target="tpu_custom_call" | custom-call | flops 575000000 | bytes 65536 | tf_op jit(solution)/shard_map/attend/pallas_call | solution.py:45
  14.5 5.0 %feed_forward.1 = (f32[512,512]{1,0:T(8,128)S(1)}, bf16[512,512]{1,0:T(8,128)(2,1)S(1)}, bf16[512,2048]{1,0:T(8,128)(2,1)S(1)}, bf16[512,2048]{1,0:T(8,128)(2,1)...) custom-call(bf16[512,512]{1,0:T(8,128)(2,1)S(1)} %get-tuple-element.68.refs_0_.refs_7_, ...), custom_call_target="tpu_custom_call" | custom-call | flops 575000000 | bytes 65536 | tf_op jit(solution)/shard_map/feed_forward/pallas_call | solution.py:45
  19.5 1.5 %up_back.1 = (bf16[1024,512]{1,0:T(8,128)(2,1)S(1)}, bf16[1024,512]{1,0:T(8,128)(2,1)S(1)}) custom-call(bf16[512,512]{1,0:T(8,128)(2,1)S(1)} %get-tuple-element.75.refs_0_, bf16[512,2048]{1,0:T(8,128)(2,1)S(1)} %get-tuple-element.72.refs_1_.refs_3_), custom_call_target="tpu_custom_call" | custom-call | flops 575000000 | bytes 65536 | tf_op jit(solution)/shard_map/up_back/pallas_call | solution.py:45
  21.1 0.6 collective-permute-start.2
  21.7 0.5 collective-permute-done.1.refs_1_
  22.2 0.1 add_split.9
  22.3 2.4 %collective-permute-start.4 = (bf16[512,512]{1,0:T(8,128)(2,1)S(1)}, bf16[512,512]{1,0:T(8,128)(2,1)S(1)}, u32[]{:S(2)}, u32[]{:S(2)}) collective-permute-start(bf16[512,512]{1,0:T(8,128)(2,1)S(1)} %get-tuple-element.89), channel_id=1, source_target_pairs={{0,2},{1,5},{2,0},{3,7},{4,6},{5,1},{6,4},{7,3},{8,10},{9,13},{10,... | collective-permute-start | bytes 1572872 | tf_op jit(solution)/shard_map/ppermute | solution.py:483
  24.7 3.7 %mid_back.1 = (bf16[512,512]{1,0:T(8,128)(2,1)}, f32[512,512]{1,0:T(8,128)S(1)}, bf16[512,512]{1,0:T(8,128)(2,1)S(1)}, bf16[256,512]{1,0:T(8,128)(2,1)S(1)}, bf1...) custom-call(f32[512,512]{1,0:T(8,128)S(1)} %get-tuple-element.70.refs_0_, ...), custom_call_target="tpu_custom_call" | custom-call | flops 575000000 | bytes 65536 | tf_op jit(solution)/shard_map/mid_back/pallas_call | solution.py:45
  28.4 1.5 %collective-permute-done.3.refs_3_ = bf16[256,512]{1,0:T(8,128)(2,1)S(1)} collective-permute-done((bf16[256,512]{1,0:T(8,128)(2,1)S(1)}, bf16[256,512]{1,0:T(8,128)(2,1)S(1)}, u32[]{:S(2)}, u32[]{:S(2)}) %collective-permute-start.3) | collective-permute-done | bytes 262176 | tf_op jit(solution)/shard_map/ppermute | solution.py:483
  29.9 0.2 add_split.10
  30.1 4.6 %attend_back.1 = (bf16[512,1536]{1,0:T(8,128)(2,1)S(1)}, bf16[96,1024]{1,0:T(8,128)(2,1)S(1)}) custom-call(bf16[512,512]{1,0:T(8,128)(2,1)S(1)} %get-tuple-element.63.refs_0_, bf16[512,1024]{1,0:T(8,128)(2,1)S(1)} %get-tuple-element.64.refs_1_, bf16[496,1024]{1,0:T(8,128)(2,1)S(1)} %get-tuple-element.65.refs_2_, ...), custom_call_target="tpu_custom_call" | custom-call | flops 575000000 | bytes 65536 | tf_op jit(solution)/shard_map/attend_back/pallas_call | solution.py:45
  34.8 2.7 %project_back.1 = (f32[512,512]{1,0:T(8,128)S(1)}, bf16[256,1664]{1,0:T(8,128)(2,1)S(1)}, bf16[256,1664]{1,0:T(8,128)(2,1)S(1)}) custom-call(bf16[512,1536]{1,0:T(8,128)(2,1)S(1)} %get-tuple-element.85.refs_2_.refs_0_, bf16[96,1024]{1,0:T(8,128)(2,1)S(1)} %get-tuple-element.86.refs_1_, bf16[96,1536]{1,0:T(8,128)(2,1)S(1)} %collective-permute-done.refs_3_.refs_2_, ...), custom_call_target="tpu_custom_call" | custom-call | flops 575000000 | bytes 65536 | tf_op jit(solution)/shard_map/project_back/pallas_call | solution.py:45
  37.6 0.2 collective-permute-start.6
  37.8 1.5 %collective-permute-start.7 = (bf16[640,512]{1,0:T(8,128)(2,1)S(1)}, bf16[640,512]{1,0:T(8,128)(2,1)S(1)}, u32[]{:S(2)}, u32[]{:S(2)}) collective-permute-start(bf16[640,512]{1,0:T(8,128)(2,1)S(1)} %get-tuple-element.95), channel_id=1, source_target_pairs={{0,4},{1,3},{2,6},{3,1},{4,0},{5,7},{6,2},{7,5},{8,12},{9,11},{10,... | collective-permute-start | bytes 1966088 | tf_op jit(solution)/shard_map/ppermute | solution.py:483
  39.3 0.2 collective-permute-start.5
  39.5 1.5 %collective-permute-start.9 = (bf16[256,512]{1,0:T(8,128)(2,1)S(1)}, bf16[256,512]{1,0:T(8,128)(2,1)S(1)}, u32[]{:S(2)}, u32[]{:S(2)}) collective-permute-start(bf16[256,512]{1,0:T(8,128)(2,1)S(1)} %get-tuple-element.99), channel_id=1, source_target_pairs={{0,4},{1,9},{2,6},{3,11},{4,0},{5,13},{6,2},{7,15},{8,12},{9,1},{1... | collective-permute-start | bytes 786440 | tf_op jit(solution)/shard_map/ppermute | solution.py:483
  41.0 7.4 %collective-permute-done.7.refs_1_ = bf16[640,512]{1,0:T(8,128)(2,1)S(1)} collective-permute-done((bf16[640,512]{1,0:T(8,128)(2,1)S(1)}, bf16[640,512]{1,0:T(8,128)(2,1)S(1)}, u32[]{:S(2)}, u32[]{:S(2)}) %collective-permute-start.7) | collective-permute-done | bytes 655392 | tf_op jit(solution)/shard_map/ppermute | solution.py:483
  48.4 0.1 add_split.12
  48.5 1.3 collective-permute-start.11
  49.7 0.1 add_split.13
  49.9 0.9 collective-permute-start.8
  50.7 1.9 %tokens_back.1.refs_2_ = bf16[512,512]{1,0:T(8,128)(2,1)} custom-call(f32[512,512]{1,0:T(8,128)S(1)} %get-tuple-element.91.refs_0_, bf16[96,1024]{1,0:T(8,128)(2,1)S(1)} %collective-permute-done.5.refs_1_, bf16[512,1536]{1,0:T(8,128)(2,1)S(1)} %copy-done.2, bf16[512,512]{1,0:T(8,128)(2,1)S(1)} %bitcast.7, bf16[512]{0:T(512)(128)(2,1)S(1)} %copy-done.9, ...), custom_call_target="tpu_custom_call" | custom-call | flops 575000000 | bytes 65536 | tf_op jit(solution)/shard_map/tokens_back/pallas_call | solution.py:45
  52.6 1.0 copy-done.6
  53.7 1.6 %collective-permute-start.10 = (bf16[128,512]{1,0:T(8,128)(2,1)S(1)}, bf16[128,512]{1,0:T(8,128)(2,1)S(1)}, u32[]{:S(2)}, u32[]{:S(2)}) collective-permute-start(bf16[128,512]{1,0:T(8,128)(2,1)S(1)} %get-tuple-element.101), channel_id=1, source_target_pairs={{0,8},{1,17},{2,10},{3,19},{4,12},{5,21},{6,14},{7,23},{8,0},{9,25... | collective-permute-start | bytes 393224 | tf_op jit(solution)/shard_map/ppermute | solution.py:483
  55.4 0.2 collective-permute-done.11.refs_1_
  55.6 1.6 %collective-permute-start.14 = (bf16[160,512]{1,0:T(8,128)(2,1)S(1)}, bf16[160,512]{1,0:T(8,128)(2,1)S(1)}, u32[]{:S(2)}, u32[]{:S(2)}) collective-permute-start(bf16[160,512]{1,0:T(8,128)(2,1)S(1)} %get-tuple-element.106), channel_id=1, source_target_pairs={{0,8},{1,17},{2,10},{3,19},{4,12},{5,21},{6,14},{7,23},{8,0},{9,25... | collective-permute-start | bytes 491528 | tf_op jit(solution)/shard_map/ppermute | solution.py:483
  57.3 1.5 %collective-permute-done.10.refs_1_ = bf16[128,512]{1,0:T(8,128)(2,1)S(1)} collective-permute-done((bf16[128,512]{1,0:T(8,128)(2,1)S(1)}, bf16[128,512]{1,0:T(8,128)(2,1)S(1)}, u32[]{:S(2)}, u32[]{:S(2)}) %collective-permute-start.10) | collective-permute-done | bytes 131104 | tf_op jit(solution)/shard_map/ppermute | solution.py:483
  58.8 1.4 %collective-permute-done.8.refs_1_ = bf16[128,1664]{1,0:T(8,128)(2,1)S(1)} collective-permute-done((bf16[128,1664]{1,0:T(8,128)(2,1)S(1)}, bf16[128,1664]{1,0:T(8,128)(2,1)S(1)}, u32[]{:S(2)}, u32[]{:S(2)}) %collective-permute-start.8) | collective-permute-done | bytes 426016 | tf_op jit(solution)/shard_map/ppermute | solution.py:483
  60.2 1.6 %collective-permute-start.12 = (bf16[64,1664]{1,0:T(8,128)(2,1)S(1)}, bf16[64,1664]{1,0:T(8,128)(2,1)S(1)}, u32[]{:S(2)}, u32[]{:S(2)}) collective-permute-start(bf16[64,1664]{1,0:T(8,128)(2,1)S(1)} %get-tuple-element.105), channel_id=1, source_target_pairs={{0,4},{1,9},{2,6},{3,11},{4,0},{5,13},{6,2},{7,15},{8,12},{9,1},{1... | collective-permute-start | bytes 638984 | tf_op jit(solution)/shard_map/ppermute | solution.py:483
  61.8 2.6 %collective-permute-start.13 = (bf16[128,512]{1,0:T(8,128)(2,1)S(1)}, bf16[128,512]{1,0:T(8,128)(2,1)S(1)}, u32[]{:S(2)}, u32[]{:S(2)}) collective-permute-start(bf16[128,512]{1,0:T(8,128)(2,1)S(1)} %add.6.refs_2_.refs_0_), channel_id=1, source_target_pairs={{0,16},{1,3},{2,18},{3,1},{4,20},{5,7},{6,22},{7,5},{8,24},{9,11},... | collective-permute-start | bytes 393224 | tf_op jit(solution)/shard_map/ppermute | solution.py:483
  64.4 1.8 %collective-permute-start.17 = (bf16[160,512]{1,0:T(8,128)(2,1)S(1)}, bf16[160,512]{1,0:T(8,128)(2,1)S(1)}, u32[]{:S(2)}, u32[]{:S(2)}) collective-permute-start(bf16[160,512]{1,0:T(8,128)(2,1)S(1)} %add.7.refs_2_.refs_0_), channel_id=1, source_target_pairs={{0,16},{1,5},{2,18},{3,7},{4,20},{5,1},{6,22},{7,3},{8,24},{9,13},... | collective-permute-start | bytes 491528 | tf_op jit(solution)/shard_map/ppermute | solution.py:483
  66.2 2.0 %collective-permute-done.13.refs_1_ = bf16[128,512]{1,0:T(8,128)(2,1)S(1)} collective-permute-done((bf16[128,512]{1,0:T(8,128)(2,1)S(1)}, bf16[128,512]{1,0:T(8,128)(2,1)S(1)}, u32[]{:S(2)}, u32[]{:S(2)}) %collective-permute-start.13) | collective-permute-done | bytes 131104 | tf_op jit(solution)/shard_map/ppermute | solution.py:483
  68.2 8.9 %collective-permute-start.16 = (bf16[128,512]{1,0:T(8,128)(2,1)S(1)}, bf16[128,512]{1,0:T(8,128)(2,1)S(1)}, u32[]{:S(2)}, u32[]{:S(2)}) collective-permute-start(bf16[128,512]{1,0:T(8,128)(2,1)S(1)} %add.8.refs_2_.refs_0_), channel_id=1, source_target_pairs={{0,8},{1,17},{2,10},{3,19},{4,12},{5,21},{6,14},{7,23},{8,0},{9,25... | collective-permute-start | bytes 393224 | tf_op jit(solution)/shard_map/ppermute | solution.py:483
  77.1 1.4 %collective-permute-done.17.refs_1_ = bf16[160,512]{1,0:T(8,128)(2,1)S(1)} collective-permute-done((bf16[160,512]{1,0:T(8,128)(2,1)S(1)}, bf16[160,512]{1,0:T(8,128)(2,1)S(1)}, u32[]{:S(2)}, u32[]{:S(2)}) %collective-permute-start.17) | collective-permute-done | bytes 163872 | tf_op jit(solution)/shard_map/ppermute | solution.py:483
  78.5 2.1 %collective-permute-start.19 = (bf16[160,512]{1,0:T(8,128)(2,1)S(1)}, bf16[160,512]{1,0:T(8,128)(2,1)S(1)}, u32[]{:S(2)}, u32[]{:S(2)}) collective-permute-start(bf16[160,512]{1,0:T(8,128)(2,1)S(1)} %add.9.refs_2_.refs_0_), channel_id=1, source_target_pairs={{0,8},{1,17},{2,10},{3,19},{4,12},{5,21},{6,14},{7,23},{8,0},{9,25... | collective-permute-start | bytes 491528 | tf_op jit(solution)/shard_map/ppermute | solution.py:483
  80.7 3.6 %collective-permute-done.16.refs_1_ = bf16[128,512]{1,0:T(8,128)(2,1)S(1)} collective-permute-done((bf16[128,512]{1,0:T(8,128)(2,1)S(1)}, bf16[128,512]{1,0:T(8,128)(2,1)S(1)}, u32[]{:S(2)}, u32[]{:S(2)}) %collective-permute-start.16) | collective-permute-done | bytes 131104 | tf_op jit(solution)/shard_map/ppermute | solution.py:483
  84.3 0.6 collective-permute-start.21
  84.9 6.3 %collective-permute-done.15.refs_1_ = bf16[32,1664]{1,0:T(8,128)(2,1)S(1)} collective-permute-done((bf16[32,1664]{1,0:T(8,128)(2,1)S(1)}, bf16[32,1664]{1,0:T(8,128)(2,1)S(1)}, u32[]{:S(2)}, u32[]{:S(2)}) %collective-permute-start.15) | collective-permute-done | bytes 106528 | tf_op jit(solution)/shard_map/ppermute | solution.py:483
  91.2 1.3 collective-permute-start.18
  92.6 5.2 %collective-permute-done.18.refs_1_ = bf16[32,1664]{1,0:T(8,128)(2,1)S(1)} collective-permute-done((bf16[32,1664]{1,0:T(8,128)(2,1)S(1)}, bf16[32,1664]{1,0:T(8,128)(2,1)S(1)}, u32[]{:S(2)}, u32[]{:S(2)}) %collective-permute-start.18) | collective-permute-done | bytes 106528 | tf_op jit(solution)/shard_map/ppermute | solution.py:483
  97.9 1.0 collective-permute-start.20
  98.9 3.7 %collective-permute-done.20.refs_1_ = bf16[32,1664]{1,0:T(8,128)(2,1)S(1)} collective-permute-done((bf16[32,1664]{1,0:T(8,128)(2,1)S(1)}, bf16[32,1664]{1,0:T(8,128)(2,1)S(1)}, u32[]{:S(2)}, u32[]{:S(2)}) %collective-permute-start.20) | collective-permute-done | bytes 106528 | tf_op jit(solution)/shard_map/ppermute | solution.py:483
  102.7 0.7 collective-permute-start.22
  103.4 1.5 %collective-permute-start.27 = (bf16[640,512]{1,0:T(8,128)(2,1)S(1)}, bf16[640,512]{1,0:T(8,128)(2,1)S(1)}, u32[]{:S(2)}, u32[]{:S(2)}) collective-permute-start(bf16[640,512]{1,0:T(8,128)(2,1)S(1)} %join.13.refs_2_.refs_0_), channel_id=1, source_target_pairs={{0,4},{1,3},{2,6},{3,1},{4,0},{5,7},{6,2},{7,5},{8,12},{9,11},{10,... | collective-permute-start | bytes 1966088 | tf_op jit(solution)/shard_map/ppermute | solution.py:483
  104.9 0.5 collective-permute-start.25
  105.4 3.3 %collective-permute-done.22.refs_1_ = bf16[64,1664]{1,0:T(8,128)(2,1)S(1)} collective-permute-done((bf16[64,1664]{1,0:T(8,128)(2,1)S(1)}, bf16[64,1664]{1,0:T(8,128)(2,1)S(1)}, u32[]{:S(2)}, u32[]{:S(2)}) %collective-permute-start.22) | collective-permute-done | bytes 213024 | tf_op jit(solution)/shard_map/ppermute | solution.py:483
  108.7 1.7 %collective-permute-start.24 = (bf16[128,1664]{1,0:T(8,128)(2,1)S(1)}, bf16[128,1664]{1,0:T(8,128)(2,1)S(1)}, u32[]{:S(2)}, u32[]{:S(2)}) collective-permute-start(bf16[128,1664]{1,0:T(8,128)(2,1)S(1)} %join.14.refs_2_.refs_0_), channel_id=1, source_target_pairs={{0,2},{1,5},{2,0},{3,7},{4,6},{5,1},{6,4},{7,3},{8,10},{9,13},{10,... | collective-permute-start | bytes 1277960 | tf_op jit(solution)/shard_map/ppermute | solution.py:483
  110.5 3.6 %collective-permute-done.25.refs_1_ = bf16[512,512]{1,0:T(8,128)(2,1)S(1)} collective-permute-done((bf16[512,512]{1,0:T(8,128)(2,1)S(1)}, bf16[512,512]{1,0:T(8,128)(2,1)S(1)}, u32[]{:S(2)}, u32[]{:S(2)}) %collective-permute-start.25) | collective-permute-done | bytes 524320 | tf_op jit(solution)/shard_map/ppermute | solution.py:483
  114.1 0.1 join.15.refs_2_.refs_0_
  114.2 4.5 %collective-permute-done.24.refs_1_ = bf16[128,1664]{1,0:T(8,128)(2,1)S(1)} collective-permute-done((bf16[128,1664]{1,0:T(8,128)(2,1)S(1)}, bf16[128,1664]{1,0:T(8,128)(2,1)S(1)}, u32[]{:S(2)}, u32[]{:S(2)}) %collective-permute-start.24) | collective-permute-done | bytes 426016 | tf_op jit(solution)/shard_map/ppermute | solution.py:483
  118.6 0.1 join.16.refs_0_.refs_2_
  118.7 0.1 join.17.refs_0_
  118.9 0.5 collective-permute-start.29
  119.5 5.2 %collective-permute-done.26.refs_1_ = bf16[256,1664]{1,0:T(8,128)(2,1)S(1)} collective-permute-done((bf16[256,1664]{1,0:T(8,128)(2,1)S(1)}, bf16[256,1664]{1,0:T(8,128)(2,1)S(1)}, u32[]{:S(2)}, u32[]{:S(2)}) %collective-permute-start.26) | collective-permute-done | bytes 852000 | tf_op jit(solution)/shard_map/ppermute | solution.py:483
  124.7 2.4 %finish_rest.1 = (f32[512,1536]{1,0:T(8,128)}, f32[512]{0:T(512)}, f32[512]{0:T(512)}, f32[512]{0:T(512)}, f32[512]{0:T(512)}) custom-call(bf16[256,1664]{1,0:T(8,128)(2,1)S(1)} %join.16.refs_0_.refs_2_, bf16[256,1664]{1,0:T(8,128)(2,1)S(1)} %collective-permute-done.26.refs_1_), custom_call_target="tpu_custom_call" | custom-call | flops 575000000 | bytes 65536 | tf_op jit(solution)/shard_map/finish_rest/pallas_call | solution.py:45
  127.1 2.1 %finish_down.1 = f32[2048,512]{1,0:T(8,128)} custom-call(bf16[1024,512]{1,0:T(8,128)(2,1)S(1)} %join.15.refs_2_.refs_0_, bf16[1024,512]{1,0:T(8,128)(2,1)S(1)} %collective-permute-done.29.refs_1_), custom_call_target="tpu_custom_call" | custom-call | flops 575000000 | bytes 65536 | tf_op jit(solution)/shard_map/finish_down/pallas_call | solution.py:45
  129.2 2.5 %finish_up.1 = (f32[512,2048]{1,0:T(8,128)}, f32[512,512]{1,0:T(8,128)}) custom-call(bf16[1280,512]{1,0:T(8,128)(2,1)S(1)} %join.17.refs_0_, bf16[1280,512]{1,0:T(8,128)(2,1)S(1)} %collective-permute-done.28.refs_1_), custom_call_target="tpu_custom_call" | custom-call | flops 575000000 | bytes 65536 | tf_op jit(solution)/shard_map/finish_up/pallas_call | solution.py:45
  (57 shorter events, 1.0 us)
Async XLA Ops:
  0.6 1.0 copy-start.3
  1.7 1.4 %copy-start.2 = (bf16[512,1536]{1,0:T(8,128)(2,1)S(1)}, bf16[512,1536]{1,0:T(8,128)(2,1)}, u32[]{:S(2)}) copy-start(bf16[512,1536]{1,0:T(8,128)(2,1)} %refs_2_.9) | copy-start | bytes 4718596
  1.7 1.4 %copy-start.9 = (bf16[512]{0:T(512)(128)(2,1)S(1)}, bf16[512]{0:T(512)(128)(2,1)}, u32[]{:S(2)}) copy-start(bf16[512]{0:T(512)(128)(2,1)} %refs_4_.7) | copy-start | bytes 3076
  1.7 1.4 %copy-start.11 = (bf16[512]{0:T(512)(128)(2,1)S(1)}, bf16[512]{0:T(512)(128)(2,1)}, u32[]{:S(2)}) copy-start(bf16[512]{0:T(512)(128)(2,1)} %refs_8_.3) | copy-start | bytes 3076
  3.1 2.8 %copy-start.1 = (bf16[2048,512]{1,0:T(8,128)(2,1)S(1)}, bf16[2048,512]{1,0:T(8,128)(2,1)}, u32[]{:S(2)}) copy-start(bf16[2048,512]{1,0:T(8,128)(2,1)} %refs_2_.8) | copy-start | bytes 6291460
  3.1 2.8 %copy-start.7 = (bf16[1,512,512]{2,1,0:T(8,128)(2,1)S(1)}, bf16[1,512,512]{2,1,0:T(8,128)(2,1)}, u32[]{:S(2)}) copy-start(bf16[1,512,512]{2,1,0:T(8,128)(2,1)} %param.13) | copy-start | bytes 1572868
  4.8 6.9 %collective-permute-start = (bf16[96,1536]{1,0:T(8,128)(2,1)S(1)}, bf16[96,1536]{1,0:T(8,128)(2,1)S(1)}, u32[]{:S(2)}, u32[]{:S(2)}) collective-permute-start(bf16[96,1536]{1,0:T(8,128)(2,1)S(1)} %get-tuple-element.66), channel_id=1, source_target_pairs={{0,1},{1,2},{2,3},{3,0},{4,5},{5,6},{6,7},{7,4},{8,9},{9,10},{10,1... | collective-permute-start | bytes 884744 | tf_op jit(solution)/shard_map/ppermute | solution.py:548
  7.2 7.2 %copy-start = (bf16[512,2048]{1,0:T(8,128)(2,1)S(1)}, bf16[512,2048]{1,0:T(8,128)(2,1)}, u32[]{:S(2)}) copy-start(bf16[512,2048]{1,0:T(8,128)(2,1)} %refs_4_.5) | copy-start | bytes 6291460
  7.3 7.2 %copy-start.4 = (bf16[1,512,512]{2,1,0:T(8,128)(2,1)S(1)}, bf16[1,512,512]{2,1,0:T(8,128)(2,1)}, u32[]{:S(2)}) copy-start(bf16[1,512,512]{2,1,0:T(8,128)(2,1)} %param.11) | copy-start | bytes 1572868
  7.3 7.2 %copy-start.5 = (bf16[512,512]{1,0:T(8,128)(2,1)S(1)}, bf16[512,512]{1,0:T(8,128)(2,1)}, u32[]{:S(2)}) copy-start(bf16[512,512]{1,0:T(8,128)(2,1)} %refs_8_.2) | copy-start | bytes 1572868
  7.3 7.2 %copy-start.8 = (bf16[512]{0:T(512)(128)(2,1)S(1)}, bf16[512]{0:T(512)(128)(2,1)}, u32[]{:S(2)}) copy-start(bf16[512]{0:T(512)(128)(2,1)} %refs_5_.3) | copy-start | bytes 3076
  7.3 7.2 %copy-start.10 = (bf16[512]{0:T(512)(128)(2,1)S(1)}, bf16[512]{0:T(512)(128)(2,1)}, u32[]{:S(2)}) copy-start(bf16[512]{0:T(512)(128)(2,1)} %refs_4_.4) | copy-start | bytes 3076
  19.5 2.7 %collective-permute-start.1 = (bf16[1024,512]{1,0:T(8,128)(2,1)S(1)}, bf16[1024,512]{1,0:T(8,128)(2,1)S(1)}, u32[]{:S(2)}, u32[]{:S(2)}) collective-permute-start(bf16[1024,512]{1,0:T(8,128)(2,1)S(1)} %get-tuple-element.74), channel_id=1, source_target_pairs={{0,1},{1,0},{2,3},{3,2},{4,5},{5,4},{6,7},{7,6},{8,9},{9,8},{10,11... | collective-permute-start | bytes 3145736 | tf_op jit(solution)/shard_map/ppermute | solution.py:483
  21.1 7.3 %collective-permute-start.2 = (bf16[1024,512]{1,0:T(8,128)(2,1)S(1)}, bf16[1024,512]{1,0:T(8,128)(2,1)S(1)}, u32[]{:S(2)}, u32[]{:S(2)}) collective-permute-start(bf16[1024,512]{1,0:T(8,128)(2,1)S(1)} %get-tuple-element.82), channel_id=1, source_target_pairs={{0,1},{1,0},{2,3},{3,2},{4,5},{5,4},{6,7},{7,6},{8,9},{9,8},{10,11... | collective-permute-start | bytes 3145736 | tf_op jit(solution)/shard_map/ppermute | solution.py:483
  22.3 12.4 %collective-permute-start.4 = (bf16[512,512]{1,0:T(8,128)(2,1)S(1)}, bf16[512,512]{1,0:T(8,128)(2,1)S(1)}, u32[]{:S(2)}, u32[]{:S(2)}) collective-permute-start(bf16[512,512]{1,0:T(8,128)(2,1)S(1)} %get-tuple-element.89), channel_id=1, source_target_pairs={{0,2},{1,5},{2,0},{3,7},{4,6},{5,1},{6,4},{7,3},{8,10},{9,13},{10,... | collective-permute-start | bytes 1572872 | tf_op jit(solution)/shard_map/ppermute | solution.py:483
  28.4 1.5 %collective-permute-start.3 = (bf16[256,512]{1,0:T(8,128)(2,1)S(1)}, bf16[256,512]{1,0:T(8,128)(2,1)S(1)}, u32[]{:S(2)}, u32[]{:S(2)}) collective-permute-start(bf16[256,512]{1,0:T(8,128)(2,1)S(1)} %get-tuple-element.83), channel_id=1, source_target_pairs={{0,1},{1,0},{2,3},{3,2},{4,5},{5,4},{6,7},{7,6},{8,9},{9,8},{10,11... | collective-permute-start | bytes 786440 | tf_op jit(solution)/shard_map/ppermute | solution.py:483
  37.6 12.2 %collective-permute-start.6 = (bf16[256,1664]{1,0:T(8,128)(2,1)S(1)}, bf16[256,1664]{1,0:T(8,128)(2,1)S(1)}, u32[]{:S(2)}, u32[]{:S(2)}) collective-permute-start(bf16[256,1664]{1,0:T(8,128)(2,1)S(1)} %get-tuple-element.94), channel_id=1, source_target_pairs={{0,1},{1,0},{2,3},{3,2},{4,5},{5,4},{6,7},{7,6},{8,9},{9,8},{10,11... | collective-permute-start | bytes 2555912 | tf_op jit(solution)/shard_map/ppermute | solution.py:483
  37.8 10.6 %collective-permute-start.7 = (bf16[640,512]{1,0:T(8,128)(2,1)S(1)}, bf16[640,512]{1,0:T(8,128)(2,1)S(1)}, u32[]{:S(2)}, u32[]{:S(2)}) collective-permute-start(bf16[640,512]{1,0:T(8,128)(2,1)S(1)} %get-tuple-element.95), channel_id=1, source_target_pairs={{0,4},{1,3},{2,6},{3,1},{4,0},{5,7},{6,2},{7,5},{8,12},{9,11},{10,... | collective-permute-start | bytes 1966088 | tf_op jit(solution)/shard_map/ppermute | solution.py:483
  39.3 11.5 %collective-permute-start.5 = (bf16[96,1024]{1,0:T(8,128)(2,1)S(1)}, bf16[96,1024]{1,0:T(8,128)(2,1)S(1)}, u32[]{:S(2)}, u32[]{:S(2)}) collective-permute-start(bf16[96,1024]{1,0:T(8,128)(2,1)S(1)} %get-tuple-element.86.refs_1_), channel_id=1, source_target_pairs={{1,0},{2,1},{3,2},{0,3},{5,4},{6,5},{7,6},{4,7},{9,8},{10,9},{11,1... | collective-permute-start | bytes 589832 | tf_op jit(solution)/shard_map/ppermute | solution.py:604
  39.5 13.2 %collective-permute-start.9 = (bf16[256,512]{1,0:T(8,128)(2,1)S(1)}, bf16[256,512]{1,0:T(8,128)(2,1)S(1)}, u32[]{:S(2)}, u32[]{:S(2)}) collective-permute-start(bf16[256,512]{1,0:T(8,128)(2,1)S(1)} %get-tuple-element.99), channel_id=1, source_target_pairs={{0,4},{1,9},{2,6},{3,11},{4,0},{5,13},{6,2},{7,15},{8,12},{9,1},{1... | collective-permute-start | bytes 786440 | tf_op jit(solution)/shard_map/ppermute | solution.py:483
  48.5 7.1 %collective-permute-start.11 = (bf16[320,512]{1,0:T(8,128)(2,1)S(1)}, bf16[320,512]{1,0:T(8,128)(2,1)S(1)}, u32[]{:S(2)}, u32[]{:S(2)}) collective-permute-start(bf16[320,512]{1,0:T(8,128)(2,1)S(1)} %get-tuple-element.102), channel_id=1, source_target_pairs={{0,2},{1,9},{2,0},{3,11},{4,6},{5,13},{6,4},{7,15},{8,10},{9,1},{1... | collective-permute-start | bytes 983048 | tf_op jit(solution)/shard_map/ppermute | solution.py:483
  49.9 10.3 %collective-permute-start.8 = (bf16[128,1664]{1,0:T(8,128)(2,1)S(1)}, bf16[128,1664]{1,0:T(8,128)(2,1)S(1)}, u32[]{:S(2)}, u32[]{:S(2)}) collective-permute-start(bf16[128,1664]{1,0:T(8,128)(2,1)S(1)} %get-tuple-element.98), channel_id=1, source_target_pairs={{0,2},{1,5},{2,0},{3,7},{4,6},{5,1},{6,4},{7,3},{8,10},{9,13},{10,... | collective-permute-start | bytes 1277960 | tf_op jit(solution)/shard_map/ppermute | solution.py:483
  52.6 1.0 copy-start.6
  53.7 5.0 %collective-permute-start.10 = (bf16[128,512]{1,0:T(8,128)(2,1)S(1)}, bf16[128,512]{1,0:T(8,128)(2,1)S(1)}, u32[]{:S(2)}, u32[]{:S(2)}) collective-permute-start(bf16[128,512]{1,0:T(8,128)(2,1)S(1)} %get-tuple-element.101), channel_id=1, source_target_pairs={{0,8},{1,17},{2,10},{3,19},{4,12},{5,21},{6,14},{7,23},{8,0},{9,25... | collective-permute-start | bytes 393224 | tf_op jit(solution)/shard_map/ppermute | solution.py:483
  55.6 8.7 %collective-permute-start.14 = (bf16[160,512]{1,0:T(8,128)(2,1)S(1)}, bf16[160,512]{1,0:T(8,128)(2,1)S(1)}, u32[]{:S(2)}, u32[]{:S(2)}) collective-permute-start(bf16[160,512]{1,0:T(8,128)(2,1)S(1)} %get-tuple-element.106), channel_id=1, source_target_pairs={{0,8},{1,17},{2,10},{3,19},{4,12},{5,21},{6,14},{7,23},{8,0},{9,25... | collective-permute-start | bytes 491528 | tf_op jit(solution)/shard_map/ppermute | solution.py:483
  60.2 16.9 %collective-permute-start.12 = (bf16[64,1664]{1,0:T(8,128)(2,1)S(1)}, bf16[64,1664]{1,0:T(8,128)(2,1)S(1)}, u32[]{:S(2)}, u32[]{:S(2)}) collective-permute-start(bf16[64,1664]{1,0:T(8,128)(2,1)S(1)} %get-tuple-element.105), channel_id=1, source_target_pairs={{0,4},{1,9},{2,6},{3,11},{4,0},{5,13},{6,2},{7,15},{8,12},{9,1},{1... | collective-permute-start | bytes 638984 | tf_op jit(solution)/shard_map/ppermute | solution.py:483
  61.8 6.4 %collective-permute-start.13 = (bf16[128,512]{1,0:T(8,128)(2,1)S(1)}, bf16[128,512]{1,0:T(8,128)(2,1)S(1)}, u32[]{:S(2)}, u32[]{:S(2)}) collective-permute-start(bf16[128,512]{1,0:T(8,128)(2,1)S(1)} %add.6.refs_2_.refs_0_), channel_id=1, source_target_pairs={{0,16},{1,3},{2,18},{3,1},{4,20},{5,7},{6,22},{7,5},{8,24},{9,11},... | collective-permute-start | bytes 393224 | tf_op jit(solution)/shard_map/ppermute | solution.py:483
  64.4 14.1 %collective-permute-start.17 = (bf16[160,512]{1,0:T(8,128)(2,1)S(1)}, bf16[160,512]{1,0:T(8,128)(2,1)S(1)}, u32[]{:S(2)}, u32[]{:S(2)}) collective-permute-start(bf16[160,512]{1,0:T(8,128)(2,1)S(1)} %add.7.refs_2_.refs_0_), channel_id=1, source_target_pairs={{0,16},{1,5},{2,18},{3,7},{4,20},{5,1},{6,22},{7,3},{8,24},{9,13},... | collective-permute-start | bytes 491528 | tf_op jit(solution)/shard_map/ppermute | solution.py:483
  68.2 16.1 %collective-permute-start.16 = (bf16[128,512]{1,0:T(8,128)(2,1)S(1)}, bf16[128,512]{1,0:T(8,128)(2,1)S(1)}, u32[]{:S(2)}, u32[]{:S(2)}) collective-permute-start(bf16[128,512]{1,0:T(8,128)(2,1)S(1)} %add.8.refs_2_.refs_0_), channel_id=1, source_target_pairs={{0,8},{1,17},{2,10},{3,19},{4,12},{5,21},{6,14},{7,23},{8,0},{9,25... | collective-permute-start | bytes 393224 | tf_op jit(solution)/shard_map/ppermute | solution.py:483
  78.5 14.0 %collective-permute-start.19 = (bf16[160,512]{1,0:T(8,128)(2,1)S(1)}, bf16[160,512]{1,0:T(8,128)(2,1)S(1)}, u32[]{:S(2)}, u32[]{:S(2)}) collective-permute-start(bf16[160,512]{1,0:T(8,128)(2,1)S(1)} %add.9.refs_2_.refs_0_), channel_id=1, source_target_pairs={{0,8},{1,17},{2,10},{3,19},{4,12},{5,21},{6,14},{7,23},{8,0},{9,25... | collective-permute-start | bytes 491528 | tf_op jit(solution)/shard_map/ppermute | solution.py:483
  80.6 10.6 %collective-permute-start.15 = (bf16[32,1664]{1,0:T(8,128)(2,1)S(1)}, bf16[32,1664]{1,0:T(8,128)(2,1)S(1)}, u32[]{:S(2)}, u32[]{:S(2)}) collective-permute-start(bf16[32,1664]{1,0:T(8,128)(2,1)S(1)} %get-tuple-element.108), channel_id=1, source_target_pairs={{0,8},{1,17},{2,10},{3,19},{4,12},{5,21},{6,14},{7,23},{8,0},{9,25... | collective-permute-start | bytes 319496 | tf_op jit(solution)/shard_map/ppermute | solution.py:483
  84.3 14.6 %collective-permute-start.21 = (bf16[256,512]{1,0:T(8,128)(2,1)S(1)}, bf16[256,512]{1,0:T(8,128)(2,1)S(1)}, u32[]{:S(2)}, u32[]{:S(2)}) collective-permute-start(bf16[256,512]{1,0:T(8,128)(2,1)S(1)} %join.9.refs_2_.refs_0_), channel_id=1, source_target_pairs={{0,4},{1,9},{2,6},{3,11},{4,0},{5,13},{6,2},{7,15},{8,12},{9,1},{1... | collective-permute-start | bytes 786440 | tf_op jit(solution)/shard_map/ppermute | solution.py:483
  91.2 6.6 %collective-permute-start.18 = (bf16[32,1664]{1,0:T(8,128)(2,1)S(1)}, bf16[32,1664]{1,0:T(8,128)(2,1)S(1)}, u32[]{:S(2)}, u32[]{:S(2)}) collective-permute-start(bf16[32,1664]{1,0:T(8,128)(2,1)S(1)} %add.10.refs_2_.refs_0_), channel_id=1, source_target_pairs={{0,16},{1,3},{2,18},{3,1},{4,20},{5,7},{6,22},{7,5},{8,24},{9,11},... | collective-permute-start | bytes 319496 | tf_op jit(solution)/shard_map/ppermute | solution.py:483
  92.6 10.8 %collective-permute-start.23 = (bf16[320,512]{1,0:T(8,128)(2,1)S(1)}, bf16[320,512]{1,0:T(8,128)(2,1)S(1)}, u32[]{:S(2)}, u32[]{:S(2)}) collective-permute-start(bf16[320,512]{1,0:T(8,128)(2,1)S(1)} %join.10.refs_2_.refs_0_), channel_id=1, source_target_pairs={{0,2},{1,9},{2,0},{3,11},{4,6},{5,13},{6,4},{7,15},{8,10},{9,1},{1... | collective-permute-start | bytes 983048 | tf_op jit(solution)/shard_map/ppermute | solution.py:483
  97.9 4.8 %collective-permute-start.20 = (bf16[32,1664]{1,0:T(8,128)(2,1)S(1)}, bf16[32,1664]{1,0:T(8,128)(2,1)S(1)}, u32[]{:S(2)}, u32[]{:S(2)}) collective-permute-start(bf16[32,1664]{1,0:T(8,128)(2,1)S(1)} %add.11.refs_2_.refs_0_), channel_id=1, source_target_pairs={{0,8},{1,17},{2,10},{3,19},{4,12},{5,21},{6,14},{7,23},{8,0},{9,25... | collective-permute-start | bytes 319496 | tf_op jit(solution)/shard_map/ppermute | solution.py:483
  102.7 6.0 %collective-permute-start.22 = (bf16[64,1664]{1,0:T(8,128)(2,1)S(1)}, bf16[64,1664]{1,0:T(8,128)(2,1)S(1)}, u32[]{:S(2)}, u32[]{:S(2)}) collective-permute-start(bf16[64,1664]{1,0:T(8,128)(2,1)S(1)} %join.12.refs_2_.refs_0_), channel_id=1, source_target_pairs={{0,4},{1,9},{2,6},{3,11},{4,0},{5,13},{6,2},{7,15},{8,12},{9,1},{1... | collective-permute-start | bytes 638984 | tf_op jit(solution)/shard_map/ppermute | solution.py:483
  103.4 15.3 %collective-permute-start.27 = (bf16[640,512]{1,0:T(8,128)(2,1)S(1)}, bf16[640,512]{1,0:T(8,128)(2,1)S(1)}, u32[]{:S(2)}, u32[]{:S(2)}) collective-permute-start(bf16[640,512]{1,0:T(8,128)(2,1)S(1)} %join.13.refs_2_.refs_0_), channel_id=1, source_target_pairs={{0,4},{1,3},{2,6},{3,1},{4,0},{5,7},{6,2},{7,5},{8,12},{9,11},{10,... | collective-permute-start | bytes 1966088 | tf_op jit(solution)/shard_map/ppermute | solution.py:483
  104.9 9.2 %collective-permute-start.25 = (bf16[512,512]{1,0:T(8,128)(2,1)S(1)}, bf16[512,512]{1,0:T(8,128)(2,1)S(1)}, u32[]{:S(2)}, u32[]{:S(2)}) collective-permute-start(bf16[512,512]{1,0:T(8,128)(2,1)S(1)} %join.11.refs_2_.refs_0_), channel_id=1, source_target_pairs={{0,2},{1,5},{2,0},{3,7},{4,6},{5,1},{6,4},{7,3},{8,10},{9,13},{10,... | collective-permute-start | bytes 1572872 | tf_op jit(solution)/shard_map/ppermute | solution.py:483
  108.7 9.9 %collective-permute-start.24 = (bf16[128,1664]{1,0:T(8,128)(2,1)S(1)}, bf16[128,1664]{1,0:T(8,128)(2,1)S(1)}, u32[]{:S(2)}, u32[]{:S(2)}) collective-permute-start(bf16[128,1664]{1,0:T(8,128)(2,1)S(1)} %join.14.refs_2_.refs_0_), channel_id=1, source_target_pairs={{0,2},{1,5},{2,0},{3,7},{4,6},{5,1},{6,4},{7,3},{8,10},{9,13},{10,... | collective-permute-start | bytes 1277960 | tf_op jit(solution)/shard_map/ppermute | solution.py:483
  118.8 10.4 %collective-permute-start.28 = (bf16[1280,512]{1,0:T(8,128)(2,1)S(1)}, bf16[1280,512]{1,0:T(8,128)(2,1)S(1)}, u32[]{:S(2)}, u32[]{:S(2)}) collective-permute-start(bf16[1280,512]{1,0:T(8,128)(2,1)S(1)} %join.17.refs_0_), channel_id=1, source_target_pairs={{0,1},{1,0},{2,3},{3,2},{4,5},{5,4},{6,7},{7,6},{8,9},{9,8},{10,11... | collective-permute-start | bytes 3932168 | tf_op jit(solution)/shard_map/ppermute | solution.py:483
  118.9 8.1 %collective-permute-start.29 = (bf16[1024,512]{1,0:T(8,128)(2,1)S(1)}, bf16[1024,512]{1,0:T(8,128)(2,1)S(1)}, u32[]{:S(2)}, u32[]{:S(2)}) collective-permute-start(bf16[1024,512]{1,0:T(8,128)(2,1)S(1)} %join.15.refs_2_.refs_0_), channel_id=1, source_target_pairs={{0,1},{1,0},{2,3},{3,2},{4,5},{5,4},{6,7},{7,6},{8,9},{9,8},{10,11... | collective-permute-start | bytes 3145736 | tf_op jit(solution)/shard_map/ppermute | solution.py:483
  119.4 5.2 %collective-permute-start.26 = (bf16[256,1664]{1,0:T(8,128)(2,1)S(1)}, bf16[256,1664]{1,0:T(8,128)(2,1)S(1)}, u32[]{:S(2)}, u32[]{:S(2)}) collective-permute-start(bf16[256,1664]{1,0:T(8,128)(2,1)S(1)} %join.16.refs_0_.refs_2_), channel_id=1, source_target_pairs={{0,1},{1,0},{2,3},{3,2},{4,5},{5,4},{6,7},{7,6},{8,9},{9,8},{10,11... | collective-permute-start | bytes 2555912 | tf_op jit(solution)/shard_map/ppermute | solution.py:483

commit v3 on v2

v3 whole, which is shorter than its diff:
```python
from functools import partial
import math

import jax
import jax.numpy as jnp
from jax import lax
from jax.experimental import pallas as pl
from jax.experimental.pallas import tpu as pltpu
from jax.sharding import PartitionSpec as P

HEADS = 8
BLOCK = 16
LEVELS = 6
CHUNK = 32
KEYS = 128
f32 = jnp.float32
bf16 = jnp.bfloat16


def nn(a, b):
    return lax.dot_general(a, b, (((1,), (0,)), ((), ())), preferred_element_type=f32)


def nt(a, b):
    return lax.dot_general(a, b, (((1,), (1,)), ((), ())), preferred_element_type=f32)


def tn(a, b):
    return lax.dot_general(a, b, (((0,), (0,)), ((), ())), preferred_element_type=f32)


def call(kernel, outs, *args, scratch=(), smem=(), far=(), far_out=(), deps=(), alias=None, name=None, us=0.5, limit=8):
    def spec(at, apart):
        return pl.BlockSpec(memory_space=pltpu.HBM if at in apart else pltpu.VMEM)

    specs = [
        pl.BlockSpec(memory_space=pltpu.SMEM) if i in smem else spec(i, far) for i in range(len(args))
    ]
    specs += [pl.BlockSpec(memory_space=pl.ANY)] * len(deps)
    count = len(args)
    us = COSTS.get(name, us)

    def run(*refs):
        kernel(*refs[:count], *refs[count + len(deps) :])

    return pl.pallas_call(
        run,
        out_shape=[jax.ShapeDtypeStruct(s, d) for s, d in outs],
        in_specs=specs,
        out_specs=[spec(i, far_out) for i in range(len(outs))],
        scratch_shapes=scratch,
        input_output_aliases=alias or {},
        compiler_params=pltpu.CompilerParams(vmem_limit_bytes=limit * 2**20),
        cost_estimate=pl.CostEstimate(
            flops=int(us * 1.15e9), bytes_accessed=2**16, transcendentals=0
        ),
        name=name,
    )(*args, *deps)


def level_start(span, level):
    return span - (span >> (level - 1)) if level else 0


def unit(values):
    centred = values - jnp.mean(values, axis=-1, keepdims=True)
    inv = lax.rsqrt(jnp.mean(centred * centred, axis=-1, keepdims=True) + 1e-05)
    return centred * inv, inv


def unit_back(grad, hat, inv):
    along = jnp.mean(grad * hat, axis=-1, keepdims=True)
    return inv * (grad - jnp.mean(grad, axis=-1, keepdims=True) - hat * along)


def pool_matrix(span):
    parts = []
    for level in range(1, LEVELS):
        rows = span >> level
        row = lax.broadcasted_iota(jnp.int32, (rows, span), 0)
        col = lax.broadcasted_iota(jnp.int32, (rows, span), 1)
        parts.append(jnp.where((col >> level) == row, 1.0 / 2**level, 0.0))
    return jnp.concatenate(parts, axis=0).astype(bf16)


def edge_matrix(span):
    parts = []
    row = lax.broadcasted_iota(jnp.int32, (BLOCK, span), 0)
    col = lax.broadcasted_iota(jnp.int32, (BLOCK, span), 1)
    for level in range(LEVELS):
        group = (span >> level) - BLOCK + row
        parts.append(jnp.where((col >> level) == group, 1.0 / 2**level, 0.0))
    return jnp.concatenate(parts, axis=0).astype(bf16)


def standardize(tokens, hat):
    hat[...] = unit(tokens[...].astype(f32))[0]


def project(hat, gain, bias, w_qkv, normed, kv, coarse, edge):
    span, width = hat.shape
    rows = (hat[...] * gain[...].astype(f32)[None] + bias[...].astype(f32)[None]).astype(bf16)
    normed[...] = rows
    both = nn(rows, w_qkv[:, width:]).astype(bf16)
    kv[...] = both
    pooled = nn(pool_matrix(span), both).astype(bf16)
    coarse[...] = pooled
    edge[0:BLOCK] = both[span - BLOCK :]
    for level in range(1, LEVELS):
        end = level_start(span, level + 1)
        edge[BLOCK * level : BLOCK * (level + 1)] = pooled[end - BLOCK : end]


def project_q(normed, w_qkv, queries):
    span, width = normed.shape
    q = nn(normed[...], w_qkv[:, :width]).astype(bf16).astype(f32)
    queries[...] = (q * (1.0 / math.sqrt(width // HEADS))).astype(bf16)


def hidden_back(prefix, cotangent, w_down, d_ffn, d_hidden):
    span, width = cotangent.shape
    position = lax.axis_index("seq") * span + lax.broadcasted_iota(jnp.int32, (span, width), 0)
    masked = jnp.where(position >= prefix[0], cotangent[...].astype(f32), 0.0).astype(bf16)
    d_ffn[...] = masked
    d_hidden[...] = nt(masked, w_down[...])


def window_bias(chunk, first):
    row = lax.broadcasted_iota(jnp.int32, (CHUNK, KEYS), 0)
    col = lax.broadcasted_iota(jnp.int32, (CHUNK, KEYS), 1)
    late = row >= BLOCK
    low = jnp.where(late, BLOCK, 0)
    edge = 3 * BLOCK
    ok = (col >= low) & (col <= BLOCK + row)
    if chunk == 0:
        ok = ok & ((col >= BLOCK) | jnp.logical_not(first))
    bias = jnp.where(ok & (col < edge), 0.0, -1e30)
    for level in range(1, LEVELS):
        start = edge + BLOCK * (level - 1)
        inside = (col >= start) & (col < start + BLOCK)
        half = inside & (col < start + BLOCK // 2)
        if level == 1:
            ok = half | (inside & late)
        else:
            ok = inside if (chunk >> (level - 2)) & 1 else half
        if chunk >> (level - 1) == 0:
            ok = ok & jnp.logical_not(first)
        bias = jnp.where(ok, math.log(2**level), bias)
    return bias


def window_rows(kv, coarse, recv, chunk, low, high, span):
    start = CHUNK * chunk
    if chunk == 0:
        parts = [recv[0:BLOCK, low:high], kv[0:CHUNK, low:high]]
    else:
        parts = [kv[start - BLOCK : start + CHUNK, low:high]]
    for level in range(1, LEVELS):
        block = chunk >> (level - 1)
        if block == 0:
            parts.append(recv[BLOCK * level : BLOCK * (level + 1), low:high])
        else:
            base = level_start(span, level) + BLOCK * (block - 1)
            parts.append(coarse[base : base + BLOCK, low:high])
    return jnp.concatenate(parts, axis=0)


def by_head(rows):
    lane = lax.broadcasted_iota(jnp.int32, (CHUNK, 128), 1)
    zero = jnp.zeros((CHUNK, 128), bf16)
    pairs = []
    for pair in range(HEADS // 2):
        part = rows[:, 128 * pair : 128 * (pair + 1)]
        pairs.append(
            jnp.concatenate(
                [jnp.where(lane < 64, part, zero), jnp.where(lane >= 64, part, zero)], axis=0
            )
        )
    return pairs


def from_heads(pairs):
    lane = lax.broadcasted_iota(jnp.int32, (CHUNK, 128), 1)
    return jnp.concatenate([jnp.where(lane < 64, p[:CHUNK], p[CHUNK:]) for p in pairs], axis=1)


SIDE = 8
PIECES = 1


def attend(queries, kv, coarse, recv, hat, attended, probs, edge_hat):
    span, width = queries.shape
    edge_hat[...] = nn(edge_matrix(span), hat[...].astype(bf16)).astype(bf16)
    first = lax.axis_index("seq") == 0
    rows = CHUNK * HEADS
    for base in range(0, span // CHUNK, SIDE):
        group = range(base, base + SIDE)
        scores = []
        for chunk in group:
            bias = window_bias(chunk, first)
            keys = window_rows(kv, coarse, recv, chunk, 0, width, span)
            split = by_head(queries[CHUNK * chunk : CHUNK * (chunk + 1)])
            raw = [nt(s, keys[:, 128 * p : 128 * (p + 1)]) for p, s in enumerate(split)]
            scores.append(jnp.concatenate(raw, axis=0) + jnp.concatenate([bias] * HEADS, axis=0))
        tops = [jnp.max(s, axis=-1, keepdims=True) for s in scores]
        expos = [jnp.exp(s - t) for s, t in zip(scores, tops)]
        sums = [jnp.sum(e, axis=-1, keepdims=True) for e in expos]
        lows = [(e * (1.0 / t)).astype(bf16) for e, t in zip(expos, sums)]
        for chunk, low in zip(group, lows):
            probs[rows * chunk : rows * (chunk + 1)] = low
            vals = window_rows(kv, coarse, recv, chunk, width, 2 * width, span)
            mixed = [
                nn(low[64 * p : 64 * (p + 1)], vals[:, 128 * p : 128 * (p + 1)])
                for p in range(HEADS // 2)
            ]
            attended[CHUNK * chunk : CHUNK * (chunk + 1)] = from_heads(mixed).astype(bf16)


def core_index():
    return (lax.axis_index("batch") * lax.axis_size("seq") + lax.axis_index("seq")) & 1


def halves(whole, keeps, sends):
    core = core_index()
    rows = keeps[0].shape[0]
    for refs, half in ((keeps, core), (sends, 1 - core)):
        base = half * (rows * len(refs))
        for i, ref in enumerate(refs):
            ref[...] = whole[pl.ds(pl.multiple_of(base + rows * i, BLOCK), rows)]


def feed_forward(
    attended, tokens, w_out, gain, bias, w_up, d_hidden, d_ffn, mid, normed, hidden, d_up, keep, send, whole
):
    span, width = tokens.shape
    ff = w_up.shape[1]
    middle = tokens[...].astype(f32) + nn(attended[...], w_out[...])
    mid[...] = middle
    hat, _ = unit(middle)
    rows = (hat * gain[...].astype(f32)[None] + bias[...].astype(f32)[None]).astype(bf16)
    normed[...] = rows
    c0 = math.sqrt(2.0 / math.pi)
    tile = 256
    for start in range(0, ff, tile):
        cols = slice(start, start + tile)
        x = nn(rows, w_up[:, cols])
        square = x * x
        half = 0.5 + 0.5 * jnp.tanh(x * (c0 + (c0 * 0.044715) * square))
        act = (x * half).astype(bf16)
        slope = half + 2.0 * half * (1.0 - half) * x * (c0 + (3 * c0 * 0.044715) * square)
        hidden[:, cols] = act
        d_up[:, cols] = (slope * d_hidden[:, cols]).astype(bf16)
        whole[cols] = tn(act, d_ffn[...]).astype(bf16)
    halves(whole, [keep], [send])


def up_back(normed, d_up, keep, send, whole):
    width = normed.shape[1]
    for part in range(d_up.shape[1] // width):
        cols = slice(width * part, width * (part + 1))
        whole[cols] = tn(normed[...], d_up[:, cols]).astype(bf16)
    halves(whole, [keep], [send])


def output(mid, hidden, w_down, out, token):
    out[...] = (mid[...] + nn(hidden[...], w_down[...])).astype(bf16)
    token[...] = jnp.zeros_like(token)


def mid_back(
    mid, d_up, w_up, gain, d_ffn, attended, w_out, d_mid, d_attended, grad_out, grad_norm
):
    middle = mid[...]
    d_normed = nt(d_up[...], w_up[...])
    hat, inv = unit(middle)
    grad_norm[0:1] = jnp.sum(d_normed * hat, axis=0, keepdims=True)
    grad_norm[1:2] = jnp.sum(d_normed, axis=0, keepdims=True)
    d_middle = d_ffn[...].astype(f32) + unit_back(d_normed * gain[...].astype(f32)[None], hat, inv)
    d_mid[...] = d_middle
    d_branch = d_middle.astype(bf16)
    grad_out[...] = tn(attended[...], d_branch).astype(bf16)
    d_attended[...] = nt(d_branch, w_out[...]).astype(bf16)


def attend_back(queries, kv, coarse, recv, probs, d_attended, d_proj, lent, fine, wide):
    span, width = queries.shape
    rows = CHUNK * HEADS
    scale = 1.0 / math.sqrt(width // HEADS)
    fine[0:BLOCK] = jnp.zeros((BLOCK, 2 * width), f32)
    zero = jnp.zeros((2 * CHUNK, 128), bf16)

    def widened(split, quad):
        return jnp.concatenate(
            [
                jnp.concatenate([split[2 * quad], zero], axis=1),
                jnp.concatenate([zero, split[2 * quad + 1]], axis=1),
            ],
            axis=0,
        )

    for base in range(0, span // CHUNK, SIDE):
        group = range(base, base + SIDE)
        softs, d_probs, splits_a = [], [], []
        for chunk in group:
            vals = window_rows(kv, coarse, recv, chunk, width, 2 * width, span)
            split = by_head(d_attended[CHUNK * chunk : CHUNK * (chunk + 1)])
            splits_a.append(split)
            softs.append(probs[rows * chunk : rows * (chunk + 1)].astype(f32))
            d_probs.append(
                jnp.concatenate(
                    [nt(s, vals[:, 128 * p : 128 * (p + 1)]) for p, s in enumerate(split)], axis=0
                )
            )
        inners = [jnp.sum(s * d, axis=-1, keepdims=True) for s, d in zip(softs, d_probs)]
        d_scores = [(s * (d - t)).astype(bf16) for s, d, t in zip(softs, d_probs, inners)]
        splits_q = []
        for chunk, d_score in zip(group, d_scores):
            start = CHUNK * chunk
            keys = window_rows(kv, coarse, recv, chunk, 0, width, span)
            mixed = [
                nn(d_score[64 * p : 64 * (p + 1)], keys[:, 128 * p : 128 * (p + 1)])
                for p in range(HEADS // 2)
            ]
            d_proj[start : start + CHUNK, :width] = (from_heads(mixed) * scale).astype(bf16)
            splits_q.append(by_head(queries[start : start + CHUNK]))
        for part in range(2):
            for quad in range(HEADS // 4):
                cols = slice(width * part + 256 * quad, width * part + 256 * (quad + 1))
                grads = []
                for chunk, d_score, split_a in zip(group, d_scores, splits_a):
                    if part:
                        left, split = probs[rows * chunk : rows * (chunk + 1)], split_a
                    else:
                        left, split = d_score, splits_q[chunk - base]
                    grads.append(tn(left[128 * quad : 128 * (quad + 1)], widened(split, quad)))
                for i, grad in enumerate(grads):
                    start = CHUNK * (base + i)
                    if i:
                        head = grad[:BLOCK] + grads[i - 1][2 * BLOCK : 3 * BLOCK]
                        fine[start : start + BLOCK, cols] = head
                    else:
                        fine[start : start + BLOCK, cols] += grad[:BLOCK]
                    fine[start + BLOCK : start + 2 * BLOCK, cols] = grad[BLOCK : 2 * BLOCK]
                end = CHUNK * (base + SIDE)
                fine[end : end + BLOCK, cols] = grads[-1][2 * BLOCK : 3 * BLOCK]
                for level in range(1, LEVELS):
                    own = BLOCK * (level + 2)
                    sums = {}
                    for i, grad in enumerate(grads):
                        block = (base + i) >> (level - 1)
                        piece = grad[own : own + BLOCK]
                        sums[block] = sums[block] + piece if block in sums else piece
                    for block, total in sums.items():
                        at = level_start(span, level) + BLOCK * block
                        if base > block << (level - 1):
                            wide[at : at + BLOCK, cols] += total
                        else:
                            wide[at : at + BLOCK, cols] = total

    zero = jnp.zeros((BLOCK, 2 * width), bf16)
    lent[0:BLOCK] = fine[0:BLOCK].astype(bf16)
    parts = []
    for level in range(1, LEVELS):
        at, end = level_start(span, level), level_start(span, level + 1)
        lent[BLOCK * level : BLOCK * (level + 1)] = wide[at : at + BLOCK].astype(bf16)
        if at + BLOCK < end:
            parts.append(wide[at + BLOCK : end].astype(bf16))
        parts.append(zero)
    spread = tn(pool_matrix(span), jnp.concatenate(parts, axis=0))
    d_proj[:, width:] = (fine[BLOCK:] + spread).astype(bf16)


def project_back(
    d_proj, lent, edge_hat, normed, w_qkv, tokens, grad_norm, grad_out, gain, bias, d_normed, edge_back, *refs
):
    span, width = tokens.shape
    keeps, sends, whole = refs[:PIECES], refs[PIECES:-1], refs[-1]
    grads, away = d_proj[...], lent[...]
    gains, shifts = gain[...].astype(f32)[None], bias[...].astype(f32)[None]
    edge = edge_hat[...].astype(f32)
    edge_normed = (edge * gains + shifts).astype(bf16)
    whole[:, :width] = tn(normed[...], grads[:, :width]).astype(bf16)
    whole[:, width : 3 * width] = (
        tn(normed[...], grads[:, width:]) + tn(edge_normed, away)
    ).astype(bf16)
    whole[:, 3 * width : 4 * width] = grad_out[...]
    d_rows = nt(grads, w_qkv[...])
    d_normed[...] = d_rows
    d_edge = nt(away, w_qkv[:, width:])
    edge_back[...] = d_edge.astype(bf16)
    hat, _ = unit(tokens[...].astype(f32))
    small = [
        jnp.sum(d_rows * hat, axis=0, keepdims=True) + jnp.sum(d_edge * edge, axis=0, keepdims=True),
        jnp.sum(d_rows, axis=0, keepdims=True) + jnp.sum(d_edge, axis=0, keepdims=True),
        grad_norm[0:2],
        jnp.zeros((124, width), f32),
    ]
    whole[:, 4 * width :] = jnp.concatenate(small, axis=0).T.astype(bf16)
    halves(whole, keeps, sends)


def spacer(token):
    token[...] = jnp.zeros_like(token)


def tokens_back(d_normed, back, tokens, gain, d_mid, d_tokens, token):
    token[...] = jnp.zeros_like(token)
    span, width = tokens.shape
    grad = d_normed[...] + tn(edge_matrix(span), back[...])
    hat, inv = unit(tokens[...].astype(f32))
    d_tokens[...] = (
        d_mid[...] + unit_back(grad * gain[...].astype(f32)[None], hat, inv)
    ).astype(bf16)


def half_of(step, rows):
    index = lax.axis_index("batch") * lax.axis_size("seq") + lax.axis_index("seq")
    bit = jnp.where((index & 1) == 1, index >> step[1], index >> step[0]) & 1
    here, away = bit * rows, (1 - bit) * rows
    return pl.ds(pl.multiple_of(here, BLOCK), rows), pl.ds(pl.multiple_of(away, BLOCK), rows)


def add(own, other, total):
    total[...] = own[...] + other[...]


def join(step, own, other, both):
    here, away = half_of(step, own.shape[0])
    both[here] = own[...]
    both[away] = other[...]


def write_down(half, mine, *refs):
    out, token, tile, sems = refs[half:]
    rows, size = mine.shape[0], tile.shape[1]
    base = (core_index() ^ half) * rows
    copies = []
    for slot in range(rows // size):
        tile[slot] = mine[size * slot : size * (slot + 1)].astype(f32)
        at = pl.ds(pl.multiple_of(base + size * slot, size), size)
        copies.append(pltpu.make_async_copy(tile.at[slot], out.at[at], sems.at[slot]))
        copies[-1].start()
    token[...] = jnp.zeros_like(token)
    for copy in copies:
        copy.wait()


def write_up(half, mine, *refs):
    out, token, tile, sems = refs[half:]
    width, ff = out.shape
    across, size = ff // width // 2, tile.shape[1]
    base = (core_index() ^ half) * across
    copies = []
    for slot in range(across * width // size):
        part, row = divmod(size * slot, width)
        tile[slot] = mine[size * slot : size * (slot + 1)].astype(f32)
        cols = pl.ds(pl.multiple_of((base + part) * width, width), width)
        copies.append(
            pltpu.make_async_copy(tile.at[slot], out.at[row : row + size, cols], sems.at[slot])
        )
        copies[-1].start()
    token[...] = jnp.zeros_like(token)
    for copy in copies:
        copy.wait()


def write_rest(half, mine, *refs):
    rows = mine.shape[0]
    if half:
        own, refs = refs[0], refs[3:]
        g_qkv, g_out, gain1, bias1, gain2, bias2, token, qkv, out, sems = refs
    else:
        g_qkv, g_out, token, qkv, out, sems = refs
    width = g_out.shape[1]
    size = qkv.shape[1]
    base = (core_index() ^ half) * rows
    copies = []
    for slot in range(rows // size):
        here = slice(size * slot, size * (slot + 1))
        at = pl.ds(pl.multiple_of(base + size * slot, size), size)
        qkv[slot] = mine[here, : 3 * width].astype(f32)
        out[slot] = mine[here, 3 * width : 4 * width].astype(f32)
        for i, (src, dst) in enumerate(((qkv, g_qkv), (out, g_out))):
            copies.append(pltpu.make_async_copy(src.at[slot], dst.at[at], sems.at[2 * slot + i]))
            copies[-1].start()
    token[...] = jnp.zeros_like(token)
    if half:
        ours, theirs = own[:, 4 * width :].astype(f32), mine[:, 4 * width :].astype(f32)
        low = core_index() == 0
        small = jnp.concatenate(
            [jnp.where(low, ours, theirs), jnp.where(low, theirs, ours)], axis=0
        ).T
        for i, ref in enumerate((gain1, bias1, gain2, bias2)):
            ref[...] = small[i]
    for copy in copies:
        copy.wait()


def flips(size, even, odd):
    return [(i, i ^ (1 << (odd if i & 1 else even))) for i in range(size)]


def add_split(step, *refs):
    parts = (len(refs) - 2) // 2
    keep, send = refs[2 * parts :]
    at = 0
    for own, other in zip(refs[:parts], refs[parts : 2 * parts]):
        rows = own.shape[0] // 2
        here, away = half_of(step, rows)
        send[at : at + rows] = own[away] + other[away]
        keep[at : at + rows] = own[here] + other[here]
        at += rows


class Sum:
    def __init__(self, keep, send, orders, size):
        self.own, self.away = keep, send
        self.size = size
        steps = [(0, 0)] + list(zip(*orders))
        rows = sum(v.shape[0] for v in keep)
        self.phases = [("halve", steps[0])]
        for step in steps[1:]:
            if step == steps[-1] or rows < 2 * BLOCK:
                self.phases.append(("whole", step))
            else:
                self.phases.append(("halve", step))
                rows //= 2
        self.phases += [("join", step) for kind, step in reversed(self.phases) if kind == "halve"]
        self.at = 0

    def start(self):
        kind, step = self.phases[self.at]
        value = self.away if kind == "halve" else self.own
        pairs = flips(self.size, *step)
        self.other = [lax.ppermute(v, ("batch", "seq"), pairs) for v in value]

    def turn(self, *deps):
        result = self.done(*deps)
        if self.at < len(self.phases):
            self.start()
        return result

    def left(self):
        return len(self.phases) - self.at

    def done(self, *deps):
        own, other = self.own, self.other
        rows, cols = sum(v.shape[0] for v in own), own[0].shape[1]
        kind, step = self.phases[self.at]
        self.at += 1
        if kind == "join":
            if not self.left():
                return other[0]
            self.own = call(
                partial(join, step), [((2 * rows, cols), bf16)], *own, *other,
                deps=deps, name="join",
            )
        elif self.phases[self.at][0] == "halve":
            half = ((rows // 2, cols), bf16)
            keep, send = call(
                partial(add_split, self.phases[self.at][1]), [half, half], *own, *other,
                deps=deps, name="add_split",
            )
            self.own, self.away = [keep], [send]
        else:
            self.own = call(add, [((rows, cols), bf16)], *own, *other, deps=deps, name="add")
        return self.own[0]


COSTS = {"add_split": 6, "add": 6, "join": 6, "spacer": 10, "mid_back": 0.5, "attend_back": 20, "feed_forward": 1, "project_back": 2, "tokens_back": 20}
PLAN = "ff up - - sD sU D mid U ab pb sR D U R D U U D U R D R D R U D U R D - R U D tb R U ob R R"
ORDERS = {"D": ["xyz", "yxz"], "U": ["xzy", "yxz"], "R": ["xyz", "yxz"]}


def chain_bits(names, size, seq_size):
    seq_bits = seq_size.bit_length() - 1
    last = size.bit_length() - 1
    groups = {
        "y": list(range(1, seq_bits)),
        "x": list(range(seq_bits, min(seq_bits + 1, last))),
        "z": list(range(seq_bits + 1, last)),
        "Z": list(range(seq_bits + 1, last))[::-1],
    }
    return [bit for name in names for bit in groups[name]]


def body(
    tokens, prefix, cotangent, gain1, bias1, w_qkv, w_out, gain2, bias2, w_up, w_down
):
    row_count, span, width = tokens.shape
    ff = w_up.shape[1]
    seq_size, batch_size = lax.axis_size("seq"), lax.axis_size("batch")
    size = seq_size * batch_size
    tokens = tokens.reshape(span, width)
    cotangent = cotangent.reshape(span, width)
    edge_rows = BLOCK * LEVELS
    coarse_rows = level_start(span, LEVELS)
    dma = pltpu.SemaphoreType.DMA
    flat, flat32 = ((span, width), bf16), ((span, width), f32)
    pair = ((span, 2 * width), bf16)
    pooled = ((coarse_rows, 2 * width), bf16)
    edges = ((edge_rows, 2 * width), bf16)
    line = ((width,), f32)
    mark = ((8, 128), f32)

    def tiles(count, rows, cols):
        return pltpu.VMEM((count, rows, cols), f32)

    (hat1,) = call(standardize, [flat32], tokens, name="standardize", us=3)
    normed1, kv, coarse, edge = call(
        project, [flat, pair, pooled, edges], hat1, gain1, bias1, w_qkv, name="project", us=3,
    )
    onward = [(i, (i + 1) % seq_size) for i in range(seq_size)]
    recv = lax.ppermute(edge, "seq", onward)
    (queries,) = call(project_q, [flat], normed1, w_qkv, name="project_q", us=0.1)
    d_ffn, d_hidden = call(
        hidden_back, [flat, ((span, ff), f32)], prefix, cotangent, w_down,
        smem=(0,), deps=(queries,), name="hidden_back", us=0.2,
    )
    attended, probs, edge_hat = call(
        attend,
        [flat, ((span * HEADS, KEYS), bf16), ((edge_rows, width), bf16)],
        queries, kv, coarse, recv, hat1, deps=(d_ffn,), name="attend",
    )
    recv_hat = lax.ppermute(edge_hat, "seq", onward)

    sums, ends, state = {}, {}, {}

    def run_ff(step):
        half = ((ff // 2, width), bf16)
        mid, normed2, hidden, d_up, keep, send = call(
            feed_forward,
            [flat32, flat, ((span, ff), bf16), ((span, ff), bf16), half, half],
            attended, tokens, w_out, gain2, bias2, w_up, d_hidden, d_ffn,
            scratch=[pltpu.VMEM((ff, width), bf16)], name="feed_forward",
        )
        state.update(mid=mid, normed2=normed2, hidden=hidden, d_up=d_up)
        state["D"] = [keep], [send]
        return send

    def run_up(step):
        half = ((ff // 2, width), bf16)
        keep, send = call(
            up_back, [half, half], state["normed2"], state["d_up"],
            deps=(step, recv_hat), scratch=[pltpu.VMEM((ff, width), bf16)], name="up_back",
        )
        state["U"] = [keep], [send]
        return send

    def run_mid(step):
        square = ((width, width), bf16)
        d_mid, d_attended, grad_out, grad_norm = call(
            mid_back,
            [flat32, flat, square, ((8, width), f32)],
            state["mid"], state["d_up"], w_up, gain2, d_ffn, attended, w_out,
            deps=(step,), name="mid_back",
        )
        state.update(d_mid=d_mid, d_attended=d_attended, grad_out=grad_out, grad_norm=grad_norm)
        return d_attended

    def run_ab(step):
        state["d_proj"], lent = call(
            attend_back,
            [((span, 3 * width), bf16), edges],
            queries, kv, coarse, recv, probs, state["d_attended"],
            deps=(step,),
            scratch=[pltpu.VMEM((span + BLOCK, 2 * width), f32), pltpu.VMEM((coarse_rows, 2 * width), f32)],
            name="attend_back", limit=16,
        )
        state["lent"] = lent
        return lent

    def run_pb(step):
        piece = ((width // 2 // PIECES, 4 * width + 128), bf16)
        state["d_normed"], edge_back, *halved = call(
            project_back,
            [flat32, ((edge_rows, width), bf16)] + [piece] * (2 * PIECES),
            state["d_proj"], state["lent"], recv_hat, normed1, w_qkv, tokens, state["grad_norm"], state["grad_out"], gain1, bias1,
            deps=(step,), scratch=[pltpu.VMEM((width, 4 * width + 128), bf16)], name="project_back",
        )
        state["R"] = halved[:PIECES], halved[PIECES:]
        state["back"] = lax.ppermute(edge_back, "seq", [(b, a) for a, b in onward])
        return halved[-1]

    def run_ob(step):
        state["result"], token = call(
            output, [flat, mark], state["mid"], state["hidden"], w_down, deps=(step,), name="output",
        )
        return token

    def run_tb(step):
        state["d_tokens"], token = call(
            tokens_back, [flat, mark], state["d_normed"], state["back"], tokens, gain1, state["d_mid"],
            deps=(step,), name="tokens_back",
        )
        return token

    def finish(key, half, mine, step):
        rows = mine.shape[0]
        if key == "R":
            outs = [((width, 3 * width), f32), ((width, width), f32)]
            size = rows // 4
            scratch = [tiles(4, size, 3 * width), tiles(4, size, width), dma((8,))]
            kernel, small = write_rest, [line] * 4
        else:
            outs = [((ff, width) if key == "D" else (width, ff), f32)]
            scratch = [tiles(4, rows // 4, width), dma((4,))]
            kernel, small = (write_down if key == "D" else write_up), []
        name = {"D": "finish_down", "U": "finish_up", "R": "finish_rest"}[key]
        far_out = tuple(range(len(outs)))
        if half == 0:
            *ends[key], token = call(
                partial(kernel, 0), outs + [mark], mine, far_out=far_out, deps=(step,), scratch=scratch,
                name=name, limit=12,
            )
            return token
        first = list(sums[key].own) if small else []
        before = ends[key]
        at = 1 + len(first)
        *ends[key], token = call(
            partial(kernel, 1), outs + small + [mark], mine, *first, *before,
            far=tuple(range(at, at + len(before))), far_out=far_out, scratch=scratch,
            alias={at + i: i for i in range(len(before))}, name=name, limit=12,
        )
        return token

    kernels = dict(ff=run_ff, up=run_up, mid=run_mid, ab=run_ab, pb=run_pb, ob=run_ob, tb=run_tb)
    def turn(key, step):
        step = sums[key].turn(step)
        if sums[key].left() <= 1:
            step = finish(key, 1 - sums[key].left(), step, step)
        return step

    step = None
    for token in PLAN.split():
        if token == "-":
            (step,) = call(spacer, [mark], deps=(step,), name="spacer", us=100)
        elif token in kernels:
            step = kernels[token](step)
        elif token[0] == "s":
            orders = [chain_bits(names, size, seq_size) for names in ORDERS[token[1]]]
            sums[token[1]] = Sum(*state[token[1]], orders, size)
            sums[token[1]].start()
        else:
            step = turn(token, step)
    while any(one.left() for one in sums.values()):
        for key, one in sums.items():
            if one.left():
                step = turn(key, step)
    (grad_down,) = ends["D"]
    (grad_up,) = ends["U"]
    grad_qkv, grad_out, g_gain1, g_bias1, g_gain2, g_bias2 = ends["R"]
    shape = (row_count, span, width)
    return (
        state["result"].reshape(shape), state["d_tokens"].reshape(shape), g_gain1, g_bias1, grad_qkv,
        grad_out, g_gain2, g_bias2, grad_up, grad_down,
    )


def solution(mesh):
    placed = (
        P("batch", "seq", None),
        P("batch"),
        P("batch", "seq", None),
        P(),
        P(),
        P(),
        P(),
        P(),
        P(),
        P(),
        P(),
    )
    return jax.shard_map(
        body,
        mesh=mesh,
        in_specs=placed,
        out_specs=(
            P("batch", "seq", None),
            P("batch", "seq", None),
            P(),
            P(),
            P(),
            P(),
            P(),
            P(),
            P(),
            P(),
        ),
        check_vma=False,
    )
```

time: 132 us -> 112 us (0.85)
  waiting for transfers between devices: 55.5 us -> 39.2 us
  starting transfers between devices: 37.5 us -> 30.5 us
  Pallas kernels: 33.9 us -> 36.3 us
    ppermute x28 -> x27, waiting for transfers between devices: 51.2 us -> 36.5 us  [start(): self.other = [lax.ppermute(v, ('batch', 'seq'), pairs) for v in value]]
    ppermute x28 -> x27, starting transfers between devices: 36.7 us -> 29.7 us  [start(): self.other = [lax.ppermute(v, ('batch', 'seq'), pairs) for v in value]]
    pallas_call x37 -> x45, Pallas kernels: 33.9 us -> 36.3 us  [call(): pl.pallas_call(run, out_shape=[jax.ShapeDtypeStruct(s, d) for s, d in out...]
    ppermute x1, waiting for transfers between devices: 4.32 us -> 2.63 us  [body(): recv = lax.ppermute(edge, 'seq', onward)]
  transfers between devices with their start and end apart: 30 -> 30, of which waited for: 17 -> 17; matrix products, arithmetic and copies ran while one was open for 0% -> 0% of each run, Pallas kernels for 14% -> 27%
where the time goes in v3:
time: 112 us; the launch traced here: 111 us
  waiting for transfers between devices  39.2 us (35%)
  Pallas kernels  36.3 us (32%)
  starting transfers between devices  30.5 us (27%)
  local copies, waits for them, and re-layouts  3.11 us (3%)
  between operations  2.15 us (2%)
    ppermute x27, waiting for transfers between devices, start(): self.other = [lax.ppermute(v, ('batch', 'seq'), pairs) for v in value]  36.5 us
    pallas_call x45, Pallas kernels, call(): pl.pallas_call(run, out_shape=[jax.ShapeDtypeStruct(s, d) for s, d in out...  36.3 us
    ppermute x27, starting transfers between devices, start(): self.other = [lax.ppermute(v, ('batch', 'seq'), pairs) for v in value]  29.7 us
    unnamed x24, local copies, waits for them, and re-layouts  3.11 us
    ppermute x1, waiting for transfers between devices, body(): recv = lax.ppermute(edge, 'seq', onward)  2.63 us
  transfers between devices with their start and end apart: 30, of which 17 were waited for; matrix products, arithmetic and copies ran while one was open for 0% of the time, Pallas kernels for 27%

profile of v3, /device:TPU:0, one launch (start us, length us, event | category | flops | bytes accessed | tf_op | source)
XLA Modules:
  0.0 111.3 jit_solution(16017674319849562078)
XLA Ops:
  0.7 1.0 copy-done.5
  1.7 0.3 standardize.1.refs_0_.refs_4_
  2.0 1.1 copy-done.4
  3.1 1.2 %project.1 = (bf16[512,512]{1,0:T(8,128)(2,1)S(1)}, bf16[512,1024]{1,0:T(8,128)(2,1)S(1)}, bf16[496,1024]{1,0:T(8,128)(2,1)S(1)}, bf16[96,1024]{1,0:T(8,128)(2,1)S(1)}) custom-call(f32[512,512]{1,0:T(8,128)S(1)} %standardize.1.refs_0_.refs_4_, bf16[512]{0:T(512)(128)(2,1)S(1)} %copy-done.11, bf16[512]{0:T(512)(128)(2,1)S(1)} %copy-done.10, ...), custom_call_target="tpu_custom_call" | custom-call | flops 3449999872 | bytes 65536 | tf_op jit(solution)/shard_map/project/pallas_call | solution.py:46
  4.4 0.5 collective-permute-start
  5.8 0.4 project_q.1.refs_3_.refs_0_
  6.3 1.3 %hidden_back.1 = (bf16[512,512]{1,0:T(8,128)(2,1)S(1)}, f32[512,2048]{1,0:T(8,128)S(1)}) custom-call(s32[1]{0:T(128)S(6)} %copy.29.refs_0_, bf16[512,512]{1,0:T(8,128)(2,1)S(1)} %bitcast.8, bf16[2048,512]{1,0:T(8,128)(2,1)S(1)} %copy-done.1, bf16[512,512]{1,0:T(8,128)(2,1)S(1)} %project_q.1.refs_3_.refs_0_), custom_call_target="tpu_custom_call" | custom-call | flops 230000000 | bytes 65536 | tf_op jit(solution)/shard_map/hidden_back/pallas_call | solution.py:46
  7.6 2.6 %collective-permute-done.refs_3_ = bf16[96,1024]{1,0:T(8,128)(2,1)S(1)} collective-permute-done((bf16[96,1024]{1,0:T(8,128)(2,1)S(1)}, bf16[96,1024]{1,0:T(8,128)(2,1)S(1)}, u32[]{:S(2)}, u32[]{:S(2)}) %collective-permute-start) | collective-permute-done | bytes 196640 | tf_op jit(solution)/shard_map/ppermute | solution.py:614
  10.2 2.2 %attend.1 = (bf16[512,512]{1,0:T(8,128)(2,1)S(1)}, bf16[4096,128]{1,0:T(8,128)(2,1)S(1)}, bf16[96,512]{1,0:T(8,128)(2,1)S(1)}) custom-call(bf16[512,512]{1,0:T(8,128)(2,1)S(1)} %project_q.1.refs_3_.refs_0_, bf16[512,1024]{1,0:T(8,128)(2,1)S(1)} %get-tuple-element.75.refs_1_, bf16[496,1024]{1,0:T(8,128)(2,1)S(1)} %get-tuple-element.76.refs_2_, ...), custom_call_target="tpu_custom_call" | custom-call | flops 575000000 | bytes 65536 | tf_op jit(solution)/shard_map/attend/pallas_call | solution.py:46
  12.5 0.2 collective-permute-start.1
  12.8 4.9 %feed_forward.1 = (f32[512,512]{1,0:T(8,128)S(1)}, bf16[512,512]{1,0:T(8,128)(2,1)S(1)}, bf16[512,2048]{1,0:T(8,128)(2,1)S(1)}, bf16[512,2048]{1,0:T(8,128)(2,1)...) custom-call(bf16[512,512]{1,0:T(8,128)(2,1)S(1)} %get-tuple-element.79.refs_0_.refs_5_, ...), custom_call_target="tpu_custom_call" | custom-call | flops 1150000000 | bytes 65536 | tf_op jit(solution)/shard_map/feed_forward/pallas_call | solution.py:46
  17.7 2.4 %collective-permute-start.3 = (bf16[1024,512]{1,0:T(8,128)(2,1)S(1)}, bf16[1024,512]{1,0:T(8,128)(2,1)S(1)}, u32[]{:S(2)}, u32[]{:S(2)}) collective-permute-start(bf16[1024,512]{1,0:T(8,128)(2,1)S(1)} %get-tuple-element.85.refs_2_), channel_id=1, source_target_pairs={{0,1},{1,0},{2,3},{3,2},{4,5},{5,4},{6,7},{7,6},{8,9},{9,8},{10,11... | collective-permute-start | bytes 3145736 | tf_op jit(solution)/shard_map/ppermute | solution.py:535
  20.2 1.5 %up_back.1 = (bf16[1024,512]{1,0:T(8,128)(2,1)S(1)}, bf16[1024,512]{1,0:T(8,128)(2,1)S(1)}) custom-call(bf16[512,512]{1,0:T(8,128)(2,1)S(1)} %get-tuple-element.83.refs_0_, bf16[512,2048]{1,0:T(8,128)(2,1)S(1)} %get-tuple-element.84.refs_1_, bf16[1024,512]{1,0:T(8,128)(2,1)S(1)} %get-tuple-element.85.refs_2_, ...), custom_call_target="tpu_custom_call" | custom-call | flops 575000000 | bytes 65536 | tf_op jit(solution)/shard_map/up_back/pallas_call | solution.py:46
  21.8 0.6 collective-permute-done.3.refs_1_
  22.5 0.2 add_split.9
  22.6 1.6 %collective-permute-start.5 = (bf16[512,512]{1,0:T(8,128)(2,1)S(1)}, bf16[512,512]{1,0:T(8,128)(2,1)S(1)}, u32[]{:S(2)}, u32[]{:S(2)}) collective-permute-start(bf16[512,512]{1,0:T(8,128)(2,1)S(1)} %get-tuple-element.94), channel_id=1, source_target_pairs={{0,4},{1,3},{2,6},{3,1},{4,0},{5,7},{6,2},{7,5},{8,12},{9,11},{10,... | collective-permute-start | bytes 1572872 | tf_op jit(solution)/shard_map/ppermute | solution.py:535
  24.2 2.4 %mid_back.1 = (f32[512,512]{1,0:T(8,128)S(1)}, bf16[512,512]{1,0:T(8,128)(2,1)S(1)}, bf16[512,512]{1,0:T(8,128)(2,1)S(1)}, f32[8,512]{1,0:T(8,128)S(1)}) custom-call(f32[512,512]{1,0:T(8,128)S(1)} %get-tuple-element.81.refs_0_, bf16[512,2048]{1,0:T(8,128)(2,1)S(1)} %get-tuple-element.84.refs_1_, bf16[512,2048]{1,0:T(8,128)(2,1)S(1)} %copy-done, ...), custom_call_target="tpu_custom_call" | custom-call | flops 575000000 | bytes 65536 | tf_op jit(solution)/shard_map/mid_back/pallas_call | solution.py:46
  26.6 0.1 add_split.10
  26.7 0.6 collective-permute-start.4
  27.3 3.8 %attend_back.1 = (bf16[512,1536]{1,0:T(8,128)(2,1)S(1)}, bf16[96,1024]{1,0:T(8,128)(2,1)S(1)}) custom-call(bf16[512,512]{1,0:T(8,128)(2,1)S(1)} %project_q.1.refs_3_.refs_0_, bf16[512,1024]{1,0:T(8,128)(2,1)S(1)} %get-tuple-element.75.refs_1_, bf16[496,1024]{1,0:T(8,128)(2,1)S(1)} %get-tuple-element.76.refs_2_, ...), custom_call_target="tpu_custom_call" | custom-call | flops 23000000512 | bytes 65536 | tf_op jit(solution)/shard_map/attend_back/pallas_call | solution.py:46
  31.1 3.0 %project_back.1 = (f32[512,512]{1,0:T(8,128)S(1)}, bf16[96,512]{1,0:T(8,128)(2,1)S(1)}, bf16[256,2176]{1,0:T(8,128)(2,1)S(1)}, bf16[256,2176]{1,0:T(8,128)(2,1)S(1)}) custom-call(bf16[512,1536]{1,0:T(8,128)(2,1)S(1)} %get-tuple-element.96.refs_0_, bf16[96,1024]{1,0:T(8,128)(2,1)S(1)} %get-tuple-element.97.refs_1_.refs_10_, ...), custom_call_target="tpu_custom_call" | custom-call | flops 2300000000 | bytes 65536 | tf_op jit(solution)/shard_map/project_back/pallas_call | solution.py:46
  34.3 0.3 collective-permute-start.7
  34.6 2.9 %collective-permute-done.4.refs_1_ = bf16[512,512]{1,0:T(8,128)(2,1)S(1)} collective-permute-done((bf16[512,512]{1,0:T(8,128)(2,1)S(1)}, bf16[512,512]{1,0:T(8,128)(2,1)S(1)}, u32[]{:S(2)}, u32[]{:S(2)}) %collective-permute-start.4) | collective-permute-done | bytes 524320 | tf_op jit(solution)/shard_map/ppermute | solution.py:535
  37.5 1.6 %collective-permute-start.6 = (bf16[256,512]{1,0:T(8,128)(2,1)S(1)}, bf16[256,512]{1,0:T(8,128)(2,1)S(1)}, u32[]{:S(2)}, u32[]{:S(2)}) collective-permute-start(bf16[256,512]{1,0:T(8,128)(2,1)S(1)} %get-tuple-element.103), channel_id=1, source_target_pairs={{0,8},{1,5},{2,10},{3,7},{4,12},{5,1},{6,14},{7,3},{8,0},{9,13},{1... | collective-permute-start | bytes 786440 | tf_op jit(solution)/shard_map/ppermute | solution.py:535
  39.2 0.1 add_split.13
  39.3 1.4 %collective-permute-done.7.refs_1_ = bf16[256,512]{1,0:T(8,128)(2,1)S(1)} collective-permute-done((bf16[256,512]{1,0:T(8,128)(2,1)S(1)}, bf16[256,512]{1,0:T(8,128)(2,1)S(1)}, u32[]{:S(2)}, u32[]{:S(2)}) %collective-permute-start.7) | collective-permute-done | bytes 262176 | tf_op jit(solution)/shard_map/ppermute | solution.py:535
  40.7 3.3 %collective-permute-done.6.refs_1_ = bf16[256,512]{1,0:T(8,128)(2,1)S(1)} collective-permute-done((bf16[256,512]{1,0:T(8,128)(2,1)S(1)}, bf16[256,512]{1,0:T(8,128)(2,1)S(1)}, u32[]{:S(2)}, u32[]{:S(2)}) %collective-permute-start.6) | collective-permute-done | bytes 262176 | tf_op jit(solution)/shard_map/ppermute | solution.py:535
  44.0 2.7 %collective-permute-start.9 = (bf16[128,512]{1,0:T(8,128)(2,1)S(1)}, bf16[128,512]{1,0:T(8,128)(2,1)S(1)}, u32[]{:S(2)}, u32[]{:S(2)}) collective-permute-start(bf16[128,512]{1,0:T(8,128)(2,1)S(1)} %get-tuple-element.109), channel_id=1, source_target_pairs={{0,16},{1,9},{2,18},{3,11},{4,20},{5,13},{6,22},{7,15},{8,24},{9,1... | collective-permute-start | bytes 393224 | tf_op jit(solution)/shard_map/ppermute | solution.py:535
  46.7 1.6 %collective-permute-start.11 = (bf16[128,512]{1,0:T(8,128)(2,1)S(1)}, bf16[128,512]{1,0:T(8,128)(2,1)S(1)}, u32[]{:S(2)}, u32[]{:S(2)}) collective-permute-start(bf16[128,512]{1,0:T(8,128)(2,1)S(1)} %get-tuple-element.110), channel_id=1, source_target_pairs={{0,8},{1,9},{2,10},{3,11},{4,12},{5,13},{6,14},{7,15},{8,0},{9,1},... | collective-permute-start | bytes 393224 | tf_op jit(solution)/shard_map/ppermute | solution.py:535
  48.3 1.5 %collective-permute-start.13 = (bf16[128,2176]{1,0:T(8,128)(2,1)S(1)}, bf16[128,2176]{1,0:T(8,128)(2,1)S(1)}, u32[]{:S(2)}, u32[]{:S(2)}) collective-permute-start(bf16[128,2176]{1,0:T(8,128)(2,1)S(1)} %get-tuple-element.111), channel_id=1, source_target_pairs={{0,4},{1,3},{2,6},{3,1},{4,0},{5,7},{6,2},{7,5},{8,12},{9,11},{10,... | collective-permute-start | bytes 1671176 | tf_op jit(solution)/shard_map/ppermute | solution.py:535
  49.7 0.6 collective-permute-done.9.refs_1_
  50.4 0.1 collective-permute-start.10
  50.5 2.9 %collective-permute-done.11.refs_1_ = bf16[128,512]{1,0:T(8,128)(2,1)S(1)} collective-permute-done((bf16[128,512]{1,0:T(8,128)(2,1)S(1)}, bf16[128,512]{1,0:T(8,128)(2,1)S(1)}, u32[]{:S(2)}, u32[]{:S(2)}) %collective-permute-start.11) | collective-permute-done | bytes 131104 | tf_op jit(solution)/shard_map/ppermute | solution.py:535
  53.4 2.4 %collective-permute-start.15 = (bf16[128,512]{1,0:T(8,128)(2,1)S(1)}, bf16[128,512]{1,0:T(8,128)(2,1)S(1)}, u32[]{:S(2)}, u32[]{:S(2)}) collective-permute-start(bf16[128,512]{1,0:T(8,128)(2,1)S(1)} %add.7.refs_2_.refs_0_), channel_id=1, source_target_pairs={{0,16},{1,17},{2,18},{3,19},{4,20},{5,21},{6,22},{7,23},{8,24},{9,... | collective-permute-start | bytes 393224 | tf_op jit(solution)/shard_map/ppermute | solution.py:535
  55.8 1.0 collective-permute-done.10.refs_1_
  56.9 2.0 %collective-permute-start.12 = (bf16[128,512]{1,0:T(8,128)(2,1)S(1)}, bf16[128,512]{1,0:T(8,128)(2,1)S(1)}, u32[]{:S(2)}, u32[]{:S(2)}) collective-permute-start(bf16[128,512]{1,0:T(8,128)(2,1)S(1)} %add.8.refs_2_.refs_0_), channel_id=1, source_target_pairs={{0,16},{1,9},{2,18},{3,11},{4,20},{5,13},{6,22},{7,15},{8,24},{9,1... | collective-permute-start | bytes 393224 | tf_op jit(solution)/shard_map/ppermute | solution.py:535
  59.0 0.6 collective-permute-start.14
  59.5 2.7 %collective-permute-done.15.refs_1_ = bf16[128,512]{1,0:T(8,128)(2,1)S(1)} collective-permute-done((bf16[128,512]{1,0:T(8,128)(2,1)S(1)}, bf16[128,512]{1,0:T(8,128)(2,1)S(1)}, u32[]{:S(2)}, u32[]{:S(2)}) %collective-permute-start.15) | collective-permute-done | bytes 131104 | tf_op jit(solution)/shard_map/ppermute | solution.py:535
  62.3 3.3 %collective-permute-done.14.refs_1_ = bf16[64,2176]{1,0:T(8,128)(2,1)S(1)} collective-permute-done((bf16[64,2176]{1,0:T(8,128)(2,1)S(1)}, bf16[64,2176]{1,0:T(8,128)(2,1)S(1)}, u32[]{:S(2)}, u32[]{:S(2)}) %collective-permute-start.14) | collective-permute-done | bytes 278560 | tf_op jit(solution)/shard_map/ppermute | solution.py:535
  65.6 2.3 %collective-permute-start.16 = (bf16[32,2176]{1,0:T(8,128)(2,1)S(1)}, bf16[32,2176]{1,0:T(8,128)(2,1)S(1)}, u32[]{:S(2)}, u32[]{:S(2)}) collective-permute-start(bf16[32,2176]{1,0:T(8,128)(2,1)S(1)} %get-tuple-element.115), channel_id=1, source_target_pairs={{0,8},{1,9},{2,10},{3,11},{4,12},{5,13},{6,14},{7,15},{8,0},{9,1},... | collective-permute-start | bytes 417800 | tf_op jit(solution)/shard_map/ppermute | solution.py:535
  67.9 0.6 collective-permute-start.19
  68.5 3.1 %collective-permute-done.16.refs_1_ = bf16[32,2176]{1,0:T(8,128)(2,1)S(1)} collective-permute-done((bf16[32,2176]{1,0:T(8,128)(2,1)S(1)}, bf16[32,2176]{1,0:T(8,128)(2,1)S(1)}, u32[]{:S(2)}, u32[]{:S(2)}) %collective-permute-start.16) | collective-permute-done | bytes 139296 | tf_op jit(solution)/shard_map/ppermute | solution.py:535
  71.7 0.1 collective-permute-start.21
  71.9 2.9 %collective-permute-start.18 = (bf16[256,512]{1,0:T(8,128)(2,1)S(1)}, bf16[256,512]{1,0:T(8,128)(2,1)S(1)}, u32[]{:S(2)}, u32[]{:S(2)}) collective-permute-start(bf16[256,512]{1,0:T(8,128)(2,1)S(1)} %join.10.refs_2_.refs_0_), channel_id=1, source_target_pairs={{0,8},{1,5},{2,10},{3,7},{4,12},{5,1},{6,14},{7,3},{8,0},{9,13},{1... | collective-permute-start | bytes 786440 | tf_op jit(solution)/shard_map/ppermute | solution.py:535
  74.7 0.2 collective-permute-done.19.refs_1_
  75.0 1.7 %collective-permute-start.23 = (bf16[512,512]{1,0:T(8,128)(2,1)S(1)}, bf16[512,512]{1,0:T(8,128)(2,1)S(1)}, u32[]{:S(2)}, u32[]{:S(2)}) collective-permute-start(bf16[512,512]{1,0:T(8,128)(2,1)S(1)} %join.11.refs_2_.refs_0_), channel_id=1, source_target_pairs={{0,4},{1,3},{2,6},{3,1},{4,0},{5,7},{6,2},{7,5},{8,12},{9,11},{10,... | collective-permute-start | bytes 1572872 | tf_op jit(solution)/shard_map/ppermute | solution.py:535
  76.6 5.4 %collective-permute-done.18.refs_1_ = bf16[256,512]{1,0:T(8,128)(2,1)S(1)} collective-permute-done((bf16[256,512]{1,0:T(8,128)(2,1)S(1)}, bf16[256,512]{1,0:T(8,128)(2,1)S(1)}, u32[]{:S(2)}, u32[]{:S(2)}) %collective-permute-start.18) | collective-permute-done | bytes 262176 | tf_op jit(solution)/shard_map/ppermute | solution.py:535
  82.1 1.1 %collective-permute-start.20 = (bf16[512,512]{1,0:T(8,128)(2,1)S(1)}, bf16[512,512]{1,0:T(8,128)(2,1)S(1)}, u32[]{:S(2)}, u32[]{:S(2)}) collective-permute-start(bf16[512,512]{1,0:T(8,128)(2,1)S(1)} %join.12.refs_2_.refs_0_), channel_id=1, source_target_pairs={{0,4},{1,3},{2,6},{3,1},{4,0},{5,7},{6,2},{7,5},{8,12},{9,11},{10,... | collective-permute-start | bytes 1572872 | tf_op jit(solution)/shard_map/ppermute | solution.py:535
  83.3 1.3 %collective-permute-start.22 = (bf16[32,2176]{1,0:T(8,128)(2,1)S(1)}, bf16[32,2176]{1,0:T(8,128)(2,1)S(1)}, u32[]{:S(2)}, u32[]{:S(2)}) collective-permute-start(bf16[32,2176]{1,0:T(8,128)(2,1)S(1)} %add.11.refs_2_.refs_0_), channel_id=1, source_target_pairs={{0,8},{1,9},{2,10},{3,11},{4,12},{5,13},{6,14},{7,15},{8,0},{9,1},... | collective-permute-start | bytes 417800 | tf_op jit(solution)/shard_map/ppermute | solution.py:535
  84.8 1.4 %finish_down.2 = (f32[2048,512]{1,0:T(8,128)}, f32[8,128]{1,0:T(8,128)S(1)}) custom-call(bf16[1024,512]{1,0:T(8,128)(2,1)S(1)} %join.13.refs_0_.refs_1_, bf16[1024,512]{1,0:T(8,128)(2,1)S(1)} %join.13.refs_0_.refs_1_), custom_call_target="tpu_custom_call" | custom-call | flops 575000000 | bytes 65536 | tf_op jit(solution)/shard_map/finish_down/pallas_call | solution.py:46
  86.2 2.2 %collective-permute-done.22.refs_1_ = bf16[32,2176]{1,0:T(8,128)(2,1)S(1)} collective-permute-done((bf16[32,2176]{1,0:T(8,128)(2,1)S(1)}, bf16[32,2176]{1,0:T(8,128)(2,1)S(1)}, u32[]{:S(2)}, u32[]{:S(2)}) %collective-permute-start.22) | collective-permute-done | bytes 139296 | tf_op jit(solution)/shard_map/ppermute | solution.py:535
  88.4 0.9 collective-permute-start.27
  89.3 4.0 %collective-permute-done.20.refs_1_ = bf16[512,512]{1,0:T(8,128)(2,1)S(1)} collective-permute-done((bf16[512,512]{1,0:T(8,128)(2,1)S(1)}, bf16[512,512]{1,0:T(8,128)(2,1)S(1)}, u32[]{:S(2)}, u32[]{:S(2)}) %collective-permute-start.20) | collective-permute-done | bytes 524320 | tf_op jit(solution)/shard_map/ppermute | solution.py:535
  93.4 1.4 %finish_down.3 = (f32[2048,512]{1,0:T(8,128)}, f32[8,128]{1,0:T(8,128)S(1)}) custom-call(bf16[1024,512]{1,0:T(8,128)(2,1)S(1)} %collective-permute-done.26.refs_0_, f32[2048,512]{1,0:T(8,128)} %get-tuple-element.123.refs_1_), custom_call_target="tpu_custom_call", output_to_operand_aliasing={{0}: (1, {})} | custom-call | flops 575000000 | bytes 65536 | tf_op jit(solution)/shard_map/finish_down/pallas_call | solution.py:46
  94.8 1.7 %tokens_back.1 = (bf16[512,512]{1,0:T(8,128)(2,1)}, f32[8,128]{1,0:T(8,128)S(1)}) custom-call(f32[512,512]{1,0:T(8,128)S(1)} %get-tuple-element.120.refs_0_, bf16[96,512]{1,0:T(8,128)(2,1)S(1)} %collective-permute-done.25.refs_1_, bf16[512,512]{1,0:T(8,128)(2,1)S(1)} %bitcast.7, bf16[512]{0:T(512)(128)(2,1)S(1)} %copy-done.11, ...), custom_call_target="tpu_custom_call" | custom-call | flops 23000000512 | bytes 65536 | tf_op jit(solution)/shard_map/tokens_back/pallas_call | solution.py:46
  96.5 1.0 collective-permute-start.28
  97.5 2.0 %finish_up.2 = (f32[512,2048]{1,0:T(8,128)}, f32[8,128]{1,0:T(8,128)}) custom-call(bf16[1024,512]{1,0:T(8,128)(2,1)S(1)} %join.15.refs_0_.refs_1_, bf16[1024,512]{1,0:T(8,128)(2,1)S(1)} %join.15.refs_0_.refs_1_), custom_call_target="tpu_custom_call" | custom-call | flops 575000000 | bytes 65536 | tf_op jit(solution)/shard_map/finish_up/pallas_call | solution.py:46
  99.5 1.4 %finish_up.3 = (f32[512,2048]{1,0:T(8,128)}, f32[8,128]{1,0:T(8,128)S(1)}) custom-call(bf16[1024,512]{1,0:T(8,128)(2,1)S(1)} %collective-permute-done.24.refs_0_, f32[512,2048]{1,0:T(8,128)} %get-tuple-element.117.refs_1_), custom_call_target="tpu_custom_call", output_to_operand_aliasing={{0}: (1, {})} | custom-call | flops 575000000 | bytes 65536 | tf_op jit(solution)/shard_map/finish_up/pallas_call | solution.py:46
  100.9 0.9 copy-done.2
  101.9 2.0 %output.1 = (bf16[512,512]{1,0:T(8,128)(2,1)}, f32[8,128]{1,0:T(8,128)S(1)}) custom-call(f32[512,512]{1,0:T(8,128)S(1)} %get-tuple-element.81.refs_0_, bf16[512,2048]{1,0:T(8,128)(2,1)S(1)} %get-tuple-element.82.refs_1_, bf16[2048,512]{1,0:T(8,128)(2,1)S(1)} %copy-done.2, f32[8,128]{1,0:T(8,128)S(1)} %get-tuple-element.118.refs_3_), custom_call_target="tpu_custom_call" | custom-call | flops 575000000 | bytes 65536 | tf_op jit(solution)/shard_map/output/pallas_call | solution.py:46
  103.9 2.2 %collective-permute-done.28.refs_1_ = bf16[128,2176]{1,0:T(8,128)(2,1)S(1)} collective-permute-done((bf16[128,2176]{1,0:T(8,128)(2,1)S(1)}, bf16[128,2176]{1,0:T(8,128)(2,1)S(1)}, u32[]{:S(2)}, u32[]{:S(2)}) %collective-permute-start.28) | collective-permute-done | bytes 557088 | tf_op jit(solution)/shard_map/ppermute | solution.py:535
  106.3 2.0 %finish_rest.2 = (f32[512,1536]{1,0:T(8,128)}, f32[512,512]{1,0:T(8,128)}, f32[8,128]{1,0:T(8,128)}) custom-call(bf16[256,2176]{1,0:T(8,128)(2,1)S(1)} %join.17.refs_0_.refs_1_, bf16[256,2176]{1,0:T(8,128)(2,1)S(1)} %join.17.refs_0_.refs_1_), custom_call_target="tpu_custom_call" | custom-call | flops 575000000 | bytes 65536 | tf_op jit(solution)/shard_map/finish_rest/pallas_call | solution.py:46
  108.3 0.7 collective-permute-done.29.refs_0_
  109.1 2.0 %finish_rest.3 = (f32[512,1536]{1,0:T(8,128)}, f32[512,512]{1,0:T(8,128)}, f32[512]{0:T(512)}, f32[512]{0:T(512)}, f32[512]{0:T(512)}, /*index=5*/f32[512]{0:T(512)}, f32[8,128]{1,0:T(8,128)}) custom-call(bf16[256,2176]{1,0:T(8,128)(2,1)S(1)} %collective-permute-done.29.refs_0_, ...), custom_call_target="tpu_custom_call", output_to_operand_aliasing={{0}: (2, {}), {1}: (3, {})} | custom-call | flops 575000000 | bytes 65536 | tf_op jit(solution)/shard_map/finish_rest/pallas_call | solution.py:46
  (65 shorter events, 1.5 us)
Async XLA Ops:
  0.6 1.0 copy-start.5
  1.7 1.4 %copy-start.4 = (bf16[512,1536]{1,0:T(8,128)(2,1)S(1)}, bf16[512,1536]{1,0:T(8,128)(2,1)}, u32[]{:S(2)}) copy-start(bf16[512,1536]{1,0:T(8,128)(2,1)} %refs_4_.3) | copy-start | bytes 4718596
  1.7 1.4 %copy-start.10 = (bf16[512]{0:T(512)(128)(2,1)S(1)}, bf16[512]{0:T(512)(128)(2,1)}, u32[]{:S(2)}) copy-start(bf16[512]{0:T(512)(128)(2,1)} %refs_9_.1) | copy-start | bytes 3076
  1.7 1.4 %copy-start.11 = (bf16[512]{0:T(512)(128)(2,1)S(1)}, bf16[512]{0:T(512)(128)(2,1)}, u32[]{:S(2)}) copy-start(bf16[512]{0:T(512)(128)(2,1)} %refs_3_.7) | copy-start | bytes 3076
  4.4 1.9 %copy-start.1 = (bf16[2048,512]{1,0:T(8,128)(2,1)S(1)}, bf16[2048,512]{1,0:T(8,128)(2,1)}, u32[]{:S(2)}) copy-start(bf16[2048,512]{1,0:T(8,128)(2,1)} %refs_2_.9) | copy-start | bytes 6291460
  4.4 1.9 %copy-start.7 = (bf16[1,512,512]{2,1,0:T(8,128)(2,1)S(1)}, bf16[1,512,512]{2,1,0:T(8,128)(2,1)}, u32[]{:S(2)}) copy-start(bf16[1,512,512]{2,1,0:T(8,128)(2,1)} %param.13) | copy-start | bytes 1572868
  4.4 5.8 %collective-permute-start = (bf16[96,1024]{1,0:T(8,128)(2,1)S(1)}, bf16[96,1024]{1,0:T(8,128)(2,1)S(1)}, u32[]{:S(2)}, u32[]{:S(2)}) collective-permute-start(bf16[96,1024]{1,0:T(8,128)(2,1)S(1)} %get-tuple-element.77), channel_id=1, source_target_pairs={{0,1},{1,2},{2,3},{3,0},{4,5},{5,6},{6,7},{7,4},{8,9},{9,10},{10,1... | collective-permute-start | bytes 589832 | tf_op jit(solution)/shard_map/ppermute | solution.py:614
  10.2 2.5 %copy-start = (bf16[512,2048]{1,0:T(8,128)(2,1)S(1)}, bf16[512,2048]{1,0:T(8,128)(2,1)}, u32[]{:S(2)}) copy-start(bf16[512,2048]{1,0:T(8,128)(2,1)} %refs_2_.8) | copy-start | bytes 6291460
  10.2 2.5 %copy-start.3 = (bf16[512,512]{1,0:T(8,128)(2,1)S(1)}, bf16[512,512]{1,0:T(8,128)(2,1)}, u32[]{:S(2)}) copy-start(bf16[512,512]{1,0:T(8,128)(2,1)} %refs_6_.1) | copy-start | bytes 1572868
  10.2 2.5 %copy-start.6 = (bf16[1,512,512]{2,1,0:T(8,128)(2,1)S(1)}, bf16[1,512,512]{2,1,0:T(8,128)(2,1)}, u32[]{:S(2)}) copy-start(bf16[1,512,512]{2,1,0:T(8,128)(2,1)} %param.11) | copy-start | bytes 1572868
  10.2 2.5 %copy-start.8 = (bf16[512]{0:T(512)(128)(2,1)S(1)}, bf16[512]{0:T(512)(128)(2,1)}, u32[]{:S(2)}) copy-start(bf16[512]{0:T(512)(128)(2,1)} %refs_3_.6) | copy-start | bytes 3076
  10.2 2.6 %copy-start.9 = (bf16[512]{0:T(512)(128)(2,1)S(1)}, bf16[512]{0:T(512)(128)(2,1)}, u32[]{:S(2)}) copy-start(bf16[512]{0:T(512)(128)(2,1)} %refs_4_.2) | copy-start | bytes 3076
  12.5 7.7 %collective-permute-start.1 = (bf16[96,512]{1,0:T(8,128)(2,1)S(1)}, bf16[96,512]{1,0:T(8,128)(2,1)S(1)}, u32[]{:S(2)}, u32[]{:S(2)}) collective-permute-start(bf16[96,512]{1,0:T(8,128)(2,1)S(1)} %get-tuple-element.86), channel_id=1, source_target_pairs={{0,1},{1,2},{2,3},{3,0},{4,5},{5,6},{6,7},{7,4},{8,9},{9,10},{10,1... | collective-permute-start | bytes 294920 | tf_op jit(solution)/shard_map/ppermute | solution.py:625
  17.7 4.7 %collective-permute-start.3 = (bf16[1024,512]{1,0:T(8,128)(2,1)S(1)}, bf16[1024,512]{1,0:T(8,128)(2,1)S(1)}, u32[]{:S(2)}, u32[]{:S(2)}) collective-permute-start(bf16[1024,512]{1,0:T(8,128)(2,1)S(1)} %get-tuple-element.85.refs_2_), channel_id=1, source_target_pairs={{0,1},{1,0},{2,3},{3,2},{4,5},{5,4},{6,7},{7,6},{8,9},{9,8},{10,11... | collective-permute-start | bytes 3145736 | tf_op jit(solution)/shard_map/ppermute | solution.py:535
  21.7 4.9 %collective-permute-start.2 = (bf16[1024,512]{1,0:T(8,128)(2,1)S(1)}, bf16[1024,512]{1,0:T(8,128)(2,1)S(1)}, u32[]{:S(2)}, u32[]{:S(2)}) collective-permute-start(bf16[1024,512]{1,0:T(8,128)(2,1)S(1)} %get-tuple-element.88.refs_0_), channel_id=1, source_target_pairs={{0,1},{1,0},{2,3},{3,2},{4,5},{5,4},{6,7},{7,6},{8,9},{9,8},{10,11... | collective-permute-start | bytes 3145736 | tf_op jit(solution)/shard_map/ppermute | solution.py:535
  22.6 11.6 %collective-permute-start.5 = (bf16[512,512]{1,0:T(8,128)(2,1)S(1)}, bf16[512,512]{1,0:T(8,128)(2,1)S(1)}, u32[]{:S(2)}, u32[]{:S(2)}) collective-permute-start(bf16[512,512]{1,0:T(8,128)(2,1)S(1)} %get-tuple-element.94), channel_id=1, source_target_pairs={{0,4},{1,3},{2,6},{3,1},{4,0},{5,7},{6,2},{7,5},{8,12},{9,11},{10,... | collective-permute-start | bytes 1572872 | tf_op jit(solution)/shard_map/ppermute | solution.py:535
  26.7 10.8 %collective-permute-start.4 = (bf16[512,512]{1,0:T(8,128)(2,1)S(1)}, bf16[512,512]{1,0:T(8,128)(2,1)S(1)}, u32[]{:S(2)}, u32[]{:S(2)}) collective-permute-start(bf16[512,512]{1,0:T(8,128)(2,1)S(1)} %get-tuple-element.93), channel_id=1, source_target_pairs={{0,4},{1,3},{2,6},{3,1},{4,0},{5,7},{6,2},{7,5},{8,12},{9,11},{10,... | collective-permute-start | bytes 1572872 | tf_op jit(solution)/shard_map/ppermute | solution.py:535
  34.1 5.1 %collective-permute-start.8 = (bf16[256,2176]{1,0:T(8,128)(2,1)S(1)}, bf16[256,2176]{1,0:T(8,128)(2,1)S(1)}, u32[]{:S(2)}, u32[]{:S(2)}) collective-permute-start(bf16[256,2176]{1,0:T(8,128)(2,1)S(1)} %get-tuple-element.100.refs_2_), channel_id=1, source_target_pairs={{0,1},{1,0},{2,3},{3,2},{4,5},{5,4},{6,7},{7,6},{8,9},{9,8},{10,11... | collective-permute-start | bytes 3342344 | tf_op jit(solution)/shard_map/ppermute | solution.py:535
  34.3 6.4 %collective-permute-start.7 = (bf16[256,512]{1,0:T(8,128)(2,1)S(1)}, bf16[256,512]{1,0:T(8,128)(2,1)S(1)}, u32[]{:S(2)}, u32[]{:S(2)}) collective-permute-start(bf16[256,512]{1,0:T(8,128)(2,1)S(1)} %get-tuple-element.104), channel_id=1, source_target_pairs={{0,2},{1,5},{2,0},{3,7},{4,6},{5,1},{6,4},{7,3},{8,10},{9,13},{10,... | collective-permute-start | bytes 786440 | tf_op jit(solution)/shard_map/ppermute | solution.py:535
  37.5 6.4 %collective-permute-start.6 = (bf16[256,512]{1,0:T(8,128)(2,1)S(1)}, bf16[256,512]{1,0:T(8,128)(2,1)S(1)}, u32[]{:S(2)}, u32[]{:S(2)}) collective-permute-start(bf16[256,512]{1,0:T(8,128)(2,1)S(1)} %get-tuple-element.103), channel_id=1, source_target_pairs={{0,8},{1,5},{2,10},{3,7},{4,12},{5,1},{6,14},{7,3},{8,0},{9,13},{1... | collective-permute-start | bytes 786440 | tf_op jit(solution)/shard_map/ppermute | solution.py:535
  44.0 6.3 %collective-permute-start.9 = (bf16[128,512]{1,0:T(8,128)(2,1)S(1)}, bf16[128,512]{1,0:T(8,128)(2,1)S(1)}, u32[]{:S(2)}, u32[]{:S(2)}) collective-permute-start(bf16[128,512]{1,0:T(8,128)(2,1)S(1)} %get-tuple-element.109), channel_id=1, source_target_pairs={{0,16},{1,9},{2,18},{3,11},{4,20},{5,13},{6,22},{7,15},{8,24},{9,1... | collective-permute-start | bytes 393224 | tf_op jit(solution)/shard_map/ppermute | solution.py:535
  46.7 48.1 %collective-permute-start.25 = (bf16[96,512]{1,0:T(8,128)(2,1)S(1)}, bf16[96,512]{1,0:T(8,128)(2,1)S(1)}, u32[]{:S(2)}, u32[]{:S(2)}) collective-permute-start(bf16[96,512]{1,0:T(8,128)(2,1)S(1)} %get-tuple-element.121), channel_id=1, source_target_pairs={{1,0},{2,1},{3,2},{0,3},{5,4},{6,5},{7,6},{4,7},{9,8},{10,9},{11,1... | collective-permute-start | bytes 294920 | tf_op jit(solution)/shard_map/ppermute | solution.py:682
  46.7 6.7 %collective-permute-start.11 = (bf16[128,512]{1,0:T(8,128)(2,1)S(1)}, bf16[128,512]{1,0:T(8,128)(2,1)S(1)}, u32[]{:S(2)}, u32[]{:S(2)}) collective-permute-start(bf16[128,512]{1,0:T(8,128)(2,1)S(1)} %get-tuple-element.110), channel_id=1, source_target_pairs={{0,8},{1,9},{2,10},{3,11},{4,12},{5,13},{6,14},{7,15},{8,0},{9,1},... | collective-permute-start | bytes 393224 | tf_op jit(solution)/shard_map/ppermute | solution.py:535
  48.3 10.6 %collective-permute-start.13 = (bf16[128,2176]{1,0:T(8,128)(2,1)S(1)}, bf16[128,2176]{1,0:T(8,128)(2,1)S(1)}, u32[]{:S(2)}, u32[]{:S(2)}) collective-permute-start(bf16[128,2176]{1,0:T(8,128)(2,1)S(1)} %get-tuple-element.111), channel_id=1, source_target_pairs={{0,4},{1,3},{2,6},{3,1},{4,0},{5,7},{6,2},{7,5},{8,12},{9,11},{10,... | collective-permute-start | bytes 1671176 | tf_op jit(solution)/shard_map/ppermute | solution.py:535
  50.4 6.5 %collective-permute-start.10 = (bf16[128,512]{1,0:T(8,128)(2,1)S(1)}, bf16[128,512]{1,0:T(8,128)(2,1)S(1)}, u32[]{:S(2)}, u32[]{:S(2)}) collective-permute-start(bf16[128,512]{1,0:T(8,128)(2,1)S(1)} %add.6.refs_2_.refs_0_), channel_id=1, source_target_pairs={{0,2},{1,17},{2,0},{3,19},{4,6},{5,21},{6,4},{7,23},{8,10},{9,25},... | collective-permute-start | bytes 393224 | tf_op jit(solution)/shard_map/ppermute | solution.py:535
  53.4 8.8 %collective-permute-start.15 = (bf16[128,512]{1,0:T(8,128)(2,1)S(1)}, bf16[128,512]{1,0:T(8,128)(2,1)S(1)}, u32[]{:S(2)}, u32[]{:S(2)}) collective-permute-start(bf16[128,512]{1,0:T(8,128)(2,1)S(1)} %add.7.refs_2_.refs_0_), channel_id=1, source_target_pairs={{0,16},{1,17},{2,18},{3,19},{4,20},{5,21},{6,22},{7,23},{8,24},{9,... | collective-permute-start | bytes 393224 | tf_op jit(solution)/shard_map/ppermute | solution.py:535
  56.9 14.9 %collective-permute-start.12 = (bf16[128,512]{1,0:T(8,128)(2,1)S(1)}, bf16[128,512]{1,0:T(8,128)(2,1)S(1)}, u32[]{:S(2)}, u32[]{:S(2)}) collective-permute-start(bf16[128,512]{1,0:T(8,128)(2,1)S(1)} %add.8.refs_2_.refs_0_), channel_id=1, source_target_pairs={{0,16},{1,9},{2,18},{3,11},{4,20},{5,13},{6,22},{7,15},{8,24},{9,1... | collective-permute-start | bytes 393224 | tf_op jit(solution)/shard_map/ppermute | solution.py:535
  59.0 6.6 %collective-permute-start.14 = (bf16[64,2176]{1,0:T(8,128)(2,1)S(1)}, bf16[64,2176]{1,0:T(8,128)(2,1)S(1)}, u32[]{:S(2)}, u32[]{:S(2)}) collective-permute-start(bf16[64,2176]{1,0:T(8,128)(2,1)S(1)} %get-tuple-element.113), channel_id=1, source_target_pairs={{0,2},{1,5},{2,0},{3,7},{4,6},{5,1},{6,4},{7,3},{8,10},{9,13},{10,... | collective-permute-start | bytes 835592 | tf_op jit(solution)/shard_map/ppermute | solution.py:535
  62.2 5.7 %collective-permute-start.17 = (bf16[128,512]{1,0:T(8,128)(2,1)S(1)}, bf16[128,512]{1,0:T(8,128)(2,1)S(1)}, u32[]{:S(2)}, u32[]{:S(2)}) collective-permute-start(bf16[128,512]{1,0:T(8,128)(2,1)S(1)} %add.9.refs_2_.refs_0_), channel_id=1, source_target_pairs={{0,8},{1,9},{2,10},{3,11},{4,12},{5,13},{6,14},{7,15},{8,0},{9,1},... | collective-permute-start | bytes 393224 | tf_op jit(solution)/shard_map/ppermute | solution.py:535
  65.6 6.1 %collective-permute-start.16 = (bf16[32,2176]{1,0:T(8,128)(2,1)S(1)}, bf16[32,2176]{1,0:T(8,128)(2,1)S(1)}, u32[]{:S(2)}, u32[]{:S(2)}) collective-permute-start(bf16[32,2176]{1,0:T(8,128)(2,1)S(1)} %get-tuple-element.115), channel_id=1, source_target_pairs={{0,8},{1,9},{2,10},{3,11},{4,12},{5,13},{6,14},{7,15},{8,0},{9,1},... | collective-permute-start | bytes 417800 | tf_op jit(solution)/shard_map/ppermute | solution.py:535
  67.9 7.0 %collective-permute-start.19 = (bf16[256,512]{1,0:T(8,128)(2,1)S(1)}, bf16[256,512]{1,0:T(8,128)(2,1)S(1)}, u32[]{:S(2)}, u32[]{:S(2)}) collective-permute-start(bf16[256,512]{1,0:T(8,128)(2,1)S(1)} %join.9.refs_2_.refs_0_), channel_id=1, source_target_pairs={{0,2},{1,5},{2,0},{3,7},{4,6},{5,1},{6,4},{7,3},{8,10},{9,13},{10,... | collective-permute-start | bytes 786440 | tf_op jit(solution)/shard_map/ppermute | solution.py:535
  71.7 11.5 %collective-permute-start.21 = (bf16[32,2176]{1,0:T(8,128)(2,1)S(1)}, bf16[32,2176]{1,0:T(8,128)(2,1)S(1)}, u32[]{:S(2)}, u32[]{:S(2)}) collective-permute-start(bf16[32,2176]{1,0:T(8,128)(2,1)S(1)} %add.10.refs_2_.refs_0_), channel_id=1, source_target_pairs={{0,16},{1,17},{2,18},{3,19},{4,20},{5,21},{6,22},{7,23},{8,24},{9,... | collective-permute-start | bytes 417800 | tf_op jit(solution)/shard_map/ppermute | solution.py:535
  71.9 10.2 %collective-permute-start.18 = (bf16[256,512]{1,0:T(8,128)(2,1)S(1)}, bf16[256,512]{1,0:T(8,128)(2,1)S(1)}, u32[]{:S(2)}, u32[]{:S(2)}) collective-permute-start(bf16[256,512]{1,0:T(8,128)(2,1)S(1)} %join.10.refs_2_.refs_0_), channel_id=1, source_target_pairs={{0,8},{1,5},{2,10},{3,7},{4,12},{5,1},{6,14},{7,3},{8,0},{9,13},{1... | collective-permute-start | bytes 786440 | tf_op jit(solution)/shard_map/ppermute | solution.py:535
  75.0 9.6 %collective-permute-start.23 = (bf16[512,512]{1,0:T(8,128)(2,1)S(1)}, bf16[512,512]{1,0:T(8,128)(2,1)S(1)}, u32[]{:S(2)}, u32[]{:S(2)}) collective-permute-start(bf16[512,512]{1,0:T(8,128)(2,1)S(1)} %join.11.refs_2_.refs_0_), channel_id=1, source_target_pairs={{0,4},{1,3},{2,6},{3,1},{4,0},{5,7},{6,2},{7,5},{8,12},{9,11},{10,... | collective-permute-start | bytes 1572872 | tf_op jit(solution)/shard_map/ppermute | solution.py:535
  82.1 11.2 %collective-permute-start.20 = (bf16[512,512]{1,0:T(8,128)(2,1)S(1)}, bf16[512,512]{1,0:T(8,128)(2,1)S(1)}, u32[]{:S(2)}, u32[]{:S(2)}) collective-permute-start(bf16[512,512]{1,0:T(8,128)(2,1)S(1)} %join.12.refs_2_.refs_0_), channel_id=1, source_target_pairs={{0,4},{1,3},{2,6},{3,1},{4,0},{5,7},{6,2},{7,5},{8,12},{9,11},{10,... | collective-permute-start | bytes 1572872 | tf_op jit(solution)/shard_map/ppermute | solution.py:535
  83.3 5.1 %collective-permute-start.22 = (bf16[32,2176]{1,0:T(8,128)(2,1)S(1)}, bf16[32,2176]{1,0:T(8,128)(2,1)S(1)}, u32[]{:S(2)}, u32[]{:S(2)}) collective-permute-start(bf16[32,2176]{1,0:T(8,128)(2,1)S(1)} %add.11.refs_2_.refs_0_), channel_id=1, source_target_pairs={{0,8},{1,9},{2,10},{3,11},{4,12},{5,13},{6,14},{7,15},{8,0},{9,1},... | collective-permute-start | bytes 417800 | tf_op jit(solution)/shard_map/ppermute | solution.py:535
  84.7 8.7 %collective-permute-start.26 = (bf16[1024,512]{1,0:T(8,128)(2,1)S(1)}, bf16[1024,512]{1,0:T(8,128)(2,1)S(1)}, u32[]{:S(2)}, u32[]{:S(2)}) collective-permute-start(bf16[1024,512]{1,0:T(8,128)(2,1)S(1)} %join.13.refs_0_.refs_1_), channel_id=1, source_target_pairs={{0,1},{1,0},{2,3},{3,2},{4,5},{5,4},{6,7},{7,6},{8,9},{9,8},{10,11... | collective-permute-start | bytes 3145736 | tf_op jit(solution)/shard_map/ppermute | solution.py:535
  88.4 8.1 %collective-permute-start.27 = (bf16[64,2176]{1,0:T(8,128)(2,1)S(1)}, bf16[64,2176]{1,0:T(8,128)(2,1)S(1)}, u32[]{:S(2)}, u32[]{:S(2)}) collective-permute-start(bf16[64,2176]{1,0:T(8,128)(2,1)S(1)} %join.14.refs_2_.refs_0_), channel_id=1, source_target_pairs={{0,2},{1,5},{2,0},{3,7},{4,6},{5,1},{6,4},{7,3},{8,10},{9,13},{10,... | collective-permute-start | bytes 835592 | tf_op jit(solution)/shard_map/ppermute | solution.py:535
  93.3 6.2 %collective-permute-start.24 = (bf16[1024,512]{1,0:T(8,128)(2,1)S(1)}, bf16[1024,512]{1,0:T(8,128)(2,1)S(1)}, u32[]{:S(2)}, u32[]{:S(2)}) collective-permute-start(bf16[1024,512]{1,0:T(8,128)(2,1)S(1)} %join.15.refs_0_.refs_1_), channel_id=1, source_target_pairs={{0,1},{1,0},{2,3},{3,2},{4,5},{5,4},{6,7},{7,6},{8,9},{9,8},{10,11... | collective-permute-start | bytes 3145736 | tf_op jit(solution)/shard_map/ppermute | solution.py:535
  96.5 9.6 %collective-permute-start.28 = (bf16[128,2176]{1,0:T(8,128)(2,1)S(1)}, bf16[128,2176]{1,0:T(8,128)(2,1)S(1)}, u32[]{:S(2)}, u32[]{:S(2)}) collective-permute-start(bf16[128,2176]{1,0:T(8,128)(2,1)S(1)} %join.16.refs_0_), channel_id=1, source_target_pairs={{0,4},{1,3},{2,6},{3,1},{4,0},{5,7},{6,2},{7,5},{8,12},{9,11},{10,... | collective-permute-start | bytes 1671176 | tf_op jit(solution)/shard_map/ppermute | solution.py:535
  99.5 2.4 %copy-start.2 = (bf16[2048,512]{1,0:T(8,128)(2,1)S(1)}, bf16[2048,512]{1,0:T(8,128)(2,1)}, u32[]{:S(2)}) copy-start(bf16[2048,512]{1,0:T(8,128)(2,1)} %refs_2_.9) | copy-start | bytes 6291460
  106.2 2.8 %collective-permute-start.29 = (bf16[256,2176]{1,0:T(8,128)(2,1)S(1)}, bf16[256,2176]{1,0:T(8,128)(2,1)S(1)}, u32[]{:S(2)}, u32[]{:S(2)}) collective-permute-start(bf16[256,2176]{1,0:T(8,128)(2,1)S(1)} %join.17.refs_0_.refs_1_), channel_id=1, source_target_pairs={{0,1},{1,0},{2,3},{3,2},{4,5},{5,4},{6,7},{7,6},{8,9},{9,8},{10,11... | collective-permute-start | bytes 3342344 | tf_op jit(solution)/shard_map/ppermute | solution.py:535

commit v4 on v3

--- a/solution.py
+++ b/solution.py
@@ -38,7 +38,6 @@
     ]
     specs += [pl.BlockSpec(memory_space=pl.ANY)] * len(deps)
     count = len(args)
-    us = COSTS.get(name, us)
 
     def run(*refs):
         kernel(*refs[:count], *refs[count + len(deps) :])
@@ -534,8 +533,8 @@
         pairs = flips(self.size, *step)
         self.other = [lax.ppermute(v, ("batch", "seq"), pairs) for v in value]
 
-    def turn(self, *deps):
-        result = self.done(*deps)
+    def turn(self, us, *deps):
+        result = self.done(us, *deps)
         if self.at < len(self.phases):
             self.start()
         return result
@@ -543,7 +542,7 @@
     def left(self):
         return len(self.phases) - self.at
 
-    def done(self, *deps):
+    def done(self, us, *deps):
         own, other = self.own, self.other
         rows, cols = sum(v.shape[0] for v in own), own[0].shape[1]
         kind, step = self.phases[self.at]
@@ -553,22 +552,22 @@
                 return other[0]
             self.own = call(
                 partial(join, step), [((2 * rows, cols), bf16)], *own, *other,
-                deps=deps, name="join",
+                deps=deps, name="join", us=us,
             )
         elif self.phases[self.at][0] == "halve":
             half = ((rows // 2, cols), bf16)
             keep, send = call(
                 partial(add_split, self.phases[self.at][1]), [half, half], *own, *other,
-                deps=deps, name="add_split",
+                deps=deps, name="add_split", us=us,
             )
             self.own, self.away = [keep], [send]
         else:
-            self.own = call(add, [((rows, cols), bf16)], *own, *other, deps=deps, name="add")
+            self.own = call(add, [((rows, cols), bf16)], *own, *other, deps=deps, name="add", us=us)
         return self.own[0]
 
 
-COSTS = {"add_split": 6, "add": 6, "join": 6, "spacer": 10, "mid_back": 0.5, "attend_back": 20, "feed_forward": 1, "project_back": 2, "tokens_back": 20}
-PLAN = "ff up - - sD sU D mid U ab pb sR D U R D U U D U R D R D R U D U R D - R U D tb R U ob R R"
+PLAN = ["ff", "up", "sD", "-", "sU", "D", "mid", "U", "ab", "pb", "sR", "D", "U", "R", "D", "U", "U", "D", "U", "R", "D", "R", "D", "U", "R", "D", "U", "R", "D", "R", "R", "D", "ob", "U", "U", "tb", "R", "R"]
+COSTS = [1, 0.5, 0, 10, 0, 6, 0.5, 6, 20, 2, 0, 6, 6, 6, 8, 6, 8, 6, 6, 6, 6, 6, 8, 6, 6, 6, 6, 6, 6, 40, 6, 6, 0.5, 6, 6, 20, 6, 6]
 ORDERS = {"D": ["xyz", "yxz"], "U": ["xzy", "yxz"], "R": ["xyz", "yxz"]}
 
 
@@ -632,7 +631,7 @@
             feed_forward,
             [flat32, flat, ((span, ff), bf16), ((span, ff), bf16), half, half],
             attended, tokens, w_out, gain2, bias2, w_up, d_hidden, d_ffn,
-            scratch=[pltpu.VMEM((ff, width), bf16)], name="feed_forward",
+            scratch=[pltpu.VMEM((ff, width), bf16)], name="feed_forward", us=state["cost"],
         )
         state.update(mid=mid, normed2=normed2, hidden=hidden, d_up=d_up)
         state["D"] = [keep], [send]
@@ -642,7 +641,7 @@
         half = ((ff // 2, width), bf16)
         keep, send = call(
             up_back, [half, half], state["normed2"], state["d_up"],
-            deps=(step, recv_hat), scratch=[pltpu.VMEM((ff, width), bf16)], name="up_back",
+            deps=(step, recv_hat), scratch=[pltpu.VMEM((ff, width), bf16)], name="up_back", us=state["cost"],
         )
         state["U"] = [keep], [send]
         return send
@@ -653,7 +652,7 @@
             mid_back,
             [flat32, flat, square, ((8, width), f32)],
             state["mid"], state["d_up"], w_up, gain2, d_ffn, attended, w_out,
-            deps=(step,), name="mid_back",
+            deps=(step,), name="mid_back", us=state["cost"],
         )
         state.update(d_mid=d_mid, d_attended=d_attended, grad_out=grad_out, grad_norm=grad_norm)
         return d_attended
@@ -665,7 +664,7 @@
             queries, kv, coarse, recv, probs, state["d_attended"],
             deps=(step,),
             scratch=[pltpu.VMEM((span + BLOCK, 2 * width), f32), pltpu.VMEM((coarse_rows, 2 * width), f32)],
-            name="attend_back", limit=16,
+            name="attend_back", us=state["cost"], limit=16,
         )
         state["lent"] = lent
         return lent
@@ -676,7 +675,7 @@
             project_back,
             [flat32, ((edge_rows, width), bf16)] + [piece] * (2 * PIECES),
             state["d_proj"], state["lent"], recv_hat, normed1, w_qkv, tokens, state["grad_norm"], state["grad_out"], gain1, bias1,
-            deps=(step,), scratch=[pltpu.VMEM((width, 4 * width + 128), bf16)], name="project_back",
+            deps=(step,), scratch=[pltpu.VMEM((width, 4 * width + 128), bf16)], name="project_back", us=state["cost"],
         )
         state["R"] = halved[:PIECES], halved[PIECES:]
         state["back"] = lax.ppermute(edge_back, "seq", [(b, a) for a, b in onward])
@@ -684,14 +683,14 @@
 
     def run_ob(step):
         state["result"], token = call(
-            output, [flat, mark], state["mid"], state["hidden"], w_down, deps=(step,), name="output",
+            output, [flat, mark], state["mid"], state["hidden"], w_down, deps=(step,), name="output", us=state["cost"],
         )
         return token
 
     def run_tb(step):
         state["d_tokens"], token = call(
             tokens_back, [flat, mark], state["d_normed"], state["back"], tokens, gain1, state["d_mid"],
-            deps=(step,), name="tokens_back",
+            deps=(step,), name="tokens_back", us=state["cost"],
         )
         return token
 
@@ -711,7 +710,7 @@
         if half == 0:
             *ends[key], token = call(
                 partial(kernel, 0), outs + [mark], mine, far_out=far_out, deps=(step,), scratch=scratch,
-                name=name, limit=12,
+                name=name, us=state["cost"], limit=12,
             )
             return token
         first = list(sums[key].own) if small else []
@@ -720,21 +719,22 @@
         *ends[key], token = call(
             partial(kernel, 1), outs + small + [mark], mine, *first, *before,
             far=tuple(range(at, at + len(before))), far_out=far_out, scratch=scratch,
-            alias={at + i: i for i in range(len(before))}, name=name, limit=12,
+            alias={at + i: i for i in range(len(before))}, name=name, us=state["cost"], limit=12,
         )
         return token
 
     kernels = dict(ff=run_ff, up=run_up, mid=run_mid, ab=run_ab, pb=run_pb, ob=run_ob, tb=run_tb)
     def turn(key, step):
-        step = sums[key].turn(step)
+        step = sums[key].turn(state["cost"], step)
         if sums[key].left() <= 1:
             step = finish(key, 1 - sums[key].left(), step, step)
         return step
 
     step = None
-    for token in PLAN.split():
+    for token, cost in zip(PLAN, COSTS):
+        state["cost"] = cost
         if token == "-":
-            (step,) = call(spacer, [mark], deps=(step,), name="spacer", us=100)
+            (step,) = call(spacer, [mark], deps=(step,), name="spacer", us=cost)
         elif token in kernels:
             step = kernels[token](step)
         elif token[0] == "s":

time: 112 us -> 107 us (0.955)
  waiting for transfers between devices: 39.2 us -> 36.5 us
  starting transfers between devices: 30.5 us -> 27.8 us
  Pallas kernels: 36.3 us -> 37.7 us
    ppermute x27, starting transfers between devices: 29.7 us -> 27 us  [start(): self.other = [lax.ppermute(v, ('batch', 'seq'), pairs) for v in value]]
    ppermute x27, waiting for transfers between devices: 36.5 us -> 33.8 us  [start(): self.other = [lax.ppermute(v, ('batch', 'seq'), pairs) for v in value]]
    pallas_call x45 -> x43, Pallas kernels: 36.3 us -> 37.7 us  [call(): pl.pallas_call(run, out_shape=[jax.ShapeDtypeStruct(s, d) for s, d in out...]
  transfers between devices with their start and end apart: 30 -> 30, of which waited for: 17 -> 19; matrix products, arithmetic and copies ran while one was open for 0% -> 0% of each run, Pallas kernels for 27% -> 30%
where the time goes in v4:
time: 107 us
  Pallas kernels  37.7 us (35%)
  waiting for transfers between devices  36.5 us (34%)
  starting transfers between devices  27.8 us (26%)
  local copies, waits for them, and re-layouts  3.12 us (3%)
  between operations  2.11 us (2%)
    pallas_call x43, Pallas kernels, call(): pl.pallas_call(run, out_shape=[jax.ShapeDtypeStruct(s, d) for s, d in out...  37.7 us
    ppermute x27, waiting for transfers between devices, start(): self.other = [lax.ppermute(v, ('batch', 'seq'), pairs) for v in value]  33.8 us
    ppermute x27, starting transfers between devices, start(): self.other = [lax.ppermute(v, ('batch', 'seq'), pairs) for v in value]  27 us
    unnamed x24, local copies, waits for them, and re-layouts  3.12 us
    ppermute x1, waiting for transfers between devices, body(): recv = lax.ppermute(edge, 'seq', onward)  2.63 us
  transfers between devices with their start and end apart: 30, of which 19 were waited for; matrix products, arithmetic and copies ran while one was open for 0% of the time, Pallas kernels for 30%

profile of v4, /device:TPU:0, one launch (start us, length us, event | category | flops | bytes accessed | tf_op | source)
XLA Modules:
  0.0 107.2 jit_solution(2376045332595547960)
XLA Ops:
  0.7 1.0 copy-done.5
  1.7 0.3 standardize.1.refs_0_.refs_4_
  2.0 1.1 %copy-done.4 = bf16[512,1536]{1,0:T(8,128)(2,1)S(1)} copy-done((bf16[512,1536]{1,0:T(8,128)(2,1)S(1)}, bf16[512,1536]{1,0:T(8,128)(2,1)}, u32[]{:S(2)}) %copy-start.4) | copy-done | bytes 1572888
  3.1 1.2 %project.1 = (bf16[512,512]{1,0:T(8,128)(2,1)S(1)}, bf16[512,1024]{1,0:T(8,128)(2,1)S(1)}, bf16[496,1024]{1,0:T(8,128)(2,1)S(1)}, bf16[96,1024]{1,0:T(8,128)(2,1)S(1)}) custom-call(f32[512,512]{1,0:T(8,128)S(1)} %standardize.1.refs_0_.refs_4_, bf16[512]{0:T(512)(128)(2,1)S(1)} %copy-done.11, bf16[512]{0:T(512)(128)(2,1)S(1)} %copy-done.10, ...), custom_call_target="tpu_custom_call" | custom-call | flops 3449999872 | bytes 65536 | tf_op jit(solution)/shard_map/project/pallas_call | solution.py:45
  4.4 0.5 collective-permute-start
  5.8 0.4 project_q.1.refs_3_.refs_0_
  6.3 1.3 %hidden_back.1 = (bf16[512,512]{1,0:T(8,128)(2,1)S(1)}, f32[512,2048]{1,0:T(8,128)S(1)}) custom-call(s32[1]{0:T(128)S(6)} %copy.29.refs_0_, bf16[512,512]{1,0:T(8,128)(2,1)S(1)} %bitcast.8, bf16[2048,512]{1,0:T(8,128)(2,1)S(1)} %copy-done.1, bf16[512,512]{1,0:T(8,128)(2,1)S(1)} %project_q.1.refs_3_.refs_0_), custom_call_target="tpu_custom_call" | custom-call | flops 230000000 | bytes 65536 | tf_op jit(solution)/shard_map/hidden_back/pallas_call | solution.py:45
  7.6 2.6 %collective-permute-done.refs_3_ = bf16[96,1024]{1,0:T(8,128)(2,1)S(1)} collective-permute-done((bf16[96,1024]{1,0:T(8,128)(2,1)S(1)}, bf16[96,1024]{1,0:T(8,128)(2,1)S(1)}, u32[]{:S(2)}, u32[]{:S(2)}) %collective-permute-start) | collective-permute-done | bytes 196640 | tf_op jit(solution)/shard_map/ppermute | solution.py:613
  10.2 2.2 %attend.1 = (bf16[512,512]{1,0:T(8,128)(2,1)S(1)}, bf16[4096,128]{1,0:T(8,128)(2,1)S(1)}, bf16[96,512]{1,0:T(8,128)(2,1)S(1)}) custom-call(bf16[512,512]{1,0:T(8,128)(2,1)S(1)} %project_q.1.refs_3_.refs_0_, bf16[512,1024]{1,0:T(8,128)(2,1)S(1)} %get-tuple-element.75.refs_1_, bf16[496,1024]{1,0:T(8,128)(2,1)S(1)} %get-tuple-element.76.refs_2_, ...), custom_call_target="tpu_custom_call" | custom-call | flops 575000000 | bytes 65536 | tf_op jit(solution)/shard_map/attend/pallas_call | solution.py:45
  12.5 0.2 collective-permute-start.2
  12.8 4.9 %feed_forward.1 = (f32[512,512]{1,0:T(8,128)S(1)}, bf16[512,512]{1,0:T(8,128)(2,1)S(1)}, bf16[512,2048]{1,0:T(8,128)(2,1)S(1)}, bf16[512,2048]{1,0:T(8,128)(2,1)...) custom-call(bf16[512,512]{1,0:T(8,128)(2,1)S(1)} %get-tuple-element.79.refs_0_.refs_5_, ...), custom_call_target="tpu_custom_call" | custom-call | flops 1150000000 | bytes 65536 | tf_op jit(solution)/shard_map/feed_forward/pallas_call | solution.py:45
  17.7 2.4 %collective-permute-start.1 = (bf16[1024,512]{1,0:T(8,128)(2,1)S(1)}, bf16[1024,512]{1,0:T(8,128)(2,1)S(1)}, u32[]{:S(2)}, u32[]{:S(2)}) collective-permute-start(bf16[1024,512]{1,0:T(8,128)(2,1)S(1)} %get-tuple-element.84.refs_2_), channel_id=1, source_target_pairs={{0,1},{1,0},{2,3},{3,2},{4,5},{5,4},{6,7},{7,6},{8,9},{9,8},{10,11... | collective-permute-start | bytes 3145736 | tf_op jit(solution)/shard_map/ppermute | solution.py:534
  20.2 1.5 %up_back.1 = (bf16[1024,512]{1,0:T(8,128)(2,1)S(1)}, bf16[1024,512]{1,0:T(8,128)(2,1)S(1)}) custom-call(bf16[512,512]{1,0:T(8,128)(2,1)S(1)} %get-tuple-element.85.refs_0_, bf16[512,2048]{1,0:T(8,128)(2,1)S(1)} %get-tuple-element.86.refs_1_, bf16[1024,512]{1,0:T(8,128)(2,1)S(1)} %get-tuple-element.84.refs_2_, ...), custom_call_target="tpu_custom_call" | custom-call | flops 575000000 | bytes 65536 | tf_op jit(solution)/shard_map/up_back/pallas_call | solution.py:45
  21.8 0.6 collective-permute-done.1.refs_1_
  22.5 0.2 add_split.9
  22.6 1.6 %collective-permute-start.3 = (bf16[512,512]{1,0:T(8,128)(2,1)S(1)}, bf16[512,512]{1,0:T(8,128)(2,1)S(1)}, u32[]{:S(2)}, u32[]{:S(2)}) collective-permute-start(bf16[512,512]{1,0:T(8,128)(2,1)S(1)} %get-tuple-element.90), channel_id=1, source_target_pairs={{0,4},{1,3},{2,6},{3,1},{4,0},{5,7},{6,2},{7,5},{8,12},{9,11},{10,... | collective-permute-start | bytes 1572872 | tf_op jit(solution)/shard_map/ppermute | solution.py:534
  24.2 2.4 %mid_back.1 = (f32[512,512]{1,0:T(8,128)S(1)}, bf16[512,512]{1,0:T(8,128)(2,1)S(1)}, bf16[512,512]{1,0:T(8,128)(2,1)S(1)}, f32[8,512]{1,0:T(8,128)S(1)}) custom-call(f32[512,512]{1,0:T(8,128)S(1)} %get-tuple-element.81.refs_0_, bf16[512,2048]{1,0:T(8,128)(2,1)S(1)} %get-tuple-element.86.refs_1_, bf16[512,2048]{1,0:T(8,128)(2,1)S(1)} %copy-done, ...), custom_call_target="tpu_custom_call" | custom-call | flops 575000000 | bytes 65536 | tf_op jit(solution)/shard_map/mid_back/pallas_call | solution.py:45
  26.6 0.1 add_split.10
  26.7 0.6 collective-permute-start.7
  27.3 3.8 %attend_back.1 = (bf16[512,1536]{1,0:T(8,128)(2,1)S(1)}, bf16[96,1024]{1,0:T(8,128)(2,1)S(1)}) custom-call(bf16[512,512]{1,0:T(8,128)(2,1)S(1)} %project_q.1.refs_3_.refs_0_, bf16[512,1024]{1,0:T(8,128)(2,1)S(1)} %get-tuple-element.75.refs_1_, bf16[496,1024]{1,0:T(8,128)(2,1)S(1)} %get-tuple-element.76.refs_2_, ...), custom_call_target="tpu_custom_call" | custom-call | flops 23000000512 | bytes 65536 | tf_op jit(solution)/shard_map/attend_back/pallas_call | solution.py:45
  31.1 3.5 %project_back.1 = (f32[512,512]{1,0:T(8,128)S(1)}, bf16[96,512]{1,0:T(8,128)(2,1)}, bf16[256,2176]{1,0:T(8,128)(2,1)S(1)}, bf16[256,2176]{1,0:T(8,128)(2,1)S(1)}) custom-call(bf16[512,1536]{1,0:T(8,128)(2,1)S(1)} %get-tuple-element.95.refs_0_, bf16[96,1024]{1,0:T(8,128)(2,1)S(1)} %get-tuple-element.96.refs_1_.refs_10_, ...), custom_call_target="tpu_custom_call" | custom-call | flops 2300000000 | bytes 65536 | tf_op jit(solution)/shard_map/project_back/pallas_call | solution.py:45
  34.6 0.3 collective-permute-start.5
  35.0 2.5 %collective-permute-done.7.refs_1_ = bf16[512,512]{1,0:T(8,128)(2,1)S(1)} collective-permute-done((bf16[512,512]{1,0:T(8,128)(2,1)S(1)}, bf16[512,512]{1,0:T(8,128)(2,1)S(1)}, u32[]{:S(2)}, u32[]{:S(2)}) %collective-permute-start.7) | collective-permute-done | bytes 524320 | tf_op jit(solution)/shard_map/ppermute | solution.py:534
  37.5 1.6 %collective-permute-start.9 = (bf16[256,512]{1,0:T(8,128)(2,1)S(1)}, bf16[256,512]{1,0:T(8,128)(2,1)S(1)}, u32[]{:S(2)}, u32[]{:S(2)}) collective-permute-start(bf16[256,512]{1,0:T(8,128)(2,1)S(1)} %get-tuple-element.108), channel_id=1, source_target_pairs={{0,8},{1,5},{2,10},{3,7},{4,12},{5,1},{6,14},{7,3},{8,0},{9,13},{1... | collective-permute-start | bytes 786440 | tf_op jit(solution)/shard_map/ppermute | solution.py:534
  39.3 1.8 %collective-permute-done.5.refs_1_ = bf16[256,512]{1,0:T(8,128)(2,1)S(1)} collective-permute-done((bf16[256,512]{1,0:T(8,128)(2,1)S(1)}, bf16[256,512]{1,0:T(8,128)(2,1)S(1)}, u32[]{:S(2)}, u32[]{:S(2)}) %collective-permute-start.5) | collective-permute-done | bytes 262176 | tf_op jit(solution)/shard_map/ppermute | solution.py:534
  41.1 2.9 %collective-permute-done.9.refs_1_ = bf16[256,512]{1,0:T(8,128)(2,1)S(1)} collective-permute-done((bf16[256,512]{1,0:T(8,128)(2,1)S(1)}, bf16[256,512]{1,0:T(8,128)(2,1)S(1)}, u32[]{:S(2)}, u32[]{:S(2)}) %collective-permute-start.9) | collective-permute-done | bytes 262176 | tf_op jit(solution)/shard_map/ppermute | solution.py:534
  44.0 2.7 %collective-permute-start.10 = (bf16[128,512]{1,0:T(8,128)(2,1)S(1)}, bf16[128,512]{1,0:T(8,128)(2,1)S(1)}, u32[]{:S(2)}, u32[]{:S(2)}) collective-permute-start(bf16[128,512]{1,0:T(8,128)(2,1)S(1)} %get-tuple-element.110), channel_id=1, source_target_pairs={{0,16},{1,9},{2,18},{3,11},{4,20},{5,13},{6,22},{7,15},{8,24},{9,1... | collective-permute-start | bytes 393224 | tf_op jit(solution)/shard_map/ppermute | solution.py:534
  46.7 1.6 %collective-permute-start.8 = (bf16[128,512]{1,0:T(8,128)(2,1)S(1)}, bf16[128,512]{1,0:T(8,128)(2,1)S(1)}, u32[]{:S(2)}, u32[]{:S(2)}) collective-permute-start(bf16[128,512]{1,0:T(8,128)(2,1)S(1)} %get-tuple-element.107), channel_id=1, source_target_pairs={{0,8},{1,9},{2,10},{3,11},{4,12},{5,13},{6,14},{7,15},{8,0},{9,1},... | collective-permute-start | bytes 393224 | tf_op jit(solution)/shard_map/ppermute | solution.py:534
  48.3 1.5 %collective-permute-start.12 = (bf16[128,2176]{1,0:T(8,128)(2,1)S(1)}, bf16[128,2176]{1,0:T(8,128)(2,1)S(1)}, u32[]{:S(2)}, u32[]{:S(2)}) collective-permute-start(bf16[128,2176]{1,0:T(8,128)(2,1)S(1)} %get-tuple-element.111), channel_id=1, source_target_pairs={{0,4},{1,3},{2,6},{3,1},{4,0},{5,7},{6,2},{7,5},{8,12},{9,11},{10,... | collective-permute-start | bytes 1671176 | tf_op jit(solution)/shard_map/ppermute | solution.py:534
  49.7 0.5 collective-permute-done.10.refs_1_
  50.3 0.1 collective-permute-start.13
  50.4 3.1 %collective-permute-done.8.refs_1_ = bf16[128,512]{1,0:T(8,128)(2,1)S(1)} collective-permute-done((bf16[128,512]{1,0:T(8,128)(2,1)S(1)}, bf16[128,512]{1,0:T(8,128)(2,1)S(1)}, u32[]{:S(2)}, u32[]{:S(2)}) %collective-permute-start.8) | collective-permute-done | bytes 131104 | tf_op jit(solution)/shard_map/ppermute | solution.py:534
  53.5 2.3 %collective-permute-start.11 = (bf16[128,512]{1,0:T(8,128)(2,1)S(1)}, bf16[128,512]{1,0:T(8,128)(2,1)S(1)}, u32[]{:S(2)}, u32[]{:S(2)}) collective-permute-start(bf16[128,512]{1,0:T(8,128)(2,1)S(1)} %add.7.refs_2_.refs_0_), channel_id=1, source_target_pairs={{0,16},{1,17},{2,18},{3,19},{4,20},{5,21},{6,22},{7,23},{8,24},{9,... | collective-permute-start | bytes 393224 | tf_op jit(solution)/shard_map/ppermute | solution.py:534
  55.8 0.9 collective-permute-done.13.refs_1_
  56.8 2.6 %collective-permute-start.18 = (bf16[128,512]{1,0:T(8,128)(2,1)S(1)}, bf16[128,512]{1,0:T(8,128)(2,1)S(1)}, u32[]{:S(2)}, u32[]{:S(2)}) collective-permute-start(bf16[128,512]{1,0:T(8,128)(2,1)S(1)} %add.8.refs_2_.refs_0_), channel_id=1, source_target_pairs={{0,16},{1,9},{2,18},{3,11},{4,20},{5,13},{6,22},{7,15},{8,24},{9,1... | collective-permute-start | bytes 393224 | tf_op jit(solution)/shard_map/ppermute | solution.py:534
  59.5 0.6 collective-permute-start.15
  60.1 2.3 %collective-permute-done.11.refs_1_ = bf16[128,512]{1,0:T(8,128)(2,1)S(1)} collective-permute-done((bf16[128,512]{1,0:T(8,128)(2,1)S(1)}, bf16[128,512]{1,0:T(8,128)(2,1)S(1)}, u32[]{:S(2)}, u32[]{:S(2)}) %collective-permute-start.11) | collective-permute-done | bytes 131104 | tf_op jit(solution)/shard_map/ppermute | solution.py:534
  62.4 3.6 %collective-permute-done.15.refs_1_ = bf16[64,2176]{1,0:T(8,128)(2,1)S(1)} collective-permute-done((bf16[64,2176]{1,0:T(8,128)(2,1)S(1)}, bf16[64,2176]{1,0:T(8,128)(2,1)S(1)}, u32[]{:S(2)}, u32[]{:S(2)}) %collective-permute-start.15) | collective-permute-done | bytes 278560 | tf_op jit(solution)/shard_map/ppermute | solution.py:534
  66.1 1.4 %collective-permute-start.17 = (bf16[32,2176]{1,0:T(8,128)(2,1)S(1)}, bf16[32,2176]{1,0:T(8,128)(2,1)S(1)}, u32[]{:S(2)}, u32[]{:S(2)}) collective-permute-start(bf16[32,2176]{1,0:T(8,128)(2,1)S(1)} %get-tuple-element.115), channel_id=1, source_target_pairs={{0,8},{1,9},{2,10},{3,11},{4,12},{5,13},{6,14},{7,15},{8,0},{9,1},... | collective-permute-start | bytes 417800 | tf_op jit(solution)/shard_map/ppermute | solution.py:534
  67.5 0.5 collective-permute-done.14.refs_1_
  68.2 0.7 collective-permute-start.21
  68.9 2.3 %collective-permute-done.17.refs_1_ = bf16[32,2176]{1,0:T(8,128)(2,1)S(1)} collective-permute-done((bf16[32,2176]{1,0:T(8,128)(2,1)S(1)}, bf16[32,2176]{1,0:T(8,128)(2,1)S(1)}, u32[]{:S(2)}, u32[]{:S(2)}) %collective-permute-start.17) | collective-permute-done | bytes 139296 | tf_op jit(solution)/shard_map/ppermute | solution.py:534
  71.2 0.6 collective-permute-start.20
  71.9 3.0 %collective-permute-done.16.refs_1_ = bf16[256,512]{1,0:T(8,128)(2,1)S(1)} collective-permute-done((bf16[256,512]{1,0:T(8,128)(2,1)S(1)}, bf16[256,512]{1,0:T(8,128)(2,1)S(1)}, u32[]{:S(2)}, u32[]{:S(2)}) %collective-permute-start.16) | collective-permute-done | bytes 262176 | tf_op jit(solution)/shard_map/ppermute | solution.py:534
  74.9 1.5 %collective-permute-start.19 = (bf16[512,512]{1,0:T(8,128)(2,1)S(1)}, bf16[512,512]{1,0:T(8,128)(2,1)S(1)}, u32[]{:S(2)}, u32[]{:S(2)}) collective-permute-start(bf16[512,512]{1,0:T(8,128)(2,1)S(1)} %join.11.refs_2_.refs_0_), channel_id=1, source_target_pairs={{0,4},{1,3},{2,6},{3,1},{4,0},{5,7},{6,2},{7,5},{8,12},{9,11},{10,... | collective-permute-start | bytes 1572872 | tf_op jit(solution)/shard_map/ppermute | solution.py:534
  76.4 1.3 %collective-permute-done.21.refs_1_ = bf16[256,512]{1,0:T(8,128)(2,1)S(1)} collective-permute-done((bf16[256,512]{1,0:T(8,128)(2,1)S(1)}, bf16[256,512]{1,0:T(8,128)(2,1)S(1)}, u32[]{:S(2)}, u32[]{:S(2)}) %collective-permute-start.21) | collective-permute-done | bytes 262176 | tf_op jit(solution)/shard_map/ppermute | solution.py:534
  77.7 1.2 %collective-permute-start.24 = (bf16[512,512]{1,0:T(8,128)(2,1)S(1)}, bf16[512,512]{1,0:T(8,128)(2,1)S(1)}, u32[]{:S(2)}, u32[]{:S(2)}) collective-permute-start(bf16[512,512]{1,0:T(8,128)(2,1)S(1)} %join.12.refs_2_.refs_0_), channel_id=1, source_target_pairs={{0,4},{1,3},{2,6},{3,1},{4,0},{5,7},{6,2},{7,5},{8,12},{9,11},{10,... | collective-permute-start | bytes 1572872 | tf_op jit(solution)/shard_map/ppermute | solution.py:534
  79.0 1.0 collective-permute-start.26
  80.0 4.1 %collective-permute-done.19.refs_1_ = bf16[512,512]{1,0:T(8,128)(2,1)S(1)} collective-permute-done((bf16[512,512]{1,0:T(8,128)(2,1)S(1)}, bf16[512,512]{1,0:T(8,128)(2,1)S(1)}, u32[]{:S(2)}, u32[]{:S(2)}) %collective-permute-start.19) | collective-permute-done | bytes 524320 | tf_op jit(solution)/shard_map/ppermute | solution.py:534
  84.3 1.4 %finish_down.2 = (f32[2048,512]{1,0:T(8,128)}, f32[8,128]{1,0:T(8,128)S(1)}) custom-call(bf16[1024,512]{1,0:T(8,128)(2,1)S(1)} %join.13.refs_0_.refs_1_, bf16[1024,512]{1,0:T(8,128)(2,1)S(1)} %join.13.refs_0_.refs_1_), custom_call_target="tpu_custom_call" | custom-call | flops 6899999744 | bytes 65536 | tf_op jit(solution)/shard_map/finish_down/pallas_call | solution.py:45
  85.8 1.1 %collective-permute-done.22.refs_0_ = bf16[1024,512]{1,0:T(8,128)(2,1)S(1)} collective-permute-done((bf16[1024,512]{1,0:T(8,128)(2,1)S(1)}, bf16[1024,512]{1,0:T(8,128)(2,1)S(1)}, u32[]{:S(2)}, u32[]{:S(2)}) %collective-permute-start.22) | collective-permute-done | bytes 1048608 | tf_op jit(solution)/shard_map/ppermute | solution.py:534
  87.0 1.4 %finish_down.3 = (f32[2048,512]{1,0:T(8,128)}, f32[8,128]{1,0:T(8,128)S(1)}) custom-call(bf16[1024,512]{1,0:T(8,128)(2,1)S(1)} %collective-permute-done.22.refs_0_, f32[2048,512]{1,0:T(8,128)} %get-tuple-element.116.refs_1_), custom_call_target="tpu_custom_call", output_to_operand_aliasing={{0}: (1, {})} | custom-call | flops 6899999744 | bytes 65536 | tf_op jit(solution)/shard_map/finish_down/pallas_call | solution.py:45
  88.3 1.0 copy-done.2
  89.3 2.0 %output.1 = (bf16[512,512]{1,0:T(8,128)(2,1)}, f32[8,128]{1,0:T(8,128)S(1)}) custom-call(f32[512,512]{1,0:T(8,128)S(1)} %get-tuple-element.81.refs_0_, bf16[512,2048]{1,0:T(8,128)(2,1)S(1)} %get-tuple-element.82.refs_1_, bf16[2048,512]{1,0:T(8,128)(2,1)S(1)} %copy-done.2, f32[8,128]{1,0:T(8,128)S(1)} %get-tuple-element.117.refs_3_), custom_call_target="tpu_custom_call" | custom-call | flops 575000000 | bytes 65536 | tf_op jit(solution)/shard_map/output/pallas_call | solution.py:45
  91.4 0.6 collective-permute-start.25
  92.0 0.4 collective-permute-done.27.refs_1_
  92.4 1.5 %collective-permute-start.28 = (bf16[128,2176]{1,0:T(8,128)(2,1)S(1)}, bf16[128,2176]{1,0:T(8,128)(2,1)S(1)}, u32[]{:S(2)}, u32[]{:S(2)}) collective-permute-start(bf16[128,2176]{1,0:T(8,128)(2,1)S(1)} %join.16.refs_0_), channel_id=1, source_target_pairs={{0,4},{1,3},{2,6},{3,1},{4,0},{5,7},{6,2},{7,5},{8,12},{9,11},{10,... | collective-permute-start | bytes 1671176 | tf_op jit(solution)/shard_map/ppermute | solution.py:534
  93.9 2.0 %finish_up.2 = (f32[512,2048]{1,0:T(8,128)}, f32[8,128]{1,0:T(8,128)}) custom-call(bf16[1024,512]{1,0:T(8,128)(2,1)S(1)} %join.14.refs_0_.refs_1_, bf16[1024,512]{1,0:T(8,128)(2,1)S(1)} %join.14.refs_0_.refs_1_), custom_call_target="tpu_custom_call" | custom-call | flops 6899999744 | bytes 65536 | tf_op jit(solution)/shard_map/finish_up/pallas_call | solution.py:45
  95.9 1.4 %finish_up.3 = (f32[512,2048]{1,0:T(8,128)}, f32[8,128]{1,0:T(8,128)S(1)}) custom-call(bf16[1024,512]{1,0:T(8,128)(2,1)S(1)} %collective-permute-done.25.refs_0_, f32[512,2048]{1,0:T(8,128)} %get-tuple-element.123.refs_1_), custom_call_target="tpu_custom_call", output_to_operand_aliasing={{0}: (1, {})} | custom-call | flops 6899999744 | bytes 65536 | tf_op jit(solution)/shard_map/finish_up/pallas_call | solution.py:45
  97.3 2.5 %tokens_back.1 = (bf16[512,512]{1,0:T(8,128)(2,1)}, f32[8,128]{1,0:T(8,128)S(1)}) custom-call(f32[512,512]{1,0:T(8,128)S(1)} %get-tuple-element.119.refs_0_, bf16[96,512]{1,0:T(8,128)(2,1)} %collective-permute-done.23.refs_1_, bf16[512,512]{1,0:T(8,128)(2,1)S(1)} %bitcast.7, bf16[512]{0:T(512)(128)(2,1)S(1)} %copy-done.11, ...), custom_call_target="tpu_custom_call" | custom-call | flops 23000000512 | bytes 65536 | tf_op jit(solution)/shard_map/tokens_back/pallas_call | solution.py:45
  99.8 2.2 %collective-permute-done.28.refs_1_ = bf16[128,2176]{1,0:T(8,128)(2,1)S(1)} collective-permute-done((bf16[128,2176]{1,0:T(8,128)(2,1)S(1)}, bf16[128,2176]{1,0:T(8,128)(2,1)S(1)}, u32[]{:S(2)}, u32[]{:S(2)}) %collective-permute-start.28) | collective-permute-done | bytes 557088 | tf_op jit(solution)/shard_map/ppermute | solution.py:534
  102.2 2.0 %finish_rest.2 = (f32[512,1536]{1,0:T(8,128)}, f32[512,512]{1,0:T(8,128)}, f32[8,128]{1,0:T(8,128)}) custom-call(bf16[256,2176]{1,0:T(8,128)(2,1)S(1)} %join.17.refs_0_.refs_1_, bf16[256,2176]{1,0:T(8,128)(2,1)S(1)} %join.17.refs_0_.refs_1_), custom_call_target="tpu_custom_call" | custom-call | flops 6899999744 | bytes 65536 | tf_op jit(solution)/shard_map/finish_rest/pallas_call | solution.py:45
  104.2 0.7 collective-permute-done.29.refs_0_
  104.9 2.0 %finish_rest.3 = (f32[512,1536]{1,0:T(8,128)}, f32[512,512]{1,0:T(8,128)}, f32[512]{0:T(512)}, f32[512]{0:T(512)}, f32[512]{0:T(512)}, /*index=5*/f32[512]{0:T(512)}, f32[8,128]{1,0:T(8,128)}) custom-call(bf16[256,2176]{1,0:T(8,128)(2,1)S(1)} %collective-permute-done.29.refs_0_, ...), custom_call_target="tpu_custom_call", output_to_operand_aliasing={{0}: (2, {}), {1}: (3, {})} | custom-call | flops 6899999744 | bytes 65536 | tf_op jit(solution)/shard_map/finish_rest/pallas_call | solution.py:45
  (63 shorter events, 1.6 us)
Async XLA Ops:
  0.6 1.0 copy-start.5
  1.7 1.4 %copy-start.4 = (bf16[512,1536]{1,0:T(8,128)(2,1)S(1)}, bf16[512,1536]{1,0:T(8,128)(2,1)}, u32[]{:S(2)}) copy-start(bf16[512,1536]{1,0:T(8,128)(2,1)} %refs_4_.3) | copy-start | bytes 4718596
  1.7 1.4 %copy-start.10 = (bf16[512]{0:T(512)(128)(2,1)S(1)}, bf16[512]{0:T(512)(128)(2,1)}, u32[]{:S(2)}) copy-start(bf16[512]{0:T(512)(128)(2,1)} %refs_9_.1) | copy-start | bytes 3076
  1.7 1.4 %copy-start.11 = (bf16[512]{0:T(512)(128)(2,1)S(1)}, bf16[512]{0:T(512)(128)(2,1)}, u32[]{:S(2)}) copy-start(bf16[512]{0:T(512)(128)(2,1)} %refs_3_.7) | copy-start | bytes 3076
  4.4 1.9 %copy-start.1 = (bf16[2048,512]{1,0:T(8,128)(2,1)S(1)}, bf16[2048,512]{1,0:T(8,128)(2,1)}, u32[]{:S(2)}) copy-start(bf16[2048,512]{1,0:T(8,128)(2,1)} %refs_2_.9) | copy-start | bytes 6291460
  4.4 1.9 %copy-start.7 = (bf16[1,512,512]{2,1,0:T(8,128)(2,1)S(1)}, bf16[1,512,512]{2,1,0:T(8,128)(2,1)}, u32[]{:S(2)}) copy-start(bf16[1,512,512]{2,1,0:T(8,128)(2,1)} %param.13) | copy-start | bytes 1572868
  4.4 5.8 %collective-permute-start = (bf16[96,1024]{1,0:T(8,128)(2,1)S(1)}, bf16[96,1024]{1,0:T(8,128)(2,1)S(1)}, u32[]{:S(2)}, u32[]{:S(2)}) collective-permute-start(bf16[96,1024]{1,0:T(8,128)(2,1)S(1)} %get-tuple-element.77), channel_id=1, source_target_pairs={{0,1},{1,2},{2,3},{3,0},{4,5},{5,6},{6,7},{7,4},{8,9},{9,10},{10,1... | collective-permute-start | bytes 589832 | tf_op jit(solution)/shard_map/ppermute | solution.py:613
  10.2 2.5 %copy-start = (bf16[512,2048]{1,0:T(8,128)(2,1)S(1)}, bf16[512,2048]{1,0:T(8,128)(2,1)}, u32[]{:S(2)}) copy-start(bf16[512,2048]{1,0:T(8,128)(2,1)} %refs_2_.8) | copy-start | bytes 6291460
  10.2 2.5 %copy-start.3 = (bf16[512,512]{1,0:T(8,128)(2,1)S(1)}, bf16[512,512]{1,0:T(8,128)(2,1)}, u32[]{:S(2)}) copy-start(bf16[512,512]{1,0:T(8,128)(2,1)} %refs_6_.1) | copy-start | bytes 1572868
  10.2 2.5 %copy-start.6 = (bf16[1,512,512]{2,1,0:T(8,128)(2,1)S(1)}, bf16[1,512,512]{2,1,0:T(8,128)(2,1)}, u32[]{:S(2)}) copy-start(bf16[1,512,512]{2,1,0:T(8,128)(2,1)} %param.11) | copy-start | bytes 1572868
  10.2 2.5 %copy-start.8 = (bf16[512]{0:T(512)(128)(2,1)S(1)}, bf16[512]{0:T(512)(128)(2,1)}, u32[]{:S(2)}) copy-start(bf16[512]{0:T(512)(128)(2,1)} %refs_3_.6) | copy-start | bytes 3076
  10.2 2.6 %copy-start.9 = (bf16[512]{0:T(512)(128)(2,1)S(1)}, bf16[512]{0:T(512)(128)(2,1)}, u32[]{:S(2)}) copy-start(bf16[512]{0:T(512)(128)(2,1)} %refs_4_.2) | copy-start | bytes 3076
  12.5 7.7 %collective-permute-start.2 = (bf16[96,512]{1,0:T(8,128)(2,1)S(1)}, bf16[96,512]{1,0:T(8,128)(2,1)S(1)}, u32[]{:S(2)}, u32[]{:S(2)}) collective-permute-start(bf16[96,512]{1,0:T(8,128)(2,1)S(1)} %get-tuple-element.87), channel_id=1, source_target_pairs={{0,1},{1,2},{2,3},{3,0},{4,5},{5,6},{6,7},{7,4},{8,9},{9,10},{10,1... | collective-permute-start | bytes 294920 | tf_op jit(solution)/shard_map/ppermute | solution.py:624
  17.7 4.7 %collective-permute-start.1 = (bf16[1024,512]{1,0:T(8,128)(2,1)S(1)}, bf16[1024,512]{1,0:T(8,128)(2,1)S(1)}, u32[]{:S(2)}, u32[]{:S(2)}) collective-permute-start(bf16[1024,512]{1,0:T(8,128)(2,1)S(1)} %get-tuple-element.84.refs_2_), channel_id=1, source_target_pairs={{0,1},{1,0},{2,3},{3,2},{4,5},{5,4},{6,7},{7,6},{8,9},{9,8},{10,11... | collective-permute-start | bytes 3145736 | tf_op jit(solution)/shard_map/ppermute | solution.py:534
  21.7 4.9 %collective-permute-start.4 = (bf16[1024,512]{1,0:T(8,128)(2,1)S(1)}, bf16[1024,512]{1,0:T(8,128)(2,1)S(1)}, u32[]{:S(2)}, u32[]{:S(2)}) collective-permute-start(bf16[1024,512]{1,0:T(8,128)(2,1)S(1)} %get-tuple-element.88.refs_0_), channel_id=1, source_target_pairs={{0,1},{1,0},{2,3},{3,2},{4,5},{5,4},{6,7},{7,6},{8,9},{9,8},{10,11... | collective-permute-start | bytes 3145736 | tf_op jit(solution)/shard_map/ppermute | solution.py:534
  22.6 12.0 %collective-permute-start.3 = (bf16[512,512]{1,0:T(8,128)(2,1)S(1)}, bf16[512,512]{1,0:T(8,128)(2,1)S(1)}, u32[]{:S(2)}, u32[]{:S(2)}) collective-permute-start(bf16[512,512]{1,0:T(8,128)(2,1)S(1)} %get-tuple-element.90), channel_id=1, source_target_pairs={{0,4},{1,3},{2,6},{3,1},{4,0},{5,7},{6,2},{7,5},{8,12},{9,11},{10,... | collective-permute-start | bytes 1572872 | tf_op jit(solution)/shard_map/ppermute | solution.py:534
  26.7 10.8 %collective-permute-start.7 = (bf16[512,512]{1,0:T(8,128)(2,1)S(1)}, bf16[512,512]{1,0:T(8,128)(2,1)S(1)}, u32[]{:S(2)}, u32[]{:S(2)}) collective-permute-start(bf16[512,512]{1,0:T(8,128)(2,1)S(1)} %get-tuple-element.103), channel_id=1, source_target_pairs={{0,4},{1,3},{2,6},{3,1},{4,0},{5,7},{6,2},{7,5},{8,12},{9,11},{10,... | collective-permute-start | bytes 1572872 | tf_op jit(solution)/shard_map/ppermute | solution.py:534
  34.6 4.6 %collective-permute-start.6 = (bf16[256,2176]{1,0:T(8,128)(2,1)S(1)}, bf16[256,2176]{1,0:T(8,128)(2,1)S(1)}, u32[]{:S(2)}, u32[]{:S(2)}) collective-permute-start(bf16[256,2176]{1,0:T(8,128)(2,1)S(1)} %get-tuple-element.99.refs_2_), channel_id=1, source_target_pairs={{0,1},{1,0},{2,3},{3,2},{4,5},{5,4},{6,7},{7,6},{8,9},{9,8},{10,11... | collective-permute-start | bytes 3342344 | tf_op jit(solution)/shard_map/ppermute | solution.py:534
  34.6 6.4 %collective-permute-start.5 = (bf16[256,512]{1,0:T(8,128)(2,1)S(1)}, bf16[256,512]{1,0:T(8,128)(2,1)S(1)}, u32[]{:S(2)}, u32[]{:S(2)}) collective-permute-start(bf16[256,512]{1,0:T(8,128)(2,1)S(1)} %get-tuple-element.101), channel_id=1, source_target_pairs={{0,2},{1,5},{2,0},{3,7},{4,6},{5,1},{6,4},{7,3},{8,10},{9,13},{10,... | collective-permute-start | bytes 786440 | tf_op jit(solution)/shard_map/ppermute | solution.py:534
  37.5 6.4 %collective-permute-start.9 = (bf16[256,512]{1,0:T(8,128)(2,1)S(1)}, bf16[256,512]{1,0:T(8,128)(2,1)S(1)}, u32[]{:S(2)}, u32[]{:S(2)}) collective-permute-start(bf16[256,512]{1,0:T(8,128)(2,1)S(1)} %get-tuple-element.108), channel_id=1, source_target_pairs={{0,8},{1,5},{2,10},{3,7},{4,12},{5,1},{6,14},{7,3},{8,0},{9,13},{1... | collective-permute-start | bytes 786440 | tf_op jit(solution)/shard_map/ppermute | solution.py:534
  44.0 6.3 %collective-permute-start.10 = (bf16[128,512]{1,0:T(8,128)(2,1)S(1)}, bf16[128,512]{1,0:T(8,128)(2,1)S(1)}, u32[]{:S(2)}, u32[]{:S(2)}) collective-permute-start(bf16[128,512]{1,0:T(8,128)(2,1)S(1)} %get-tuple-element.110), channel_id=1, source_target_pairs={{0,16},{1,9},{2,18},{3,11},{4,20},{5,13},{6,22},{7,15},{8,24},{9,1... | collective-permute-start | bytes 393224 | tf_op jit(solution)/shard_map/ppermute | solution.py:534
  46.7 50.6 %collective-permute-start.23 = (bf16[96,512]{1,0:T(8,128)(2,1)}, bf16[96,512]{1,0:T(8,128)(2,1)}, u32[]{:S(2)}, u32[]{:S(2)}) collective-permute-start(bf16[96,512]{1,0:T(8,128)(2,1)} %get-tuple-element.120), channel_id=1, source_target_pairs={{1,0},{2,1},{3,2},{0,3},{5,4},{6,5},{7,6},{4,7},{9,8},{10,9},{11,1... | collective-permute-start | bytes 294920 | tf_op jit(solution)/shard_map/ppermute | solution.py:681
  46.7 6.8 %collective-permute-start.8 = (bf16[128,512]{1,0:T(8,128)(2,1)S(1)}, bf16[128,512]{1,0:T(8,128)(2,1)S(1)}, u32[]{:S(2)}, u32[]{:S(2)}) collective-permute-start(bf16[128,512]{1,0:T(8,128)(2,1)S(1)} %get-tuple-element.107), channel_id=1, source_target_pairs={{0,8},{1,9},{2,10},{3,11},{4,12},{5,13},{6,14},{7,15},{8,0},{9,1},... | collective-permute-start | bytes 393224 | tf_op jit(solution)/shard_map/ppermute | solution.py:534
  48.3 11.1 %collective-permute-start.12 = (bf16[128,2176]{1,0:T(8,128)(2,1)S(1)}, bf16[128,2176]{1,0:T(8,128)(2,1)S(1)}, u32[]{:S(2)}, u32[]{:S(2)}) collective-permute-start(bf16[128,2176]{1,0:T(8,128)(2,1)S(1)} %get-tuple-element.111), channel_id=1, source_target_pairs={{0,4},{1,3},{2,6},{3,1},{4,0},{5,7},{6,2},{7,5},{8,12},{9,11},{10,... | collective-permute-start | bytes 1671176 | tf_op jit(solution)/shard_map/ppermute | solution.py:534
  50.3 6.5 %collective-permute-start.13 = (bf16[128,512]{1,0:T(8,128)(2,1)S(1)}, bf16[128,512]{1,0:T(8,128)(2,1)S(1)}, u32[]{:S(2)}, u32[]{:S(2)}) collective-permute-start(bf16[128,512]{1,0:T(8,128)(2,1)S(1)} %add.6.refs_2_.refs_0_), channel_id=1, source_target_pairs={{0,2},{1,17},{2,0},{3,19},{4,6},{5,21},{6,4},{7,23},{8,10},{9,25},... | collective-permute-start | bytes 393224 | tf_op jit(solution)/shard_map/ppermute | solution.py:534
  53.5 8.8 %collective-permute-start.11 = (bf16[128,512]{1,0:T(8,128)(2,1)S(1)}, bf16[128,512]{1,0:T(8,128)(2,1)S(1)}, u32[]{:S(2)}, u32[]{:S(2)}) collective-permute-start(bf16[128,512]{1,0:T(8,128)(2,1)S(1)} %add.7.refs_2_.refs_0_), channel_id=1, source_target_pairs={{0,16},{1,17},{2,18},{3,19},{4,20},{5,21},{6,22},{7,23},{8,24},{9,... | collective-permute-start | bytes 393224 | tf_op jit(solution)/shard_map/ppermute | solution.py:534
  56.8 11.4 %collective-permute-start.18 = (bf16[128,512]{1,0:T(8,128)(2,1)S(1)}, bf16[128,512]{1,0:T(8,128)(2,1)S(1)}, u32[]{:S(2)}, u32[]{:S(2)}) collective-permute-start(bf16[128,512]{1,0:T(8,128)(2,1)S(1)} %add.8.refs_2_.refs_0_), channel_id=1, source_target_pairs={{0,16},{1,9},{2,18},{3,11},{4,20},{5,13},{6,22},{7,15},{8,24},{9,1... | collective-permute-start | bytes 393224 | tf_op jit(solution)/shard_map/ppermute | solution.py:534
  59.5 6.6 %collective-permute-start.15 = (bf16[64,2176]{1,0:T(8,128)(2,1)S(1)}, bf16[64,2176]{1,0:T(8,128)(2,1)S(1)}, u32[]{:S(2)}, u32[]{:S(2)}) collective-permute-start(bf16[64,2176]{1,0:T(8,128)(2,1)S(1)} %get-tuple-element.113), channel_id=1, source_target_pairs={{0,2},{1,5},{2,0},{3,7},{4,6},{5,1},{6,4},{7,3},{8,10},{9,13},{10,... | collective-permute-start | bytes 835592 | tf_op jit(solution)/shard_map/ppermute | solution.py:534
  62.4 5.7 %collective-permute-start.14 = (bf16[128,512]{1,0:T(8,128)(2,1)S(1)}, bf16[128,512]{1,0:T(8,128)(2,1)S(1)}, u32[]{:S(2)}, u32[]{:S(2)}) collective-permute-start(bf16[128,512]{1,0:T(8,128)(2,1)S(1)} %add.9.refs_2_.refs_0_), channel_id=1, source_target_pairs={{0,8},{1,9},{2,10},{3,11},{4,12},{5,13},{6,14},{7,15},{8,0},{9,1},... | collective-permute-start | bytes 393224 | tf_op jit(solution)/shard_map/ppermute | solution.py:534
  66.1 5.1 %collective-permute-start.17 = (bf16[32,2176]{1,0:T(8,128)(2,1)S(1)}, bf16[32,2176]{1,0:T(8,128)(2,1)S(1)}, u32[]{:S(2)}, u32[]{:S(2)}) collective-permute-start(bf16[32,2176]{1,0:T(8,128)(2,1)S(1)} %get-tuple-element.115), channel_id=1, source_target_pairs={{0,8},{1,9},{2,10},{3,11},{4,12},{5,13},{6,14},{7,15},{8,0},{9,1},... | collective-permute-start | bytes 417800 | tf_op jit(solution)/shard_map/ppermute | solution.py:534
  68.1 6.8 %collective-permute-start.16 = (bf16[256,512]{1,0:T(8,128)(2,1)S(1)}, bf16[256,512]{1,0:T(8,128)(2,1)S(1)}, u32[]{:S(2)}, u32[]{:S(2)}) collective-permute-start(bf16[256,512]{1,0:T(8,128)(2,1)S(1)} %join.9.refs_2_.refs_0_), channel_id=1, source_target_pairs={{0,2},{1,5},{2,0},{3,7},{4,6},{5,1},{6,4},{7,3},{8,10},{9,13},{10,... | collective-permute-start | bytes 786440 | tf_op jit(solution)/shard_map/ppermute | solution.py:534
  68.2 9.5 %collective-permute-start.21 = (bf16[256,512]{1,0:T(8,128)(2,1)S(1)}, bf16[256,512]{1,0:T(8,128)(2,1)S(1)}, u32[]{:S(2)}, u32[]{:S(2)}) collective-permute-start(bf16[256,512]{1,0:T(8,128)(2,1)S(1)} %join.10.refs_2_.refs_0_), channel_id=1, source_target_pairs={{0,8},{1,5},{2,10},{3,7},{4,12},{5,1},{6,14},{7,3},{8,0},{9,13},{1... | collective-permute-start | bytes 786440 | tf_op jit(solution)/shard_map/ppermute | solution.py:534
  71.2 7.7 %collective-permute-start.20 = (bf16[32,2176]{1,0:T(8,128)(2,1)S(1)}, bf16[32,2176]{1,0:T(8,128)(2,1)S(1)}, u32[]{:S(2)}, u32[]{:S(2)}) collective-permute-start(bf16[32,2176]{1,0:T(8,128)(2,1)S(1)} %add.10.refs_2_.refs_0_), channel_id=1, source_target_pairs={{0,16},{1,17},{2,18},{3,19},{4,20},{5,21},{6,22},{7,23},{8,24},{9,... | collective-permute-start | bytes 417800 | tf_op jit(solution)/shard_map/ppermute | solution.py:534
  74.9 9.2 %collective-permute-start.19 = (bf16[512,512]{1,0:T(8,128)(2,1)S(1)}, bf16[512,512]{1,0:T(8,128)(2,1)S(1)}, u32[]{:S(2)}, u32[]{:S(2)}) collective-permute-start(bf16[512,512]{1,0:T(8,128)(2,1)S(1)} %join.11.refs_2_.refs_0_), channel_id=1, source_target_pairs={{0,4},{1,3},{2,6},{3,1},{4,0},{5,7},{6,2},{7,5},{8,12},{9,11},{10,... | collective-permute-start | bytes 1572872 | tf_op jit(solution)/shard_map/ppermute | solution.py:534
  77.7 13.6 %collective-permute-start.24 = (bf16[512,512]{1,0:T(8,128)(2,1)S(1)}, bf16[512,512]{1,0:T(8,128)(2,1)S(1)}, u32[]{:S(2)}, u32[]{:S(2)}) collective-permute-start(bf16[512,512]{1,0:T(8,128)(2,1)S(1)} %join.12.refs_2_.refs_0_), channel_id=1, source_target_pairs={{0,4},{1,3},{2,6},{3,1},{4,0},{5,7},{6,2},{7,5},{8,12},{9,11},{10,... | collective-permute-start | bytes 1572872 | tf_op jit(solution)/shard_map/ppermute | solution.py:534
  79.0 6.7 %collective-permute-start.26 = (bf16[32,2176]{1,0:T(8,128)(2,1)S(1)}, bf16[32,2176]{1,0:T(8,128)(2,1)S(1)}, u32[]{:S(2)}, u32[]{:S(2)}) collective-permute-start(bf16[32,2176]{1,0:T(8,128)(2,1)S(1)} %add.11.refs_2_.refs_0_), channel_id=1, source_target_pairs={{0,8},{1,9},{2,10},{3,11},{4,12},{5,13},{6,14},{7,15},{8,0},{9,1},... | collective-permute-start | bytes 417800 | tf_op jit(solution)/shard_map/ppermute | solution.py:534
  84.2 2.7 %collective-permute-start.22 = (bf16[1024,512]{1,0:T(8,128)(2,1)S(1)}, bf16[1024,512]{1,0:T(8,128)(2,1)S(1)}, u32[]{:S(2)}, u32[]{:S(2)}) collective-permute-start(bf16[1024,512]{1,0:T(8,128)(2,1)S(1)} %join.13.refs_0_.refs_1_), channel_id=1, source_target_pairs={{0,1},{1,0},{2,3},{3,2},{4,5},{5,4},{6,7},{7,6},{8,9},{9,8},{10,11... | collective-permute-start | bytes 3145736 | tf_op jit(solution)/shard_map/ppermute | solution.py:534
  85.7 6.6 %collective-permute-start.27 = (bf16[64,2176]{1,0:T(8,128)(2,1)S(1)}, bf16[64,2176]{1,0:T(8,128)(2,1)S(1)}, u32[]{:S(2)}, u32[]{:S(2)}) collective-permute-start(bf16[64,2176]{1,0:T(8,128)(2,1)S(1)} %join.15.refs_0_.refs_2_), channel_id=1, source_target_pairs={{0,2},{1,5},{2,0},{3,7},{4,6},{5,1},{6,4},{7,3},{8,10},{9,13},{10,... | collective-permute-start | bytes 835592 | tf_op jit(solution)/shard_map/ppermute | solution.py:534
  87.0 2.3 %copy-start.2 = (bf16[2048,512]{1,0:T(8,128)(2,1)S(1)}, bf16[2048,512]{1,0:T(8,128)(2,1)}, u32[]{:S(2)}) copy-start(bf16[2048,512]{1,0:T(8,128)(2,1)} %refs_2_.9) | copy-start | bytes 6291460
  91.4 4.5 %collective-permute-start.25 = (bf16[1024,512]{1,0:T(8,128)(2,1)S(1)}, bf16[1024,512]{1,0:T(8,128)(2,1)S(1)}, u32[]{:S(2)}, u32[]{:S(2)}) collective-permute-start(bf16[1024,512]{1,0:T(8,128)(2,1)S(1)} %join.14.refs_0_.refs_1_), channel_id=1, source_target_pairs={{0,1},{1,0},{2,3},{3,2},{4,5},{5,4},{6,7},{7,6},{8,9},{9,8},{10,11... | collective-permute-start | bytes 3145736 | tf_op jit(solution)/shard_map/ppermute | solution.py:534
  92.4 9.6 %collective-permute-start.28 = (bf16[128,2176]{1,0:T(8,128)(2,1)S(1)}, bf16[128,2176]{1,0:T(8,128)(2,1)S(1)}, u32[]{:S(2)}, u32[]{:S(2)}) collective-permute-start(bf16[128,2176]{1,0:T(8,128)(2,1)S(1)} %join.16.refs_0_), channel_id=1, source_target_pairs={{0,4},{1,3},{2,6},{3,1},{4,0},{5,7},{6,2},{7,5},{8,12},{9,11},{10,... | collective-permute-start | bytes 1671176 | tf_op jit(solution)/shard_map/ppermute | solution.py:534
  102.1 2.8 %collective-permute-start.29 = (bf16[256,2176]{1,0:T(8,128)(2,1)S(1)}, bf16[256,2176]{1,0:T(8,128)(2,1)S(1)}, u32[]{:S(2)}, u32[]{:S(2)}) collective-permute-start(bf16[256,2176]{1,0:T(8,128)(2,1)S(1)} %join.17.refs_0_.refs_1_), channel_id=1, source_target_pairs={{0,1},{1,0},{2,3},{3,2},{4,5},{5,4},{6,7},{7,6},{8,9},{9,8},{10,11... | collective-permute-start | bytes 3342344 | tf_op jit(solution)/shard_map/ppermute | solution.py:534

commit v5 on v4

--- a/solution.py
+++ b/solution.py
@@ -229,7 +229,7 @@
 
 
 def feed_forward(
-    attended, tokens, w_out, gain, bias, w_up, d_hidden, d_ffn, mid, normed, hidden, d_up, keep, send, whole
+    attended, tokens, w_out, gain, bias, w_up, d_hidden, d_ffn, mid, normed, hidden, d_up, keep, send
 ):
     span, width = tokens.shape
     ff = w_up.shape[1]
@@ -240,25 +240,27 @@
     normed[...] = rows
     c0 = math.sqrt(2.0 / math.pi)
     tile = 256
-    for start in range(0, ff, tile):
-        cols = slice(start, start + tile)
-        x = nn(rows, w_up[:, cols])
-        square = x * x
-        half = 0.5 + 0.5 * jnp.tanh(x * (c0 + (c0 * 0.044715) * square))
-        act = (x * half).astype(bf16)
-        slope = half + 2.0 * half * (1.0 - half) * x * (c0 + (3 * c0 * 0.044715) * square)
-        hidden[:, cols] = act
-        d_up[:, cols] = (slope * d_hidden[:, cols]).astype(bf16)
-        whole[cols] = tn(act, d_ffn[...]).astype(bf16)
-    halves(whole, [keep], [send])
-
-
-def up_back(normed, d_up, keep, send, whole):
+    core = core_index()
+    for half_at, ref in ((core, keep), (1 - core, send)):
+        for start in range(0, ff // 2, tile):
+            cols = pl.ds(pl.multiple_of(half_at * (ff // 2) + start, tile), tile)
+            x = nn(rows, w_up[:, cols])
+            square = x * x
+            half = 0.5 + 0.5 * jnp.tanh(x * (c0 + (c0 * 0.044715) * square))
+            act = (x * half).astype(bf16)
+            slope = half + 2.0 * half * (1.0 - half) * x * (c0 + (3 * c0 * 0.044715) * square)
+            hidden[:, cols] = act
+            d_up[:, cols] = (slope * d_hidden[:, cols]).astype(bf16)
+            ref[start : start + tile] = tn(act, d_ffn[...]).astype(bf16)
+
+
+def up_back(normed, d_up, keep, send):
     width = normed.shape[1]
-    for part in range(d_up.shape[1] // width):
-        cols = slice(width * part, width * (part + 1))
-        whole[cols] = tn(normed[...], d_up[:, cols]).astype(bf16)
-    halves(whole, [keep], [send])
+    core, parts = core_index(), keep.shape[0] // width
+    for half_at, ref in ((core, keep), (1 - core, send)):
+        for part in range(parts):
+            cols = pl.ds(pl.multiple_of((half_at * parts + part) * width, width), width)
+            ref[width * part : width * (part + 1)] = tn(normed[...], d_up[:, cols]).astype(bf16)
 
 
 def output(mid, hidden, w_down, out, token):
@@ -631,7 +633,7 @@
             feed_forward,
             [flat32, flat, ((span, ff), bf16), ((span, ff), bf16), half, half],
             attended, tokens, w_out, gain2, bias2, w_up, d_hidden, d_ffn,
-            scratch=[pltpu.VMEM((ff, width), bf16)], name="feed_forward", us=state["cost"],
+            name="feed_forward", us=state["cost"],
         )
         state.update(mid=mid, normed2=normed2, hidden=hidden, d_up=d_up)
         state["D"] = [keep], [send]
@@ -641,7 +643,7 @@
         half = ((ff // 2, width), bf16)
         keep, send = call(
             up_back, [half, half], state["normed2"], state["d_up"],
-            deps=(step, recv_hat), scratch=[pltpu.VMEM((ff, width), bf16)], name="up_back", us=state["cost"],
+            deps=(step, recv_hat), name="up_back", us=state["cost"],
         )
         state["U"] = [keep], [send]
         return send

time: 107 us -> 107 us (level)
  transfers between devices with their start and end apart: 30 -> 30, of which waited for: 19 -> 19; matrix products, arithmetic and copies ran while one was open for 0% -> 0% of each run, Pallas kernels for 30% -> 29%
where the time goes in v5:
time: 107 us
  Pallas kernels  37.2 us (35%)
  waiting for transfers between devices  37.2 us (35%)
  starting transfers between devices  27.3 us (26%)
  local copies, waits for them, and re-layouts  3.12 us (3%)
  between operations  2.12 us (2%)
    pallas_call x43, Pallas kernels, call(): pl.pallas_call(run, out_shape=[jax.ShapeDtypeStruct(s, d) for s, d in out...  37.2 us
    ppermute x27, waiting for transfers between devices, start(): self.other = [lax.ppermute(v, ('batch', 'seq'), pairs) for v in value]  34.6 us
    ppermute x27, starting transfers between devices, start(): self.other = [lax.ppermute(v, ('batch', 'seq'), pairs) for v in value]  26.5 us
    unnamed x24, local copies, waits for them, and re-layouts  3.12 us
    ppermute x1, waiting for transfers between devices, body(): recv = lax.ppermute(edge, 'seq', onward)  2.63 us
  transfers between devices with their start and end apart: 30, of which 19 were waited for; matrix products, arithmetic and copies ran while one was open for 0% of the time, Pallas kernels for 29%

profile of v5, /device:TPU:0, one launch (start us, length us, event | category | flops | bytes accessed | tf_op | source)
XLA Modules:
  0.0 106.9 jit_solution(12518486289673889787)
XLA Ops:
  0.7 1.0 copy-done.5
  1.7 0.3 standardize.1.refs_0_.refs_4_
  2.0 1.1 %copy-done.4 = bf16[512,1536]{1,0:T(8,128)(2,1)S(1)} copy-done((bf16[512,1536]{1,0:T(8,128)(2,1)S(1)}, bf16[512,1536]{1,0:T(8,128)(2,1)}, u32[]{:S(2)}) %copy-start.4) | copy-done | bytes 1572888
  3.1 1.2 %project.1 = (bf16[512,512]{1,0:T(8,128)(2,1)S(1)}, bf16[512,1024]{1,0:T(8,128)(2,1)S(1)}, bf16[496,1024]{1,0:T(8,128)(2,1)S(1)}, bf16[96,1024]{1,0:T(8,128)(2,1)S(1)}) custom-call(f32[512,512]{1,0:T(8,128)S(1)} %standardize.1.refs_0_.refs_4_, bf16[512]{0:T(512)(128)(2,1)S(1)} %copy-done.11, bf16[512]{0:T(512)(128)(2,1)S(1)} %copy-done.10, ...), custom_call_target="tpu_custom_call" | custom-call | flops 3449999872 | bytes 65536 | tf_op jit(solution)/shard_map/project/pallas_call | solution.py:45
  4.4 0.5 collective-permute-start
  5.8 0.4 project_q.1.refs_3_.refs_0_
  6.3 1.3 %hidden_back.1 = (bf16[512,512]{1,0:T(8,128)(2,1)S(1)}, f32[512,2048]{1,0:T(8,128)S(1)}) custom-call(s32[1]{0:T(128)S(6)} %copy.29.refs_0_, bf16[512,512]{1,0:T(8,128)(2,1)S(1)} %bitcast.8, bf16[2048,512]{1,0:T(8,128)(2,1)S(1)} %copy-done.1, bf16[512,512]{1,0:T(8,128)(2,1)S(1)} %project_q.1.refs_3_.refs_0_), custom_call_target="tpu_custom_call" | custom-call | flops 230000000 | bytes 65536 | tf_op jit(solution)/shard_map/hidden_back/pallas_call | solution.py:45
  7.6 2.6 %collective-permute-done.refs_3_ = bf16[96,1024]{1,0:T(8,128)(2,1)S(1)} collective-permute-done((bf16[96,1024]{1,0:T(8,128)(2,1)S(1)}, bf16[96,1024]{1,0:T(8,128)(2,1)S(1)}, u32[]{:S(2)}, u32[]{:S(2)}) %collective-permute-start) | collective-permute-done | bytes 196640 | tf_op jit(solution)/shard_map/ppermute | solution.py:615
  10.2 2.2 %attend.1 = (bf16[512,512]{1,0:T(8,128)(2,1)S(1)}, bf16[4096,128]{1,0:T(8,128)(2,1)S(1)}, bf16[96,512]{1,0:T(8,128)(2,1)S(1)}) custom-call(bf16[512,512]{1,0:T(8,128)(2,1)S(1)} %project_q.1.refs_3_.refs_0_, bf16[512,1024]{1,0:T(8,128)(2,1)S(1)} %get-tuple-element.75.refs_1_, bf16[496,1024]{1,0:T(8,128)(2,1)S(1)} %get-tuple-element.76.refs_2_, ...), custom_call_target="tpu_custom_call" | custom-call | flops 575000000 | bytes 65536 | tf_op jit(solution)/shard_map/attend/pallas_call | solution.py:45
  12.5 0.2 collective-permute-start.2
  12.8 4.7 %feed_forward.1 = (f32[512,512]{1,0:T(8,128)S(1)}, bf16[512,512]{1,0:T(8,128)(2,1)S(1)}, bf16[512,2048]{1,0:T(8,128)(2,1)S(1)}, bf16[512,2048]{1,0:T(8,128)(2,1)...) custom-call(bf16[512,512]{1,0:T(8,128)(2,1)S(1)} %get-tuple-element.79.refs_0_.refs_5_, ...), custom_call_target="tpu_custom_call" | custom-call | flops 1150000000 | bytes 65536 | tf_op jit(solution)/shard_map/feed_forward/pallas_call | solution.py:45
  17.5 2.4 %collective-permute-start.1 = (bf16[1024,512]{1,0:T(8,128)(2,1)S(1)}, bf16[1024,512]{1,0:T(8,128)(2,1)S(1)}, u32[]{:S(2)}, u32[]{:S(2)}) collective-permute-start(bf16[1024,512]{1,0:T(8,128)(2,1)S(1)} %get-tuple-element.84.refs_2_), channel_id=1, source_target_pairs={{0,1},{1,0},{2,3},{3,2},{4,5},{5,4},{6,7},{7,6},{8,9},{9,8},{10,11... | collective-permute-start | bytes 3145736 | tf_op jit(solution)/shard_map/ppermute | solution.py:536
  19.9 1.3 %up_back.1 = (bf16[1024,512]{1,0:T(8,128)(2,1)S(1)}, bf16[1024,512]{1,0:T(8,128)(2,1)S(1)}) custom-call(bf16[512,512]{1,0:T(8,128)(2,1)S(1)} %get-tuple-element.85.refs_0_, bf16[512,2048]{1,0:T(8,128)(2,1)S(1)} %get-tuple-element.86.refs_1_, bf16[1024,512]{1,0:T(8,128)(2,1)S(1)} %get-tuple-element.84.refs_2_, ...), custom_call_target="tpu_custom_call" | custom-call | flops 575000000 | bytes 65536 | tf_op jit(solution)/shard_map/up_back/pallas_call | solution.py:45
  21.3 0.9 collective-permute-done.1.refs_1_
  22.2 0.2 add_split.9
  22.4 1.6 %collective-permute-start.3 = (bf16[512,512]{1,0:T(8,128)(2,1)S(1)}, bf16[512,512]{1,0:T(8,128)(2,1)S(1)}, u32[]{:S(2)}, u32[]{:S(2)}) collective-permute-start(bf16[512,512]{1,0:T(8,128)(2,1)S(1)} %get-tuple-element.90), channel_id=1, source_target_pairs={{0,4},{1,3},{2,6},{3,1},{4,0},{5,7},{6,2},{7,5},{8,12},{9,11},{10,... | collective-permute-start | bytes 1572872 | tf_op jit(solution)/shard_map/ppermute | solution.py:536
  23.9 2.4 %mid_back.1 = (f32[512,512]{1,0:T(8,128)S(1)}, bf16[512,512]{1,0:T(8,128)(2,1)S(1)}, bf16[512,512]{1,0:T(8,128)(2,1)S(1)}, f32[8,512]{1,0:T(8,128)S(1)}) custom-call(f32[512,512]{1,0:T(8,128)S(1)} %get-tuple-element.81.refs_0_, bf16[512,2048]{1,0:T(8,128)(2,1)S(1)} %get-tuple-element.86.refs_1_, bf16[512,2048]{1,0:T(8,128)(2,1)S(1)} %copy-done, ...), custom_call_target="tpu_custom_call" | custom-call | flops 575000000 | bytes 65536 | tf_op jit(solution)/shard_map/mid_back/pallas_call | solution.py:45
  26.4 0.1 add_split.10
  26.5 0.6 collective-permute-start.7
  27.1 3.8 %attend_back.1 = (bf16[512,1536]{1,0:T(8,128)(2,1)S(1)}, bf16[96,1024]{1,0:T(8,128)(2,1)S(1)}) custom-call(bf16[512,512]{1,0:T(8,128)(2,1)S(1)} %project_q.1.refs_3_.refs_0_, bf16[512,1024]{1,0:T(8,128)(2,1)S(1)} %get-tuple-element.75.refs_1_, bf16[496,1024]{1,0:T(8,128)(2,1)S(1)} %get-tuple-element.76.refs_2_, ...), custom_call_target="tpu_custom_call" | custom-call | flops 23000000512 | bytes 65536 | tf_op jit(solution)/shard_map/attend_back/pallas_call | solution.py:45
  30.9 3.4 %project_back.1 = (f32[512,512]{1,0:T(8,128)S(1)}, bf16[96,512]{1,0:T(8,128)(2,1)}, bf16[256,2176]{1,0:T(8,128)(2,1)S(1)}, bf16[256,2176]{1,0:T(8,128)(2,1)S(1)}) custom-call(bf16[512,1536]{1,0:T(8,128)(2,1)S(1)} %get-tuple-element.95.refs_0_, bf16[96,1024]{1,0:T(8,128)(2,1)S(1)} %get-tuple-element.96.refs_1_.refs_10_, ...), custom_call_target="tpu_custom_call" | custom-call | flops 2300000000 | bytes 65536 | tf_op jit(solution)/shard_map/project_back/pallas_call | solution.py:45
  34.4 0.4 collective-permute-start.5
  34.8 2.5 %collective-permute-done.7.refs_1_ = bf16[512,512]{1,0:T(8,128)(2,1)S(1)} collective-permute-done((bf16[512,512]{1,0:T(8,128)(2,1)S(1)}, bf16[512,512]{1,0:T(8,128)(2,1)S(1)}, u32[]{:S(2)}, u32[]{:S(2)}) %collective-permute-start.7) | collective-permute-done | bytes 524320 | tf_op jit(solution)/shard_map/ppermute | solution.py:536
  37.3 1.6 %collective-permute-start.9 = (bf16[256,512]{1,0:T(8,128)(2,1)S(1)}, bf16[256,512]{1,0:T(8,128)(2,1)S(1)}, u32[]{:S(2)}, u32[]{:S(2)}) collective-permute-start(bf16[256,512]{1,0:T(8,128)(2,1)S(1)} %get-tuple-element.108), channel_id=1, source_target_pairs={{0,8},{1,5},{2,10},{3,7},{4,12},{5,1},{6,14},{7,3},{8,0},{9,13},{1... | collective-permute-start | bytes 786440 | tf_op jit(solution)/shard_map/ppermute | solution.py:536
  39.1 1.8 %collective-permute-done.5.refs_1_ = bf16[256,512]{1,0:T(8,128)(2,1)S(1)} collective-permute-done((bf16[256,512]{1,0:T(8,128)(2,1)S(1)}, bf16[256,512]{1,0:T(8,128)(2,1)S(1)}, u32[]{:S(2)}, u32[]{:S(2)}) %collective-permute-start.5) | collective-permute-done | bytes 262176 | tf_op jit(solution)/shard_map/ppermute | solution.py:536
  40.9 2.9 %collective-permute-done.9.refs_1_ = bf16[256,512]{1,0:T(8,128)(2,1)S(1)} collective-permute-done((bf16[256,512]{1,0:T(8,128)(2,1)S(1)}, bf16[256,512]{1,0:T(8,128)(2,1)S(1)}, u32[]{:S(2)}, u32[]{:S(2)}) %collective-permute-start.9) | collective-permute-done | bytes 262176 | tf_op jit(solution)/shard_map/ppermute | solution.py:536
  43.8 2.7 %collective-permute-start.10 = (bf16[128,512]{1,0:T(8,128)(2,1)S(1)}, bf16[128,512]{1,0:T(8,128)(2,1)S(1)}, u32[]{:S(2)}, u32[]{:S(2)}) collective-permute-start(bf16[128,512]{1,0:T(8,128)(2,1)S(1)} %get-tuple-element.110), channel_id=1, source_target_pairs={{0,16},{1,9},{2,18},{3,11},{4,20},{5,13},{6,22},{7,15},{8,24},{9,1... | collective-permute-start | bytes 393224 | tf_op jit(solution)/shard_map/ppermute | solution.py:536
  46.4 1.6 %collective-permute-start.8 = (bf16[128,512]{1,0:T(8,128)(2,1)S(1)}, bf16[128,512]{1,0:T(8,128)(2,1)S(1)}, u32[]{:S(2)}, u32[]{:S(2)}) collective-permute-start(bf16[128,512]{1,0:T(8,128)(2,1)S(1)} %get-tuple-element.107), channel_id=1, source_target_pairs={{0,8},{1,9},{2,10},{3,11},{4,12},{5,13},{6,14},{7,15},{8,0},{9,1},... | collective-permute-start | bytes 393224 | tf_op jit(solution)/shard_map/ppermute | solution.py:536
  48.0 1.5 %collective-permute-start.12 = (bf16[128,2176]{1,0:T(8,128)(2,1)S(1)}, bf16[128,2176]{1,0:T(8,128)(2,1)S(1)}, u32[]{:S(2)}, u32[]{:S(2)}) collective-permute-start(bf16[128,2176]{1,0:T(8,128)(2,1)S(1)} %get-tuple-element.111), channel_id=1, source_target_pairs={{0,4},{1,3},{2,6},{3,1},{4,0},{5,7},{6,2},{7,5},{8,12},{9,11},{10,... | collective-permute-start | bytes 1671176 | tf_op jit(solution)/shard_map/ppermute | solution.py:536
  49.5 0.5 collective-permute-done.10.refs_1_
  50.1 0.2 collective-permute-start.13
  50.2 3.1 %collective-permute-done.8.refs_1_ = bf16[128,512]{1,0:T(8,128)(2,1)S(1)} collective-permute-done((bf16[128,512]{1,0:T(8,128)(2,1)S(1)}, bf16[128,512]{1,0:T(8,128)(2,1)S(1)}, u32[]{:S(2)}, u32[]{:S(2)}) %collective-permute-start.8) | collective-permute-done | bytes 131104 | tf_op jit(solution)/shard_map/ppermute | solution.py:536
  53.3 2.3 %collective-permute-start.11 = (bf16[128,512]{1,0:T(8,128)(2,1)S(1)}, bf16[128,512]{1,0:T(8,128)(2,1)S(1)}, u32[]{:S(2)}, u32[]{:S(2)}) collective-permute-start(bf16[128,512]{1,0:T(8,128)(2,1)S(1)} %add.7.refs_2_.refs_0_), channel_id=1, source_target_pairs={{0,16},{1,17},{2,18},{3,19},{4,20},{5,21},{6,22},{7,23},{8,24},{9,... | collective-permute-start | bytes 393224 | tf_op jit(solution)/shard_map/ppermute | solution.py:536
  55.6 1.0 collective-permute-done.13.refs_1_
  56.6 2.6 %collective-permute-start.18 = (bf16[128,512]{1,0:T(8,128)(2,1)S(1)}, bf16[128,512]{1,0:T(8,128)(2,1)S(1)}, u32[]{:S(2)}, u32[]{:S(2)}) collective-permute-start(bf16[128,512]{1,0:T(8,128)(2,1)S(1)} %add.8.refs_2_.refs_0_), channel_id=1, source_target_pairs={{0,16},{1,9},{2,18},{3,11},{4,20},{5,13},{6,22},{7,15},{8,24},{9,1... | collective-permute-start | bytes 393224 | tf_op jit(solution)/shard_map/ppermute | solution.py:536
  59.2 0.6 collective-permute-start.15
  59.8 2.3 %collective-permute-done.11.refs_1_ = bf16[128,512]{1,0:T(8,128)(2,1)S(1)} collective-permute-done((bf16[128,512]{1,0:T(8,128)(2,1)S(1)}, bf16[128,512]{1,0:T(8,128)(2,1)S(1)}, u32[]{:S(2)}, u32[]{:S(2)}) %collective-permute-start.11) | collective-permute-done | bytes 131104 | tf_op jit(solution)/shard_map/ppermute | solution.py:536
  62.2 3.6 %collective-permute-done.15.refs_1_ = bf16[64,2176]{1,0:T(8,128)(2,1)S(1)} collective-permute-done((bf16[64,2176]{1,0:T(8,128)(2,1)S(1)}, bf16[64,2176]{1,0:T(8,128)(2,1)S(1)}, u32[]{:S(2)}, u32[]{:S(2)}) %collective-permute-start.15) | collective-permute-done | bytes 278560 | tf_op jit(solution)/shard_map/ppermute | solution.py:536
  65.9 1.4 %collective-permute-start.17 = (bf16[32,2176]{1,0:T(8,128)(2,1)S(1)}, bf16[32,2176]{1,0:T(8,128)(2,1)S(1)}, u32[]{:S(2)}, u32[]{:S(2)}) collective-permute-start(bf16[32,2176]{1,0:T(8,128)(2,1)S(1)} %get-tuple-element.115), channel_id=1, source_target_pairs={{0,8},{1,9},{2,10},{3,11},{4,12},{5,13},{6,14},{7,15},{8,0},{9,1},... | collective-permute-start | bytes 417800 | tf_op jit(solution)/shard_map/ppermute | solution.py:536
  67.3 0.5 collective-permute-done.14.refs_1_
  68.0 0.7 collective-permute-start.21
  68.7 2.3 %collective-permute-done.17.refs_1_ = bf16[32,2176]{1,0:T(8,128)(2,1)S(1)} collective-permute-done((bf16[32,2176]{1,0:T(8,128)(2,1)S(1)}, bf16[32,2176]{1,0:T(8,128)(2,1)S(1)}, u32[]{:S(2)}, u32[]{:S(2)}) %collective-permute-start.17) | collective-permute-done | bytes 139296 | tf_op jit(solution)/shard_map/ppermute | solution.py:536
  71.0 0.6 collective-permute-start.20
  71.6 3.0 %collective-permute-done.16.refs_1_ = bf16[256,512]{1,0:T(8,128)(2,1)S(1)} collective-permute-done((bf16[256,512]{1,0:T(8,128)(2,1)S(1)}, bf16[256,512]{1,0:T(8,128)(2,1)S(1)}, u32[]{:S(2)}, u32[]{:S(2)}) %collective-permute-start.16) | collective-permute-done | bytes 262176 | tf_op jit(solution)/shard_map/ppermute | solution.py:536
  74.7 1.3 %collective-permute-start.19 = (bf16[512,512]{1,0:T(8,128)(2,1)S(1)}, bf16[512,512]{1,0:T(8,128)(2,1)S(1)}, u32[]{:S(2)}, u32[]{:S(2)}) collective-permute-start(bf16[512,512]{1,0:T(8,128)(2,1)S(1)} %join.11.refs_2_.refs_0_), channel_id=1, source_target_pairs={{0,4},{1,3},{2,6},{3,1},{4,0},{5,7},{6,2},{7,5},{8,12},{9,11},{10,... | collective-permute-start | bytes 1572872 | tf_op jit(solution)/shard_map/ppermute | solution.py:536
  76.0 1.5 %collective-permute-done.21.refs_1_ = bf16[256,512]{1,0:T(8,128)(2,1)S(1)} collective-permute-done((bf16[256,512]{1,0:T(8,128)(2,1)S(1)}, bf16[256,512]{1,0:T(8,128)(2,1)S(1)}, u32[]{:S(2)}, u32[]{:S(2)}) %collective-permute-start.21) | collective-permute-done | bytes 262176 | tf_op jit(solution)/shard_map/ppermute | solution.py:536
  77.6 1.5 %collective-permute-start.24 = (bf16[512,512]{1,0:T(8,128)(2,1)S(1)}, bf16[512,512]{1,0:T(8,128)(2,1)S(1)}, u32[]{:S(2)}, u32[]{:S(2)}) collective-permute-start(bf16[512,512]{1,0:T(8,128)(2,1)S(1)} %join.12.refs_2_.refs_0_), channel_id=1, source_target_pairs={{0,4},{1,3},{2,6},{3,1},{4,0},{5,7},{6,2},{7,5},{8,12},{9,11},{10,... | collective-permute-start | bytes 1572872 | tf_op jit(solution)/shard_map/ppermute | solution.py:536
  79.0 0.8 collective-permute-start.26
  79.9 4.0 %collective-permute-done.19.refs_1_ = bf16[512,512]{1,0:T(8,128)(2,1)S(1)} collective-permute-done((bf16[512,512]{1,0:T(8,128)(2,1)S(1)}, bf16[512,512]{1,0:T(8,128)(2,1)S(1)}, u32[]{:S(2)}, u32[]{:S(2)}) %collective-permute-start.19) | collective-permute-done | bytes 524320 | tf_op jit(solution)/shard_map/ppermute | solution.py:536
  84.1 1.4 %finish_down.2 = (f32[2048,512]{1,0:T(8,128)}, f32[8,128]{1,0:T(8,128)S(1)}) custom-call(bf16[1024,512]{1,0:T(8,128)(2,1)S(1)} %join.13.refs_0_.refs_1_, bf16[1024,512]{1,0:T(8,128)(2,1)S(1)} %join.13.refs_0_.refs_1_), custom_call_target="tpu_custom_call" | custom-call | flops 6899999744 | bytes 65536 | tf_op jit(solution)/shard_map/finish_down/pallas_call | solution.py:45
  85.6 1.1 %collective-permute-done.22.refs_0_ = bf16[1024,512]{1,0:T(8,128)(2,1)S(1)} collective-permute-done((bf16[1024,512]{1,0:T(8,128)(2,1)S(1)}, bf16[1024,512]{1,0:T(8,128)(2,1)S(1)}, u32[]{:S(2)}, u32[]{:S(2)}) %collective-permute-start.22) | collective-permute-done | bytes 1048608 | tf_op jit(solution)/shard_map/ppermute | solution.py:536
  86.7 1.4 %finish_down.3 = (f32[2048,512]{1,0:T(8,128)}, f32[8,128]{1,0:T(8,128)S(1)}) custom-call(bf16[1024,512]{1,0:T(8,128)(2,1)S(1)} %collective-permute-done.22.refs_0_, f32[2048,512]{1,0:T(8,128)} %get-tuple-element.116.refs_1_), custom_call_target="tpu_custom_call", output_to_operand_aliasing={{0}: (1, {})} | custom-call | flops 6899999744 | bytes 65536 | tf_op jit(solution)/shard_map/finish_down/pallas_call | solution.py:45
  88.1 1.0 copy-done.2
  89.1 2.0 %output.1 = (bf16[512,512]{1,0:T(8,128)(2,1)}, f32[8,128]{1,0:T(8,128)S(1)}) custom-call(f32[512,512]{1,0:T(8,128)S(1)} %get-tuple-element.81.refs_0_, bf16[512,2048]{1,0:T(8,128)(2,1)S(1)} %get-tuple-element.82.refs_1_, bf16[2048,512]{1,0:T(8,128)(2,1)S(1)} %copy-done.2, f32[8,128]{1,0:T(8,128)S(1)} %get-tuple-element.117.refs_3_), custom_call_target="tpu_custom_call" | custom-call | flops 575000000 | bytes 65536 | tf_op jit(solution)/shard_map/output/pallas_call | solution.py:45
  91.2 0.4 collective-permute-start.25
  91.6 0.5 collective-permute-done.27.refs_1_
  92.2 1.3 %collective-permute-start.28 = (bf16[128,2176]{1,0:T(8,128)(2,1)S(1)}, bf16[128,2176]{1,0:T(8,128)(2,1)S(1)}, u32[]{:S(2)}, u32[]{:S(2)}) collective-permute-start(bf16[128,2176]{1,0:T(8,128)(2,1)S(1)} %join.16.refs_0_), channel_id=1, source_target_pairs={{0,4},{1,3},{2,6},{3,1},{4,0},{5,7},{6,2},{7,5},{8,12},{9,11},{10,... | collective-permute-start | bytes 1671176 | tf_op jit(solution)/shard_map/ppermute | solution.py:536
  93.5 2.0 %finish_up.2 = (f32[512,2048]{1,0:T(8,128)}, f32[8,128]{1,0:T(8,128)}) custom-call(bf16[1024,512]{1,0:T(8,128)(2,1)S(1)} %join.14.refs_0_.refs_1_, bf16[1024,512]{1,0:T(8,128)(2,1)S(1)} %join.14.refs_0_.refs_1_), custom_call_target="tpu_custom_call" | custom-call | flops 6899999744 | bytes 65536 | tf_op jit(solution)/shard_map/finish_up/pallas_call | solution.py:45
  95.5 1.4 %finish_up.3 = (f32[512,2048]{1,0:T(8,128)}, f32[8,128]{1,0:T(8,128)S(1)}) custom-call(bf16[1024,512]{1,0:T(8,128)(2,1)S(1)} %collective-permute-done.25.refs_0_, f32[512,2048]{1,0:T(8,128)} %get-tuple-element.123.refs_1_), custom_call_target="tpu_custom_call", output_to_operand_aliasing={{0}: (1, {})} | custom-call | flops 6899999744 | bytes 65536 | tf_op jit(solution)/shard_map/finish_up/pallas_call | solution.py:45
  96.9 2.5 %tokens_back.1 = (bf16[512,512]{1,0:T(8,128)(2,1)}, f32[8,128]{1,0:T(8,128)S(1)}) custom-call(f32[512,512]{1,0:T(8,128)S(1)} %get-tuple-element.119.refs_0_, bf16[96,512]{1,0:T(8,128)(2,1)} %collective-permute-done.23.refs_1_, bf16[512,512]{1,0:T(8,128)(2,1)S(1)} %bitcast.7, bf16[512]{0:T(512)(128)(2,1)S(1)} %copy-done.11, ...), custom_call_target="tpu_custom_call" | custom-call | flops 23000000512 | bytes 65536 | tf_op jit(solution)/shard_map/tokens_back/pallas_call | solution.py:45
  99.4 2.4 %collective-permute-done.28.refs_1_ = bf16[128,2176]{1,0:T(8,128)(2,1)S(1)} collective-permute-done((bf16[128,2176]{1,0:T(8,128)(2,1)S(1)}, bf16[128,2176]{1,0:T(8,128)(2,1)S(1)}, u32[]{:S(2)}, u32[]{:S(2)}) %collective-permute-start.28) | collective-permute-done | bytes 557088 | tf_op jit(solution)/shard_map/ppermute | solution.py:536
  102.0 2.0 %finish_rest.2 = (f32[512,1536]{1,0:T(8,128)}, f32[512,512]{1,0:T(8,128)}, f32[8,128]{1,0:T(8,128)}) custom-call(bf16[256,2176]{1,0:T(8,128)(2,1)S(1)} %join.17.refs_0_.refs_1_, bf16[256,2176]{1,0:T(8,128)(2,1)S(1)} %join.17.refs_0_.refs_1_), custom_call_target="tpu_custom_call" | custom-call | flops 6899999744 | bytes 65536 | tf_op jit(solution)/shard_map/finish_rest/pallas_call | solution.py:45
  104.0 0.7 collective-permute-done.29.refs_0_
  104.7 2.0 %finish_rest.3 = (f32[512,1536]{1,0:T(8,128)}, f32[512,512]{1,0:T(8,128)}, f32[512]{0:T(512)}, f32[512]{0:T(512)}, f32[512]{0:T(512)}, /*index=5*/f32[512]{0:T(512)}, f32[8,128]{1,0:T(8,128)}) custom-call(bf16[256,2176]{1,0:T(8,128)(2,1)S(1)} %collective-permute-done.29.refs_0_, ...), custom_call_target="tpu_custom_call", output_to_operand_aliasing={{0}: (2, {}), {1}: (3, {})} | custom-call | flops 6899999744 | bytes 65536 | tf_op jit(solution)/shard_map/finish_rest/pallas_call | solution.py:45
  (63 shorter events, 1.6 us)
Async XLA Ops:
  0.6 1.0 copy-start.5
  1.7 1.4 %copy-start.4 = (bf16[512,1536]{1,0:T(8,128)(2,1)S(1)}, bf16[512,1536]{1,0:T(8,128)(2,1)}, u32[]{:S(2)}) copy-start(bf16[512,1536]{1,0:T(8,128)(2,1)} %refs_4_.3) | copy-start | bytes 4718596
  1.7 1.4 %copy-start.10 = (bf16[512]{0:T(512)(128)(2,1)S(1)}, bf16[512]{0:T(512)(128)(2,1)}, u32[]{:S(2)}) copy-start(bf16[512]{0:T(512)(128)(2,1)} %refs_9_.1) | copy-start | bytes 3076
  1.7 1.4 %copy-start.11 = (bf16[512]{0:T(512)(128)(2,1)S(1)}, bf16[512]{0:T(512)(128)(2,1)}, u32[]{:S(2)}) copy-start(bf16[512]{0:T(512)(128)(2,1)} %refs_3_.7) | copy-start | bytes 3076
  4.4 1.9 %copy-start.1 = (bf16[2048,512]{1,0:T(8,128)(2,1)S(1)}, bf16[2048,512]{1,0:T(8,128)(2,1)}, u32[]{:S(2)}) copy-start(bf16[2048,512]{1,0:T(8,128)(2,1)} %refs_2_.9) | copy-start | bytes 6291460
  4.4 1.9 %copy-start.7 = (bf16[1,512,512]{2,1,0:T(8,128)(2,1)S(1)}, bf16[1,512,512]{2,1,0:T(8,128)(2,1)}, u32[]{:S(2)}) copy-start(bf16[1,512,512]{2,1,0:T(8,128)(2,1)} %param.13) | copy-start | bytes 1572868
  4.4 5.8 %collective-permute-start = (bf16[96,1024]{1,0:T(8,128)(2,1)S(1)}, bf16[96,1024]{1,0:T(8,128)(2,1)S(1)}, u32[]{:S(2)}, u32[]{:S(2)}) collective-permute-start(bf16[96,1024]{1,0:T(8,128)(2,1)S(1)} %get-tuple-element.77), channel_id=1, source_target_pairs={{0,1},{1,2},{2,3},{3,0},{4,5},{5,6},{6,7},{7,4},{8,9},{9,10},{10,1... | collective-permute-start | bytes 589832 | tf_op jit(solution)/shard_map/ppermute | solution.py:615
  10.2 2.5 %copy-start = (bf16[512,2048]{1,0:T(8,128)(2,1)S(1)}, bf16[512,2048]{1,0:T(8,128)(2,1)}, u32[]{:S(2)}) copy-start(bf16[512,2048]{1,0:T(8,128)(2,1)} %refs_2_.8) | copy-start | bytes 6291460
  10.2 2.5 %copy-start.3 = (bf16[512,512]{1,0:T(8,128)(2,1)S(1)}, bf16[512,512]{1,0:T(8,128)(2,1)}, u32[]{:S(2)}) copy-start(bf16[512,512]{1,0:T(8,128)(2,1)} %refs_6_.1) | copy-start | bytes 1572868
  10.2 2.5 %copy-start.6 = (bf16[1,512,512]{2,1,0:T(8,128)(2,1)S(1)}, bf16[1,512,512]{2,1,0:T(8,128)(2,1)}, u32[]{:S(2)}) copy-start(bf16[1,512,512]{2,1,0:T(8,128)(2,1)} %param.11) | copy-start | bytes 1572868
  10.2 2.5 %copy-start.8 = (bf16[512]{0:T(512)(128)(2,1)S(1)}, bf16[512]{0:T(512)(128)(2,1)}, u32[]{:S(2)}) copy-start(bf16[512]{0:T(512)(128)(2,1)} %refs_3_.6) | copy-start | bytes 3076
  10.2 2.6 %copy-start.9 = (bf16[512]{0:T(512)(128)(2,1)S(1)}, bf16[512]{0:T(512)(128)(2,1)}, u32[]{:S(2)}) copy-start(bf16[512]{0:T(512)(128)(2,1)} %refs_4_.2) | copy-start | bytes 3076
  12.5 7.5 %collective-permute-start.2 = (bf16[96,512]{1,0:T(8,128)(2,1)S(1)}, bf16[96,512]{1,0:T(8,128)(2,1)S(1)}, u32[]{:S(2)}, u32[]{:S(2)}) collective-permute-start(bf16[96,512]{1,0:T(8,128)(2,1)S(1)} %get-tuple-element.87), channel_id=1, source_target_pairs={{0,1},{1,2},{2,3},{3,0},{4,5},{5,6},{6,7},{7,4},{8,9},{9,10},{10,1... | collective-permute-start | bytes 294920 | tf_op jit(solution)/shard_map/ppermute | solution.py:626
  17.5 4.7 %collective-permute-start.1 = (bf16[1024,512]{1,0:T(8,128)(2,1)S(1)}, bf16[1024,512]{1,0:T(8,128)(2,1)S(1)}, u32[]{:S(2)}, u32[]{:S(2)}) collective-permute-start(bf16[1024,512]{1,0:T(8,128)(2,1)S(1)} %get-tuple-element.84.refs_2_), channel_id=1, source_target_pairs={{0,1},{1,0},{2,3},{3,2},{4,5},{5,4},{6,7},{7,6},{8,9},{9,8},{10,11... | collective-permute-start | bytes 3145736 | tf_op jit(solution)/shard_map/ppermute | solution.py:536
  21.2 5.1 %collective-permute-start.4 = (bf16[1024,512]{1,0:T(8,128)(2,1)S(1)}, bf16[1024,512]{1,0:T(8,128)(2,1)S(1)}, u32[]{:S(2)}, u32[]{:S(2)}) collective-permute-start(bf16[1024,512]{1,0:T(8,128)(2,1)S(1)} %get-tuple-element.88.refs_0_), channel_id=1, source_target_pairs={{0,1},{1,0},{2,3},{3,2},{4,5},{5,4},{6,7},{7,6},{8,9},{9,8},{10,11... | collective-permute-start | bytes 3145736 | tf_op jit(solution)/shard_map/ppermute | solution.py:536
  22.4 12.0 %collective-permute-start.3 = (bf16[512,512]{1,0:T(8,128)(2,1)S(1)}, bf16[512,512]{1,0:T(8,128)(2,1)S(1)}, u32[]{:S(2)}, u32[]{:S(2)}) collective-permute-start(bf16[512,512]{1,0:T(8,128)(2,1)S(1)} %get-tuple-element.90), channel_id=1, source_target_pairs={{0,4},{1,3},{2,6},{3,1},{4,0},{5,7},{6,2},{7,5},{8,12},{9,11},{10,... | collective-permute-start | bytes 1572872 | tf_op jit(solution)/shard_map/ppermute | solution.py:536
  26.5 10.8 %collective-permute-start.7 = (bf16[512,512]{1,0:T(8,128)(2,1)S(1)}, bf16[512,512]{1,0:T(8,128)(2,1)S(1)}, u32[]{:S(2)}, u32[]{:S(2)}) collective-permute-start(bf16[512,512]{1,0:T(8,128)(2,1)S(1)} %get-tuple-element.103), channel_id=1, source_target_pairs={{0,4},{1,3},{2,6},{3,1},{4,0},{5,7},{6,2},{7,5},{8,12},{9,11},{10,... | collective-permute-start | bytes 1572872 | tf_op jit(solution)/shard_map/ppermute | solution.py:536
  34.3 4.6 %collective-permute-start.6 = (bf16[256,2176]{1,0:T(8,128)(2,1)S(1)}, bf16[256,2176]{1,0:T(8,128)(2,1)S(1)}, u32[]{:S(2)}, u32[]{:S(2)}) collective-permute-start(bf16[256,2176]{1,0:T(8,128)(2,1)S(1)} %get-tuple-element.99.refs_2_), channel_id=1, source_target_pairs={{0,1},{1,0},{2,3},{3,2},{4,5},{5,4},{6,7},{7,6},{8,9},{9,8},{10,11... | collective-permute-start | bytes 3342344 | tf_op jit(solution)/shard_map/ppermute | solution.py:536
  34.4 6.4 %collective-permute-start.5 = (bf16[256,512]{1,0:T(8,128)(2,1)S(1)}, bf16[256,512]{1,0:T(8,128)(2,1)S(1)}, u32[]{:S(2)}, u32[]{:S(2)}) collective-permute-start(bf16[256,512]{1,0:T(8,128)(2,1)S(1)} %get-tuple-element.101), channel_id=1, source_target_pairs={{0,2},{1,5},{2,0},{3,7},{4,6},{5,1},{6,4},{7,3},{8,10},{9,13},{10,... | collective-permute-start | bytes 786440 | tf_op jit(solution)/shard_map/ppermute | solution.py:536
  37.3 6.4 %collective-permute-start.9 = (bf16[256,512]{1,0:T(8,128)(2,1)S(1)}, bf16[256,512]{1,0:T(8,128)(2,1)S(1)}, u32[]{:S(2)}, u32[]{:S(2)}) collective-permute-start(bf16[256,512]{1,0:T(8,128)(2,1)S(1)} %get-tuple-element.108), channel_id=1, source_target_pairs={{0,8},{1,5},{2,10},{3,7},{4,12},{5,1},{6,14},{7,3},{8,0},{9,13},{1... | collective-permute-start | bytes 786440 | tf_op jit(solution)/shard_map/ppermute | solution.py:536
  43.8 6.3 %collective-permute-start.10 = (bf16[128,512]{1,0:T(8,128)(2,1)S(1)}, bf16[128,512]{1,0:T(8,128)(2,1)S(1)}, u32[]{:S(2)}, u32[]{:S(2)}) collective-permute-start(bf16[128,512]{1,0:T(8,128)(2,1)S(1)} %get-tuple-element.110), channel_id=1, source_target_pairs={{0,16},{1,9},{2,18},{3,11},{4,20},{5,13},{6,22},{7,15},{8,24},{9,1... | collective-permute-start | bytes 393224 | tf_op jit(solution)/shard_map/ppermute | solution.py:536
  46.4 50.5 %collective-permute-start.23 = (bf16[96,512]{1,0:T(8,128)(2,1)}, bf16[96,512]{1,0:T(8,128)(2,1)}, u32[]{:S(2)}, u32[]{:S(2)}) collective-permute-start(bf16[96,512]{1,0:T(8,128)(2,1)} %get-tuple-element.120), channel_id=1, source_target_pairs={{1,0},{2,1},{3,2},{0,3},{5,4},{6,5},{7,6},{4,7},{9,8},{10,9},{11,1... | collective-permute-start | bytes 294920 | tf_op jit(solution)/shard_map/ppermute | solution.py:683
  46.4 6.8 %collective-permute-start.8 = (bf16[128,512]{1,0:T(8,128)(2,1)S(1)}, bf16[128,512]{1,0:T(8,128)(2,1)S(1)}, u32[]{:S(2)}, u32[]{:S(2)}) collective-permute-start(bf16[128,512]{1,0:T(8,128)(2,1)S(1)} %get-tuple-element.107), channel_id=1, source_target_pairs={{0,8},{1,9},{2,10},{3,11},{4,12},{5,13},{6,14},{7,15},{8,0},{9,1},... | collective-permute-start | bytes 393224 | tf_op jit(solution)/shard_map/ppermute | solution.py:536
  48.0 11.1 %collective-permute-start.12 = (bf16[128,2176]{1,0:T(8,128)(2,1)S(1)}, bf16[128,2176]{1,0:T(8,128)(2,1)S(1)}, u32[]{:S(2)}, u32[]{:S(2)}) collective-permute-start(bf16[128,2176]{1,0:T(8,128)(2,1)S(1)} %get-tuple-element.111), channel_id=1, source_target_pairs={{0,4},{1,3},{2,6},{3,1},{4,0},{5,7},{6,2},{7,5},{8,12},{9,11},{10,... | collective-permute-start | bytes 1671176 | tf_op jit(solution)/shard_map/ppermute | solution.py:536
  50.1 6.5 %collective-permute-start.13 = (bf16[128,512]{1,0:T(8,128)(2,1)S(1)}, bf16[128,512]{1,0:T(8,128)(2,1)S(1)}, u32[]{:S(2)}, u32[]{:S(2)}) collective-permute-start(bf16[128,512]{1,0:T(8,128)(2,1)S(1)} %add.6.refs_2_.refs_0_), channel_id=1, source_target_pairs={{0,2},{1,17},{2,0},{3,19},{4,6},{5,21},{6,4},{7,23},{8,10},{9,25},... | collective-permute-start | bytes 393224 | tf_op jit(solution)/shard_map/ppermute | solution.py:536
  53.3 8.8 %collective-permute-start.11 = (bf16[128,512]{1,0:T(8,128)(2,1)S(1)}, bf16[128,512]{1,0:T(8,128)(2,1)S(1)}, u32[]{:S(2)}, u32[]{:S(2)}) collective-permute-start(bf16[128,512]{1,0:T(8,128)(2,1)S(1)} %add.7.refs_2_.refs_0_), channel_id=1, source_target_pairs={{0,16},{1,17},{2,18},{3,19},{4,20},{5,21},{6,22},{7,23},{8,24},{9,... | collective-permute-start | bytes 393224 | tf_op jit(solution)/shard_map/ppermute | solution.py:536
  56.6 11.4 %collective-permute-start.18 = (bf16[128,512]{1,0:T(8,128)(2,1)S(1)}, bf16[128,512]{1,0:T(8,128)(2,1)S(1)}, u32[]{:S(2)}, u32[]{:S(2)}) collective-permute-start(bf16[128,512]{1,0:T(8,128)(2,1)S(1)} %add.8.refs_2_.refs_0_), channel_id=1, source_target_pairs={{0,16},{1,9},{2,18},{3,11},{4,20},{5,13},{6,22},{7,15},{8,24},{9,1... | collective-permute-start | bytes 393224 | tf_op jit(solution)/shard_map/ppermute | solution.py:536
  59.2 6.6 %collective-permute-start.15 = (bf16[64,2176]{1,0:T(8,128)(2,1)S(1)}, bf16[64,2176]{1,0:T(8,128)(2,1)S(1)}, u32[]{:S(2)}, u32[]{:S(2)}) collective-permute-start(bf16[64,2176]{1,0:T(8,128)(2,1)S(1)} %get-tuple-element.113), channel_id=1, source_target_pairs={{0,2},{1,5},{2,0},{3,7},{4,6},{5,1},{6,4},{7,3},{8,10},{9,13},{10,... | collective-permute-start | bytes 835592 | tf_op jit(solution)/shard_map/ppermute | solution.py:536
  62.2 5.7 %collective-permute-start.14 = (bf16[128,512]{1,0:T(8,128)(2,1)S(1)}, bf16[128,512]{1,0:T(8,128)(2,1)S(1)}, u32[]{:S(2)}, u32[]{:S(2)}) collective-permute-start(bf16[128,512]{1,0:T(8,128)(2,1)S(1)} %add.9.refs_2_.refs_0_), channel_id=1, source_target_pairs={{0,8},{1,9},{2,10},{3,11},{4,12},{5,13},{6,14},{7,15},{8,0},{9,1},... | collective-permute-start | bytes 393224 | tf_op jit(solution)/shard_map/ppermute | solution.py:536
  65.9 5.1 %collective-permute-start.17 = (bf16[32,2176]{1,0:T(8,128)(2,1)S(1)}, bf16[32,2176]{1,0:T(8,128)(2,1)S(1)}, u32[]{:S(2)}, u32[]{:S(2)}) collective-permute-start(bf16[32,2176]{1,0:T(8,128)(2,1)S(1)} %get-tuple-element.115), channel_id=1, source_target_pairs={{0,8},{1,9},{2,10},{3,11},{4,12},{5,13},{6,14},{7,15},{8,0},{9,1},... | collective-permute-start | bytes 417800 | tf_op jit(solution)/shard_map/ppermute | solution.py:536
  67.9 6.7 %collective-permute-start.16 = (bf16[256,512]{1,0:T(8,128)(2,1)S(1)}, bf16[256,512]{1,0:T(8,128)(2,1)S(1)}, u32[]{:S(2)}, u32[]{:S(2)}) collective-permute-start(bf16[256,512]{1,0:T(8,128)(2,1)S(1)} %join.9.refs_2_.refs_0_), channel_id=1, source_target_pairs={{0,2},{1,5},{2,0},{3,7},{4,6},{5,1},{6,4},{7,3},{8,10},{9,13},{10,... | collective-permute-start | bytes 786440 | tf_op jit(solution)/shard_map/ppermute | solution.py:536
  68.0 9.5 %collective-permute-start.21 = (bf16[256,512]{1,0:T(8,128)(2,1)S(1)}, bf16[256,512]{1,0:T(8,128)(2,1)S(1)}, u32[]{:S(2)}, u32[]{:S(2)}) collective-permute-start(bf16[256,512]{1,0:T(8,128)(2,1)S(1)} %join.10.refs_2_.refs_0_), channel_id=1, source_target_pairs={{0,8},{1,5},{2,10},{3,7},{4,12},{5,1},{6,14},{7,3},{8,0},{9,13},{1... | collective-permute-start | bytes 786440 | tf_op jit(solution)/shard_map/ppermute | solution.py:536
  71.0 8.0 %collective-permute-start.20 = (bf16[32,2176]{1,0:T(8,128)(2,1)S(1)}, bf16[32,2176]{1,0:T(8,128)(2,1)S(1)}, u32[]{:S(2)}, u32[]{:S(2)}) collective-permute-start(bf16[32,2176]{1,0:T(8,128)(2,1)S(1)} %add.10.refs_2_.refs_0_), channel_id=1, source_target_pairs={{0,16},{1,17},{2,18},{3,19},{4,20},{5,21},{6,22},{7,23},{8,24},{9,... | collective-permute-start | bytes 417800 | tf_op jit(solution)/shard_map/ppermute | solution.py:536
  74.7 9.2 %collective-permute-start.19 = (bf16[512,512]{1,0:T(8,128)(2,1)S(1)}, bf16[512,512]{1,0:T(8,128)(2,1)S(1)}, u32[]{:S(2)}, u32[]{:S(2)}) collective-permute-start(bf16[512,512]{1,0:T(8,128)(2,1)S(1)} %join.11.refs_2_.refs_0_), channel_id=1, source_target_pairs={{0,4},{1,3},{2,6},{3,1},{4,0},{5,7},{6,2},{7,5},{8,12},{9,11},{10,... | collective-permute-start | bytes 1572872 | tf_op jit(solution)/shard_map/ppermute | solution.py:536
  77.6 13.6 %collective-permute-start.24 = (bf16[512,512]{1,0:T(8,128)(2,1)S(1)}, bf16[512,512]{1,0:T(8,128)(2,1)S(1)}, u32[]{:S(2)}, u32[]{:S(2)}) collective-permute-start(bf16[512,512]{1,0:T(8,128)(2,1)S(1)} %join.12.refs_2_.refs_0_), channel_id=1, source_target_pairs={{0,4},{1,3},{2,6},{3,1},{4,0},{5,7},{6,2},{7,5},{8,12},{9,11},{10,... | collective-permute-start | bytes 1572872 | tf_op jit(solution)/shard_map/ppermute | solution.py:536
  79.0 6.4 %collective-permute-start.26 = (bf16[32,2176]{1,0:T(8,128)(2,1)S(1)}, bf16[32,2176]{1,0:T(8,128)(2,1)S(1)}, u32[]{:S(2)}, u32[]{:S(2)}) collective-permute-start(bf16[32,2176]{1,0:T(8,128)(2,1)S(1)} %add.11.refs_2_.refs_0_), channel_id=1, source_target_pairs={{0,8},{1,9},{2,10},{3,11},{4,12},{5,13},{6,14},{7,15},{8,0},{9,1},... | collective-permute-start | bytes 417800 | tf_op jit(solution)/shard_map/ppermute | solution.py:536
  84.0 2.7 %collective-permute-start.22 = (bf16[1024,512]{1,0:T(8,128)(2,1)S(1)}, bf16[1024,512]{1,0:T(8,128)(2,1)S(1)}, u32[]{:S(2)}, u32[]{:S(2)}) collective-permute-start(bf16[1024,512]{1,0:T(8,128)(2,1)S(1)} %join.13.refs_0_.refs_1_), channel_id=1, source_target_pairs={{0,1},{1,0},{2,3},{3,2},{4,5},{5,4},{6,7},{7,6},{8,9},{9,8},{10,11... | collective-permute-start | bytes 3145736 | tf_op jit(solution)/shard_map/ppermute | solution.py:536
  85.5 6.6 %collective-permute-start.27 = (bf16[64,2176]{1,0:T(8,128)(2,1)S(1)}, bf16[64,2176]{1,0:T(8,128)(2,1)S(1)}, u32[]{:S(2)}, u32[]{:S(2)}) collective-permute-start(bf16[64,2176]{1,0:T(8,128)(2,1)S(1)} %join.15.refs_0_.refs_2_), channel_id=1, source_target_pairs={{0,2},{1,5},{2,0},{3,7},{4,6},{5,1},{6,4},{7,3},{8,10},{9,13},{10,... | collective-permute-start | bytes 835592 | tf_op jit(solution)/shard_map/ppermute | solution.py:536
  86.7 2.3 %copy-start.2 = (bf16[2048,512]{1,0:T(8,128)(2,1)S(1)}, bf16[2048,512]{1,0:T(8,128)(2,1)}, u32[]{:S(2)}) copy-start(bf16[2048,512]{1,0:T(8,128)(2,1)} %refs_2_.9) | copy-start | bytes 6291460
  91.2 4.3 %collective-permute-start.25 = (bf16[1024,512]{1,0:T(8,128)(2,1)S(1)}, bf16[1024,512]{1,0:T(8,128)(2,1)S(1)}, u32[]{:S(2)}, u32[]{:S(2)}) collective-permute-start(bf16[1024,512]{1,0:T(8,128)(2,1)S(1)} %join.14.refs_0_.refs_1_), channel_id=1, source_target_pairs={{0,1},{1,0},{2,3},{3,2},{4,5},{5,4},{6,7},{7,6},{8,9},{9,8},{10,11... | collective-permute-start | bytes 3145736 | tf_op jit(solution)/shard_map/ppermute | solution.py:536
  92.2 9.6 %collective-permute-start.28 = (bf16[128,2176]{1,0:T(8,128)(2,1)S(1)}, bf16[128,2176]{1,0:T(8,128)(2,1)S(1)}, u32[]{:S(2)}, u32[]{:S(2)}) collective-permute-start(bf16[128,2176]{1,0:T(8,128)(2,1)S(1)} %join.16.refs_0_), channel_id=1, source_target_pairs={{0,4},{1,3},{2,6},{3,1},{4,0},{5,7},{6,2},{7,5},{8,12},{9,11},{10,... | collective-permute-start | bytes 1671176 | tf_op jit(solution)/shard_map/ppermute | solution.py:536
  101.9 2.8 %collective-permute-start.29 = (bf16[256,2176]{1,0:T(8,128)(2,1)S(1)}, bf16[256,2176]{1,0:T(8,128)(2,1)S(1)}, u32[]{:S(2)}, u32[]{:S(2)}) collective-permute-start(bf16[256,2176]{1,0:T(8,128)(2,1)S(1)} %join.17.refs_0_.refs_1_), channel_id=1, source_target_pairs={{0,1},{1,0},{2,3},{3,2},{4,5},{5,4},{6,7},{7,6},{8,9},{9,8},{10,11... | collective-permute-start | bytes 3342344 | tf_op jit(solution)/shard_map/ppermute | solution.py:536
